TPU v7x, 128 devices: a whole 4x4x4 slice. The times are simulated.
128 devices in a mesh: fsdp: 128 (over x, z, y, core).
Axes of the slice: x: 4, y: 4, z: 4, core: 2. Of those that a mesh axis runs over, the one named last changes fastest.
Arguments:
- tokens: bfloat16 [128, 128, 1536], P('fsdp'), may hold values from -6 to 6
- lengths: int32 [128], P('fsdp'), may hold values from 64 to 128, as said below
- gain_attn: bfloat16 [1536], P('fsdp'), may hold values from 0.5 to 1.5
- w_query: bfloat16 [1536, 1536], P('fsdp'), may hold values from -0.15625 to 0.15625
- w_key: bfloat16 [1536, 1536], P('fsdp'), may hold values from -0.15625 to 0.15625
- w_value: bfloat16 [1536, 1536], P('fsdp'), may hold values from -0.15625 to 0.15625
- w_house: bfloat16 [1536, 1536], P('fsdp'), may hold values from -0.15625 to 0.15625
- w_beta: bfloat16 [1536, 12], P('fsdp'), may hold values from -0.15625 to 0.15625
- w_out: bfloat16 [1536, 1536], P('fsdp'), may hold values from -0.4375 to 0.4375
- gain_ffn: bfloat16 [1536], P('fsdp'), may hold values from 0.5 to 1.5
- w_gate: bfloat16 [1536, 4096], P('fsdp'), may hold values from -0.15625 to 0.15625
- w_up: bfloat16 [1536, 4096], P('fsdp'), may hold values from -0.15625 to 0.15625
- w_down: bfloat16 [4096, 1536], P('fsdp'), may hold values from -0.09375 to 0.09375
- cotangent: bfloat16 [128, 128, 1536], P('fsdp'), may hold values from -6 to 6
Outputs:
- mixed_out: bfloat16 [128, 128, 1536], P('fsdp')
- grad_tokens: float32 [128, 128, 1536], P('fsdp')
- grad_gain_attn: float32 [1536], P('fsdp')
- grad_w_query: float32 [1536, 1536], P('fsdp')
- grad_w_key: float32 [1536, 1536], P('fsdp')
- grad_w_value: float32 [1536, 1536], P('fsdp')
- grad_w_house: float32 [1536, 1536], P('fsdp')
- grad_w_beta: float32 [1536, 12], P('fsdp')
- grad_w_out: float32 [1536, 1536], P('fsdp')
- grad_gain_ffn: float32 [1536], P('fsdp')
- grad_w_gate: float32 [1536, 4096], P('fsdp')
- grad_w_up: float32 [1536, 4096], P('fsdp')
- grad_w_down: float32 [4096, 1536], P('fsdp')
Inputs may be any that keep to these rules, and one draw needn't show every extreme that they name: `lengths`: some sequence has all 128 tokens valid.
All inputs are finite; a program needn't handle non-finite values.
Results may differ from a plain program's by a relative error of at most 0.02.
Values may be sent and summed in bfloat16 or wider, within the bound.
No kernel may reach another device: no remote copies, remote signals or barrier semaphores. Data moves between devices by JAX's collectives and lax.ppermute only.
A program may use at most 320 MiB of HBM per device.

v0:
```python
import jax
import jax.numpy as jnp
from jax import lax
from jax.sharding import PartitionSpec as P

EPSILON = 1e-06
EXACT_PRECISION = lax.Precision.HIGHEST


def rms_scale(vector, gain_vec):
    return (
        vector * lax.rsqrt(jnp.mean(vector * vector, axis=-1, keepdims=True) + EPSILON) * gain_vec
    )


def reflector_probabilities(queries, key_rows, house_raw, beta_raw, length):
    count = queries.shape[0]
    position = jnp.arange(count, dtype=jnp.int32)
    strict = position[:, None] > position[None, :]
    upto = position[:, None] >= position[None, :]
    unit_house = house_raw * lax.rsqrt(
        jnp.sum(house_raw * house_raw, axis=-1, keepdims=True) + EPSILON
    )
    betas = 2.0 * jax.nn.sigmoid(beta_raw)
    coupling = jnp.where(
        strict, betas[:, None] * jnp.dot(unit_house, unit_house.T, precision=EXACT_PRECISION), 0.0
    )
    system = jnp.eye(count, dtype=queries.dtype) + coupling
    source = jnp.where(
        strict, betas[:, None] * jnp.dot(unit_house, key_rows.T, precision=EXACT_PRECISION), 0.0
    )
    carried = lax.linalg.triangular_solve(
        system, source, left_side=True, lower=True, unit_diagonal=True
    )
    direct = jnp.dot(queries, key_rows.T, precision=EXACT_PRECISION)
    through = jnp.where(upto, jnp.dot(queries, unit_house.T, precision=EXACT_PRECISION), 0.0)
    logits = (direct - jnp.dot(through, carried, precision=EXACT_PRECISION)) * queries.shape[1] ** (
        -0.5
    )
    allowed = upto & (position[None, :] < length)
    logits = jnp.where(allowed, logits, -1e30)
    highest = jnp.max(logits, axis=-1, keepdims=True)
    weights = jnp.where(allowed, jnp.exp(logits - highest), 0.0)
    return weights / jnp.sum(weights, axis=-1, keepdims=True)


def all_probs(queries, key_rows, house_raw, beta_raw, lengths):
    per_head = jax.vmap(reflector_probabilities, in_axes=(1, 1, 1, 1, None), out_axes=0)
    return jax.vmap(per_head, in_axes=(0, 0, 0, 0, 0), out_axes=0)(
        queries, key_rows, house_raw, beta_raw, lengths
    )


def matmul(left, right):
    return jnp.dot(left, right, preferred_element_type=jnp.float32)


def matmul_tn(left, right):
    return lax.dot_general(
        left, right, (((0,), (0,)), ((), ())), preferred_element_type=jnp.float32
    )


def matmul_nt(left, right):
    return lax.dot_general(
        left, right, (((1,), (1,)), ((), ())), preferred_element_type=jnp.float32
    )


def swish_product(gate_in, upward_in):
    return jax.nn.silu(gate_in) * upward_in


def stacked(grad, owners):
    return grad.reshape((owners, grad.shape[0] // owners) + grad.shape[1:])


def added(received):
    return tuple((jnp.sum(piece, axis=0) for piece in received))


def body(
    tokens,
    lengths,
    gain_attn,
    w_query,
    w_key,
    w_value,
    w_house,
    w_beta,
    w_out,
    gain_ffn,
    w_gate,
    w_up,
    w_down,
    cotangent,
):
    seqs, count, width = tokens.shape
    total_rows = seqs * count
    owners = lax.axis_size("fsdp")
    attn_set = (
        lax.all_gather(gain_attn, "fsdp", axis=0, tiled=True),
        lax.all_gather(w_query, "fsdp", axis=0, tiled=True),
        lax.all_gather(w_key, "fsdp", axis=0, tiled=True),
        lax.all_gather(w_value, "fsdp", axis=0, tiled=True),
        lax.all_gather(w_house, "fsdp", axis=0, tiled=True),
        lax.all_gather(w_beta, "fsdp", axis=0, tiled=True),
        lax.all_gather(w_out, "fsdp", axis=0, tiled=True),
    )
    full_gain_attn, full_query, full_key, full_value, full_house, full_beta, full_out = attn_set
    heads = full_beta.shape[1]
    shape_heads = (seqs, count, heads, width // heads)
    flat_in = tokens.astype(jnp.float32).reshape(total_rows, width)
    normed = rms_scale(flat_in, full_gain_attn.astype(jnp.float32)).astype(jnp.bfloat16)
    queries = matmul(normed, full_query).astype(jnp.bfloat16)
    key_rows = matmul(normed, full_key).astype(jnp.bfloat16)
    values_in = matmul(normed, full_value).astype(jnp.bfloat16)
    house_in = matmul(normed, full_house).astype(jnp.bfloat16)
    beta_raw = matmul(normed, full_beta)

    def probs_of(query_in, key_in, house_raw, beta_in):
        return all_probs(query_in, key_in, house_raw, beta_in, lengths)

    probs, probs_pull = jax.vjp(
        probs_of,
        queries.astype(jnp.float32).reshape(shape_heads),
        key_rows.astype(jnp.float32).reshape(shape_heads),
        house_in.astype(jnp.float32).reshape(shape_heads),
        beta_raw.reshape(seqs, count, heads),
    )
    probs_low = probs.astype(jnp.bfloat16)
    values_heads = values_in.reshape(shape_heads)
    attended = (
        jnp.einsum("shqk,skhd->sqhd", probs_low, values_heads, preferred_element_type=jnp.float32)
        .astype(jnp.bfloat16)
        .reshape(total_rows, width)
    )
    hidden = flat_in + matmul(attended, full_out)
    ffn_set = (
        lax.all_gather(gain_ffn, "fsdp", axis=0, tiled=True),
        lax.all_gather(w_gate, "fsdp", axis=0, tiled=True),
        lax.all_gather(w_up, "fsdp", axis=0, tiled=True),
        lax.all_gather(w_down, "fsdp", axis=0, tiled=True),
    )
    full_gain_ffn, full_gate, full_up, full_down = ffn_set
    second = rms_scale(hidden, full_gain_ffn.astype(jnp.float32)).astype(jnp.bfloat16)
    gate = matmul(second, full_gate)
    upward = matmul(second, full_up)
    product = swish_product(gate, upward).astype(jnp.bfloat16)
    feed = matmul(product, full_down)
    unpadded_row_mask = (
        (jnp.arange(count, dtype=jnp.int32)[None, :] < lengths[:, None])
        .astype(jnp.float32)
        .reshape(total_rows, 1)
    )
    mixed_out = (
        (unpadded_row_mask * (hidden + feed)).astype(jnp.bfloat16).reshape(seqs, count, width)
    )
    ffn_back = (
        lax.all_gather(gain_ffn, "fsdp", axis=0, tiled=True),
        lax.all_gather(w_gate, "fsdp", axis=0, tiled=True),
        lax.all_gather(w_up, "fsdp", axis=0, tiled=True),
        lax.all_gather(w_down, "fsdp", axis=0, tiled=True),
    )
    backward_feedforward_gain, back_gate, back_up, back_down = ffn_back
    out_grad = cotangent.astype(jnp.float32).reshape(total_rows, width) * unpadded_row_mask
    out_low = out_grad.astype(jnp.bfloat16)
    grad_down = matmul_tn(product, out_low)
    product_grad = matmul_nt(out_low, back_down)
    swish_value, swish_pull = jax.vjp(swish_product, gate, upward)
    gate_grad, upward_grad = swish_pull(product_grad)
    gate_low = gate_grad.astype(jnp.bfloat16)
    upward_low = upward_grad.astype(jnp.bfloat16)
    gate_gradient_rows = matmul_tn(second, gate_low)
    grad_up = matmul_tn(second, upward_low)
    second_grad = matmul_nt(gate_low, back_gate) + matmul_nt(upward_low, back_up)
    norm_value, norm_pull = jax.vjp(
        rms_scale, hidden, backward_feedforward_gain.astype(jnp.float32)
    )
    hidden_part, grad_gain_ffn = norm_pull(second_grad)
    hidden_grad = out_grad + hidden_part
    ffn_received = (
        lax.all_to_all(
            stacked(grad_gain_ffn, owners).astype(jnp.bfloat16),
            "fsdp",
            split_axis=0,
            concat_axis=0,
            tiled=True,
        ).astype(jnp.float32),
        lax.all_to_all(
            stacked(gate_gradient_rows, owners).astype(jnp.bfloat16),
            "fsdp",
            split_axis=0,
            concat_axis=0,
            tiled=True,
        ).astype(jnp.float32),
        lax.all_to_all(
            stacked(grad_up, owners).astype(jnp.bfloat16),
            "fsdp",
            split_axis=0,
            concat_axis=0,
            tiled=True,
        ).astype(jnp.float32),
        lax.all_to_all(
            stacked(grad_down, owners).astype(jnp.bfloat16),
            "fsdp",
            split_axis=0,
            concat_axis=0,
            tiled=True,
        ).astype(jnp.float32),
    )
    ffn_sums = added(ffn_received)
    attn_back = (
        lax.all_gather(gain_attn, "fsdp", axis=0, tiled=True),
        lax.all_gather(w_query, "fsdp", axis=0, tiled=True),
        lax.all_gather(w_key, "fsdp", axis=0, tiled=True),
        lax.all_gather(w_value, "fsdp", axis=0, tiled=True),
        lax.all_gather(w_house, "fsdp", axis=0, tiled=True),
        lax.all_gather(w_beta, "fsdp", axis=0, tiled=True),
        lax.all_gather(w_out, "fsdp", axis=0, tiled=True),
    )
    back_gain_attn, back_query, back_key, back_value, back_house, back_beta, back_out = attn_back
    branch_low = hidden_grad.astype(jnp.bfloat16)
    grad_out = matmul_tn(attended, branch_low)
    attended_grad = matmul_nt(branch_low, back_out).astype(jnp.bfloat16).reshape(shape_heads)
    values_grad = (
        jnp.einsum("shqk,sqhd->skhd", probs_low, attended_grad, preferred_element_type=jnp.float32)
        .astype(jnp.bfloat16)
        .reshape(total_rows, width)
    )
    probs_grad = jnp.einsum(
        "sqhd,skhd->shqk", attended_grad, values_heads, preferred_element_type=jnp.float32
    )
    query_grad, key_grad, house_grad, beta_grad = probs_pull(probs_grad)
    query_low = query_grad.astype(jnp.bfloat16).reshape(total_rows, width)
    key_low = key_grad.astype(jnp.bfloat16).reshape(total_rows, width)
    house_low = house_grad.astype(jnp.bfloat16).reshape(total_rows, width)
    beta_low = beta_grad.astype(jnp.bfloat16).reshape(total_rows, heads)
    grad_query = matmul_tn(normed, query_low)
    grad_key = matmul_tn(normed, key_low)
    grad_value = matmul_tn(normed, values_grad)
    grad_house = matmul_tn(normed, house_low)
    grad_beta = matmul_tn(normed, beta_low)
    normed_grad = (
        matmul_nt(query_low, back_query)
        + matmul_nt(key_low, back_key)
        + matmul_nt(values_grad, back_value)
        + matmul_nt(house_low, back_house)
        + matmul_nt(beta_low, back_beta)
    )
    first_value, first_pull = jax.vjp(rms_scale, flat_in, back_gain_attn.astype(jnp.float32))
    input_part, grad_gain_attn = first_pull(normed_grad)
    grad_tokens = (hidden_grad + input_part).reshape(seqs, count, width)
    attn_received = (
        lax.all_to_all(
            stacked(grad_gain_attn, owners).astype(jnp.bfloat16),
            "fsdp",
            split_axis=0,
            concat_axis=0,
            tiled=True,
        ).astype(jnp.float32),
        lax.all_to_all(
            stacked(grad_query, owners).astype(jnp.bfloat16),
            "fsdp",
            split_axis=0,
            concat_axis=0,
            tiled=True,
        ).astype(jnp.float32),
        lax.all_to_all(
            stacked(grad_key, owners).astype(jnp.bfloat16),
            "fsdp",
            split_axis=0,
            concat_axis=0,
            tiled=True,
        ).astype(jnp.float32),
        lax.all_to_all(
            stacked(grad_value, owners).astype(jnp.bfloat16),
            "fsdp",
            split_axis=0,
            concat_axis=0,
            tiled=True,
        ).astype(jnp.float32),
        lax.all_to_all(
            stacked(grad_house, owners).astype(jnp.bfloat16),
            "fsdp",
            split_axis=0,
            concat_axis=0,
            tiled=True,
        ).astype(jnp.float32),
        lax.all_to_all(
            stacked(grad_beta, owners).astype(jnp.bfloat16),
            "fsdp",
            split_axis=0,
            concat_axis=0,
            tiled=True,
        ).astype(jnp.float32),
        lax.all_to_all(
            stacked(grad_out, owners).astype(jnp.bfloat16),
            "fsdp",
            split_axis=0,
            concat_axis=0,
            tiled=True,
        ).astype(jnp.float32),
    )
    attn_sums = added(attn_received)
    return (
        mixed_out,
        grad_tokens,
        attn_sums[0],
        attn_sums[1],
        attn_sums[2],
        attn_sums[3],
        attn_sums[4],
        attn_sums[5],
        attn_sums[6],
        ffn_sums[0],
        ffn_sums[1],
        ffn_sums[2],
        ffn_sums[3],
    )


def solution(mesh):
    in_specs = (
        P("fsdp", None, None),
        P("fsdp"),
        P("fsdp"),
        P("fsdp", None),
        P("fsdp", None),
        P("fsdp", None),
        P("fsdp", None),
        P("fsdp", None),
        P("fsdp", None),
        P("fsdp"),
        P("fsdp", None),
        P("fsdp", None),
        P("fsdp", None),
        P("fsdp", None, None),
    )
    out_specs = (
        P("fsdp", None, None),
        P("fsdp", None, None),
        P("fsdp"),
        P("fsdp", None),
        P("fsdp", None),
        P("fsdp", None),
        P("fsdp", None),
        P("fsdp", None),
        P("fsdp", None),
        P("fsdp"),
        P("fsdp", None),
        P("fsdp", None),
        P("fsdp", None),
    )
    return jax.shard_map(body, mesh=mesh, in_specs=in_specs, out_specs=out_specs, check_vma=False)
```

profile of v0, /device:TPU:1, one launch (start us, length us, event | category | flops | bytes accessed | tf_op | source)
XLA Modules:
  0.0 1850.5 jit_solution(15749214629127245885)
XLA Ops:
  15.0 69.7 %all-reduce.2 = (bf16[1536]{0:T(1024)(128)(2,1)S(1)}, bf16[1536]{0:T(1024)(128)(2,1)S(1)}) all-reduce(bf16[1536]{0:T(1024)(128)(2,1)S(1)} %dynamic-update-slice, bf16[1536]{0:T(1024)(128)(2,1)S(1)} %dynamic-update-slice.1), channel_id=1, replica_groups=mesh['fsdp'=128] {'fsdp'}, use_global_device_ids=true, to_apply=%add | all-reduce | flops 3072 | bytes 12288
  86.9 34.7 %all-gather.4 = bf16[128,12,12]{2,1,0:T(8,128)(2,1)S(1)} all-gather(bf16[1,12,12]{2,1,0:T(8,128)(2,1)} %bitcast.350), channel_id=1, replica_groups=mesh['fsdp'=128] {'fsdp'}, dimensions={0}, use_global_device_ids=true | all-gather | bytes 37152 | tf_op jit(solution)/shard_map/all_gather | solution.py:107
  138.0 14.3 all-gather.21.cloned.1.call-done
  163.9 57.3 %all-gather.19.cloned.1.call-done = bf16[128,12,1536]{2,1,0:T(8,128)(2,1)} async-done(((bf16[1,12,1536]{2,1,0:T(8,128)(2,1)}), bf16[128,12,1536]{2,1,0:T(8,128)(2,1)}) %all-gather.19.cloned.1.call-update) | async-done | bytes 4718608 | tf_op jit(solution)/shard_map/all_gather | solution.py:105
  233.5 56.6 %all-gather.25.cloned.1.call-done = bf16[128,12,1536]{2,1,0:T(8,128)(2,1)} async-done(((bf16[1,12,1536]{2,1,0:T(8,128)(2,1)}), bf16[128,12,1536]{2,1,0:T(8,128)(2,1)}) %all-gather.25.cloned.1.call-update) | async-done | bytes 4718608 | tf_op jit(solution)/shard_map/all_gather | solution.py:106
  311.3 119.3 %custom-call.8 = f32[1,12,1,128,128]{3,4,2,1,0:T(8,128)} custom-call(f32[1,12,1,128,128]{4,3,2,1,0:T(8,128)} %fusion.48), custom_call_target="InvertDiagBlocksLowerTriangular" | custom-call | tf_op jit(solution)/shard_map/transpose(jvp(vmap(vmap())))/triangular_solve/custom-call.0 | solution.py:32
  432.7 119.8 %custom-call.6 = f32[1,12,1,128,128]{3,4,2,1,0:T(8,128)} custom-call(f32[1,12,1,128,128]{4,3,2,1,0:T(8,128)} %add_bitcast_fusion), custom_call_target="InvertDiagBlocksLowerTriangular" | custom-call | tf_op jit(solution)/shard_map/jvp(vmap(vmap()))/triangular_solve | solution.py:32
  573.4 18.6 %reshape.568 = bf16[1536,4096]{1,0:T(8,128)(2,1)} reshape(bf16[128,12,4096]{2,1,0:T(8,128)(2,1)} %all-gather.29.cloned.1.call-done) | data formatting | bytes 25165824
  592.1 18.6 %reshape.570 = bf16[1536,4096]{1,0:T(8,128)(2,1)} reshape(bf16[128,12,4096]{2,1,0:T(8,128)(2,1)} %all-gather.31.cloned.1.call-done) | data formatting | bytes 25165824
  623.7 10.1 multiply_convert_fusion
  633.9 9.6 fusion.135
  643.6 9.8 multiply_reduce_fusion
  709.5 9.8 all-to-all-start
  760.1 68.9 %all-to-all-done.6 = bf16[128,12,1536]{2,1,0:T(8,128)(2,1)} async-done(((bf16[128,12,1536]{2,1,0:T(8,128)(2,1)}), bf16[128,12,1536]{2,1,0:T(8,128)(2,1)}, u32[]{:S(2)}, u32[]{:S(2)}) %all-to-all-start.6) | async-done | bytes 4718624 | tf_op jit(solution)/shard_map/all_to_all | solution.py:297
  829.0 9.7 all-to-all-start.2
  845.6 69.0 %all-to-all-done.2 = bf16[128,12,1536]{2,1,0:T(8,128)(2,1)} async-done(((bf16[128,12,1536]{2,1,0:T(8,128)(2,1)}), bf16[128,12,1536]{2,1,0:T(8,128)(2,1)}, u32[]{:S(2)}, u32[]{:S(2)}) %all-to-all-start.2) | async-done | bytes 4718624 | tf_op jit(solution)/shard_map/all_to_all | solution.py:269
  914.6 8.8 all-to-all-start.3
  930.3 68.7 %all-to-all-done.3 = bf16[128,12,1536]{2,1,0:T(8,128)(2,1)} async-done(((bf16[128,12,1536]{2,1,0:T(8,128)(2,1)}), bf16[128,12,1536]{2,1,0:T(8,128)(2,1)}, u32[]{:S(2)}, u32[]{:S(2)}) %all-to-all-start.3) | async-done | bytes 4718624 | tf_op jit(solution)/shard_map/all_to_all | solution.py:276
  998.9 9.4 all-to-all-start.4
  1015.1 69.1 %all-to-all-done.4 = bf16[128,12,1536]{2,1,0:T(8,128)(2,1)} async-done(((bf16[128,12,1536]{2,1,0:T(8,128)(2,1)}), bf16[128,12,1536]{2,1,0:T(8,128)(2,1)}, u32[]{:S(2)}, u32[]{:S(2)}) %all-to-all-start.4) | async-done | bytes 4718624 | tf_op jit(solution)/shard_map/all_to_all | solution.py:283
  1084.2 9.0 all-to-all-start.1
  1098.7 27.5 %copy.183 = bf16[128,32,1536]{2,1,0:T(8,128)(2,1)} copy(bf16[128,32,1536]{2,0,1:T(8,128)(2,1)S(1)} %convolution_convert_fusion.2) | data formatting | bytes 25165824 | tf_op jit(solution)/shard_map/convert_element_type | solution.py:205
  1126.2 42.5 %all-to-all-done.1 = bf16[128,12,1536]{2,1,0:T(8,128)(2,1)} async-done(((bf16[128,12,1536]{2,1,0:T(8,128)(2,1)}), bf16[128,12,1536]{2,1,0:T(8,128)(2,1)}, u32[]{:S(2)}, u32[]{:S(2)}) %all-to-all-start.1) | async-done | bytes 4718624 | tf_op jit(solution)/shard_map/all_to_all | solution.py:262
  1168.7 9.4 all-to-all-start.10
  1184.5 17.9 convert_element_type.278
  1202.4 138.1 %all-to-all-done.10 = bf16[128,32,1536]{2,1,0:T(8,128)(2,1)} async-done(((bf16[128,32,1536]{2,1,0:T(8,128)(2,1)}), bf16[128,32,1536]{2,1,0:T(8,128)(2,1)}, u32[]{:S(2)}, u32[]{:S(2)}) %all-to-all-start.10) | async-done | bytes 12582944 | tf_op jit(solution)/shard_map/all_to_all | solution.py:204
  1340.5 15.9 all-to-all-start.9
  1362.8 17.9 convert_element_type.275
  1380.7 208.2 %all-to-all-done.9 = bf16[128,12,4096]{2,1,0:T(8,128)(2,1)} async-done(((bf16[128,12,4096]{2,1,0:T(8,128)(2,1)}), bf16[128,12,4096]{2,1,0:T(8,128)(2,1)}, u32[]{:S(2)}, u32[]{:S(2)}) %all-to-all-start.9) | async-done | bytes 12582944 | tf_op jit(solution)/shard_map/all_to_all | solution.py:197
  1588.8 14.4 all-to-all-start.8
  1603.2 8.6 fusion.3
  1653.6 182.1 %all-to-all-done.8 = bf16[128,12,4096]{2,1,0:T(8,128)(2,1)} async-done(((bf16[128,12,4096]{2,1,0:T(8,128)(2,1)}), bf16[128,12,4096]{2,1,0:T(8,128)(2,1)}, u32[]{:S(2)}, u32[]{:S(2)}) %all-to-all-start.8) | async-done | bytes 12582944 | tf_op jit(solution)/shard_map/all_to_all | solution.py:190
  (301 shorter events, 290.8 us)
Async XLA Ops:
  7.2 119.0 %all-gather.23.cloned.1.call-start = ((), (), s32[]{:S(2)}) async-start(), calls=%async_computation.14 | async-start | bytes 6340608 | tf_op jit(solution)/shard_map/all_gather | solution.py:104
  7.9 144.4 %all-gather.21.cloned.1.call-start = ((), (), s32[]{:S(2)}) async-start(), calls=%async_computation.13 | async-start | bytes 6340608 | tf_op jit(solution)/shard_map/all_gather | solution.py:103
  8.7 212.6 %all-gather.19.cloned.1.call-start = ((), (), s32[]{:S(2)}) async-start(), calls=%async_computation.12 | async-start | bytes 6340608 | tf_op jit(solution)/shard_map/all_gather | solution.py:105
  9.4 280.7 %all-gather.25.cloned.1.call-start = ((), (), s32[]{:S(2)}) async-start(), calls=%async_computation.15 | async-start | bytes 6340608 | tf_op jit(solution)/shard_map/all_gather | solution.py:106
  10.0 551.2 %all-gather.27.cloned.1.call-start = ((), (), s32[]{:S(2)}) async-start(), calls=%async_computation.16 | async-start | bytes 6340608 | tf_op jit(solution)/shard_map/all_gather | solution.py:108
  10.6 562.8 %all-gather.29.cloned.1.call-start = ((), (), s32[]{:S(2)}) async-start(), calls=%async_computation.17 | async-start | bytes 16908288 | tf_op jit(solution)/shard_map/all_gather | solution.py:141
  11.1 580.9 %all-gather.31.cloned.1.call-start = ((), (), s32[]{:S(2)}) async-start(), calls=%async_computation.18 | async-start | bytes 16908288 | tf_op jit(solution)/shard_map/all_gather | solution.py:142
  11.9 611.9 %all-gather.17.cloned.1.call-start = ((), (), s32[]{:S(2)}) async-start(), calls=%async_computation.11 | async-start | bytes 12681216 | tf_op jit(solution)/shard_map/all_gather | solution.py:143
  84.7 213.5 %copy-start.39 = (f32[1536]{0:T(1024)}, f32[1536]{0:T(1024)S(1)}, u32[]{:S(2)}) copy-start(f32[1536]{0:T(1024)S(1)} %convert_element_type.223) | copy-start | bytes 18436
  124.1 174.1 %copy-start.57 = (f32[128]{0:T(128)}, f32[128]{0:T(128)S(1)}, u32[]{:S(2)}) copy-start(f32[128]{0:T(128)S(1)} %fusion.114) | copy-start | bytes 1540
  126.1 175.7 %copy-start.55 = (f32[128,12]{0,1:T(8,128)}, f32[128,12]{0,1:T(8,128)S(1)}, u32[]{:S(2)}) copy-start(f32[128,12]{0,1:T(8,128)S(1)} %fusion.22) | copy-start | bytes 18436
  138.0 420.2 %copy-start.4 = (bf16[128,1536]{0,1:T(8,128)(2,1)}, bf16[128,1536]{0,1:T(8,128)(2,1)S(1)}, u32[]{:S(2)}) copy-start(bf16[128,1536]{0,1:T(8,128)(2,1)S(1)} %copy.127) | copy-start | bytes 1179652
  163.9 394.2 %copy-start.6 = (bf16[128,1536]{0,1:T(8,128)(2,1)}, bf16[128,1536]{0,1:T(8,128)(2,1)S(1)}, u32[]{:S(2)}) copy-start(bf16[128,1536]{0,1:T(8,128)(2,1)S(1)} %copy.126) | copy-start | bytes 1179652
  304.4 248.0 %copy-start.10 = (f32[12,128,128]{1,2,0:T(8,128)}, f32[12,128,128]{1,2,0:T(8,128)S(1)}, u32[]{:S(2)}) copy-start(f32[12,128,128]{1,2,0:T(8,128)S(1)} %fusion.58) | copy-start | bytes 2359300
  573.4 43.8 %copy-start.8 = (bf16[128,1536]{1,0:T(8,128)(2,1)}, bf16[128,1536]{1,0:T(8,128)(2,1)S(1)}, u32[]{:S(2)}) copy-start(bf16[128,1536]{1,0:T(8,128)(2,1)S(1)} %multiply_convert_fusion.3) | copy-start | bytes 1179652
  676.1 33.4 %all-to-all-start.7 = ((bf16[128,1,12]{2,1,0:T(2,128)(2,1)}), bf16[128,1,12]{2,1,0:T(2,128)(2,1)}, u32[]{:S(2)}, u32[]{:S(2)}) async-start(bf16[128,1,12]{2,1,0:T(2,128)(2,1)} %convert_element_type.286), calls=%async_computation.7 | async-start | bytes 131072 | tf_op jit(solution)/shard_map/all_to_all | solution.py:183
  709.5 19.2 %all-to-all-start = ((bf16[128,1,12]{2,1,0:T(2,128)(2,1)}), bf16[128,1,12]{2,1,0:T(2,128)(2,1)S(1)}, u32[]{:S(2)}, u32[]{:S(2)}) async-start(bf16[128,1,12]{2,1,0:T(2,128)(2,1)} %convert_element_type.285), calls=%async_computation | async-start | bytes 131072 | tf_op jit(solution)/shard_map/all_to_all | solution.py:255
  728.7 18.7 %all-to-all-start.5 = ((bf16[128,12,12]{2,1,0:T(8,128)(2,1)}), bf16[128,12,12]{2,1,0:T(8,128)(2,1)}, u32[]{:S(2)}, u32[]{:S(2)}) async-start(bf16[128,12,12]{2,1,0:T(8,128)(2,1)} %copy.177), calls=%async_computation.5 | async-start | bytes 1048576 | tf_op jit(solution)/shard_map/all_to_all | solution.py:290
  747.4 81.7 %all-to-all-start.6 = ((bf16[128,12,1536]{2,1,0:T(8,128)(2,1)}), bf16[128,12,1536]{2,1,0:T(8,128)(2,1)}, u32[]{:S(2)}, u32[]{:S(2)}) async-start(bf16[128,12,1536]{2,1,0:T(8,128)(2,1)} %copy.179), calls=%async_computation.6 | async-start | bytes 12582912 | tf_op jit(solution)/shard_map/all_to_all | solution.py:297
  760.1 78.6 %copy-start.33 = (bf16[12,128,128]{2,1,0:T(8,128)(2,1)S(1)}, bf16[12,128,128]{2,1,0:T(8,128)(2,1)}, u32[]{:S(2)}) copy-start(bf16[12,128,128]{2,1,0:T(8,128)(2,1)} %convolution_convert_fusion.13) | copy-start | bytes 1179652
  829.0 85.5 %all-to-all-start.2 = ((bf16[128,12,1536]{2,1,0:T(8,128)(2,1)}), bf16[128,12,1536]{2,1,0:T(8,128)(2,1)}, u32[]{:S(2)}, u32[]{:S(2)}) async-start(bf16[128,12,1536]{2,1,0:T(8,128)(2,1)} %copy.169), calls=%async_computation.2 | async-start | bytes 12582912 | tf_op jit(solution)/shard_map/all_to_all | solution.py:269
  914.6 84.4 %all-to-all-start.3 = ((bf16[128,12,1536]{2,1,0:T(8,128)(2,1)}), bf16[128,12,1536]{2,1,0:T(8,128)(2,1)}, u32[]{:S(2)}, u32[]{:S(2)}) async-start(bf16[128,12,1536]{2,1,0:T(8,128)(2,1)} %copy.172), calls=%async_computation.3 | async-start | bytes 12582912 | tf_op jit(solution)/shard_map/all_to_all | solution.py:276
  998.9 85.2 %all-to-all-start.4 = ((bf16[128,12,1536]{2,1,0:T(8,128)(2,1)}), bf16[128,12,1536]{2,1,0:T(8,128)(2,1)}, u32[]{:S(2)}, u32[]{:S(2)}) async-start(bf16[128,12,1536]{2,1,0:T(8,128)(2,1)} %copy.175), calls=%async_computation.4 | async-start | bytes 12582912 | tf_op jit(solution)/shard_map/all_to_all | solution.py:283
  1015.1 79.7 %copy-start.29 = (bf16[1,128,1536]{2,1,0:T(8,128)(2,1)S(1)}, bf16[1,128,1536]{2,1,0:T(8,128)(2,1)}, u32[]{:S(2)}) copy-start(bf16[1,128,1536]{2,1,0:T(8,128)(2,1)} %param.29) | copy-start | bytes 1179652
  1015.1 79.7 %copy-start.62 = (f32[128]{0:T(128)S(1)}, f32[128]{0:T(128)}, u32[]{:S(2)}) copy-start(f32[128]{0:T(128)} %fusion.118) | copy-start | bytes 1540
  1084.2 84.6 %all-to-all-start.1 = ((bf16[128,12,1536]{2,1,0:T(8,128)(2,1)}), bf16[128,12,1536]{2,1,0:T(8,128)(2,1)}, u32[]{:S(2)}, u32[]{:S(2)}) async-start(bf16[128,12,1536]{2,1,0:T(8,128)(2,1)} %copy.166), calls=%async_computation.1 | async-start | bytes 12582912 | tf_op jit(solution)/shard_map/all_to_all | solution.py:262
  1126.2 51.9 %copy-start.9 = (bf16[128,1536]{1,0:T(8,128)(2,1)S(1)}, bf16[128,1536]{1,0:T(8,128)(2,1)}, u32[]{:S(2)}) copy-start(bf16[128,1536]{1,0:T(8,128)(2,1)} %copy-done.8) | copy-start | bytes 1179652
  1126.2 51.9 %copy-start.21 = (bf16[128,4096]{1,0:T(8,128)(2,1)S(1)}, bf16[128,4096]{1,0:T(8,128)(2,1)}, u32[]{:S(2)}) copy-start(bf16[128,4096]{1,0:T(8,128)(2,1)} %copy-done.20) | copy-start | bytes 3145732
  1168.7 171.8 %all-to-all-start.10 = ((bf16[128,32,1536]{2,1,0:T(8,128)(2,1)}), bf16[128,32,1536]{2,1,0:T(8,128)(2,1)}, u32[]{:S(2)}, u32[]{:S(2)}) async-start(bf16[128,32,1536]{2,1,0:T(8,128)(2,1)} %copy.183), calls=%async_computation.10 | async-start | bytes 25165824 | tf_op jit(solution)/shard_map/all_to_all | solution.py:204
  1202.4 154.0 %copy-start.19 = (bf16[128,4096]{1,0:T(8,128)(2,1)S(1)}, bf16[128,4096]{1,0:T(8,128)(2,1)}, u32[]{:S(2)}) copy-start(bf16[128,4096]{1,0:T(8,128)(2,1)} %copy-done.18) | copy-start | bytes 3145732
  1340.5 248.4 %all-to-all-start.9 = ((bf16[128,12,4096]{2,1,0:T(8,128)(2,1)}), bf16[128,12,4096]{2,1,0:T(8,128)(2,1)}, u32[]{:S(2)}, u32[]{:S(2)}) async-start(bf16[128,12,4096]{2,1,0:T(8,128)(2,1)} %convert_element_type.278), calls=%async_computation.9 | async-start | bytes 33554432 | tf_op jit(solution)/shard_map/all_to_all | solution.py:197
  1588.8 246.8 %all-to-all-start.8 = ((bf16[128,12,4096]{2,1,0:T(8,128)(2,1)}), bf16[128,12,4096]{2,1,0:T(8,128)(2,1)}, u32[]{:S(2)}, u32[]{:S(2)}) async-start(bf16[128,12,4096]{2,1,0:T(8,128)(2,1)} %convert_element_type.275), calls=%async_computation.8 | async-start | bytes 33554432 | tf_op jit(solution)/shard_map/all_to_all | solution.py:190
  (64 other events, 392.7 us)
Sparse Core Ops, SparseCore 0:
  11.1 72.0 all-gather.22
  86.3 65.8 all-gather.20
  155.4 65.8 all-gather.18
  224.2 65.8 all-gather.24
  293.0 66.5 all-gather.26
  362.6 78.6 all-gather.28
  444.4 80.6 all-gather.30
  528.2 72.9 all-gather.16
where the time goes:
time: 1870 us; the launch traced here: 1850 us
  waiting for transfers between devices  993 us (53%)
  other arithmetic  301 us (16%)
  local copies, waits for them, and re-layouts  191 us (10%)
  matrix products  140 us (7%)
  starting transfers between devices  104 us (6%)
  blocking collectives  104 us (6%)
    another operation x5, other arithmetic, reflector_probabilities(): lax.linalg.triangular_solve(system, source, left_side=True, lower=True, u...  243 us
    all_to_all x1, waiting for transfers between devices, body(): lax.all_to_all(stacked(grad_up, owners).astype(jnp.bfloat16), 'fsdp', spl...  208 us
    all_to_all x1, waiting for transfers between devices, body(): lax.all_to_all(stacked(gate_gradient_rows, owners).astype(jnp.bfloat16),...  182 us
    all_to_all x1, waiting for transfers between devices, body(): lax.all_to_all(stacked(grad_down, owners).astype(jnp.bfloat16), 'fsdp', s...  138 us
    unnamed x166, local copies, waits for them, and re-layouts  84.1 us
    unnamed x1, blocking collectives  69.7 us
    all_to_all x1, waiting for transfers between devices, body(): lax.all_to_all(stacked(grad_house, owners).astype(jnp.bfloat16), 'fsdp',...  69.1 us
    all_to_all x1, waiting for transfers between devices, body(): lax.all_to_all(stacked(grad_key, owners).astype(jnp.bfloat16), 'fsdp', sp...  69 us
  transfers between devices with their start and end apart: 19, of which 13 were waited for; matrix products, arithmetic and copies ran while one was open for 31% of the time, Pallas kernels for 0%

commit v1 on v0

v1 whole, which is shorter than its diff:
```python
import functools

import jax
import jax.numpy as jnp
import numpy as np
from jax import lax
from jax.experimental import pallas as pl
from jax.experimental.pallas import tpu as pltpu
from jax.sharding import PartitionSpec as P

EPSILON = 1e-06
BF = jnp.bfloat16
F32 = jnp.float32
VMEM_LIMIT = 56 * 1024 * 1024
AXIS_UNIT = {"x": 16, "z": 4, "y": 1}
ORDERS = ("xzy", "zyx", "yxz")


def step_masks(stream, core):
    masks = []
    for axis in ORDERS[stream]:
        unit = AXIS_UNIT[axis]
        masks += [unit, 3 * unit] if core == 0 else [3 * unit, unit]
    return masks


MASKS = [[step_masks(stream, core) for core in (0, 1)] for stream in range(3)]


def owner_offsets():
    table = np.zeros((2, 3, 64), np.int32)
    for core in (0, 1):
        for stream in range(3):
            for place in range(64):
                value = 0
                for step, mask in enumerate(MASKS[stream][core]):
                    if (place >> (5 - step)) & 1:
                        value ^= mask
                table[core, stream, place] = value
    return table


def dot(left, right):
    return jnp.dot(left, right, preferred_element_type=F32)


def dot_nt(left, right):
    return lax.dot_general(left, right, (((1,), (1,)), ((), ())), preferred_element_type=F32)


def dot_tn(left, right):
    return lax.dot_general(left, right, (((0,), (0,)), ((), ())), preferred_element_type=F32)


def two_parts(value):
    high = value.astype(BF)
    return high, (value - high.astype(F32)).astype(BF)


def dot_fine(left, right):
    size = right.shape[1]
    wide = jnp.concatenate(two_parts(left), axis=1)
    pair = jnp.concatenate(two_parts(right), axis=1)
    out = dot(wide, jnp.concatenate([pair, pair], axis=0))
    return out[:, :size] + out[:, size:]


def swap(value):
    count = lax.axis_size("fsdp")
    return lax.ppermute(value, "fsdp", [(d, d ^ 1) for d in range(count)])


def gain_row(misc_ref, column):
    pick = (lax.broadcasted_iota(jnp.int32, (8, 128), 1) == column).astype(F32).astype(BF)
    return dot_nt(pick, misc_ref[...])[0:1]


def triangles(count):
    row = lax.broadcasted_iota(jnp.int32, (count, count), 0)
    col = lax.broadcasted_iota(jnp.int32, (count, count), 1)
    return row, col


def beta_of(raw, head):
    lane = lax.broadcasted_iota(jnp.int32, raw.shape, 1)
    return jnp.sum(jnp.where(lane == head, raw, 0.0), axis=1, keepdims=True)


def unit_lower_inverse(systems, row, col):
    size = row.shape[0]
    eye = (row == col).astype(F32)
    step = 1
    inverses = None
    while step < size:
        lower = ((row // step) % 2 == 1) & (col // step == row // step - 1)
        parts = [jnp.where(lower, system, 0.0) for system in systems]
        if step == 1:
            inverses = [eye - part for part in parts]
        else:
            middles = [dot_fine(inv, part) for inv, part in zip(inverses, parts)]
            inverses = [inv - dot_fine(mid, inv) for inv, mid in zip(inverses, middles)]
        step *= 2
    return inverses


PER_STEP = 2


def attention_forward_kernel(
    length_ref,
    tokens_ref,
    wq_ref,
    wk_ref,
    wv_ref,
    wh_ref,
    misc_ref,
    normed_ref,
    q_ref,
    k_ref,
    v_ref,
    h_ref,
    att_ref,
    probs_ref,
    carried_ref,
    inverse_ref,
    beta_ref,
):
    at = pl.program_id(0)

    @pl.when(at == 0)
    def _():
        tokens = tokens_ref[...].astype(F32)
        scale = lax.rsqrt(jnp.mean(tokens * tokens, axis=1, keepdims=True) + EPSILON)
        normed_ref[...] = (tokens * scale * gain_row(misc_ref, 12)).astype(BF)
        beta_ref[...] = dot(normed_ref[...], misc_ref[...])

    normed = normed_ref[...]
    q_all = dot(normed, wq_ref[...]).astype(BF)
    k_all = dot(normed, wk_ref[...]).astype(BF)
    v_all = dot(normed, wv_ref[...]).astype(BF)
    h_all = dot(normed, wh_ref[...]).astype(BF)
    q_ref[...] = q_all
    k_ref[...] = k_all
    v_ref[...] = v_all
    h_ref[...] = h_all
    count = q_all.shape[0]
    row, col = triangles(count)
    strict = row > col
    upto = row >= col
    allowed = upto & (col < length_ref[0])
    raw = beta_ref[...]
    heads = range(PER_STEP)
    q, k, v, h = (
        [value[:, 128 * i : 128 * (i + 1)] for i in heads] for value in (q_all, k_all, v_all, h_all)
    )
    big = [
        dot_nt(jnp.concatenate([h[i], q[i]], axis=0), jnp.concatenate([h[i], k[i]], axis=0))
        for i in heads
    ]
    strength = []
    for i in heads:
        house = h[i].astype(F32)
        square = jnp.sum(house * house, axis=1, keepdims=True) + EPSILON
        beta = 2.0 * jax.nn.sigmoid(beta_of(raw, at * PER_STEP + i))
        strength.append(beta / square)
    systems = [jnp.where(strict, strength[i] * big[i][:count, :count], 0.0) for i in heads]
    sources = [jnp.where(strict, strength[i] * big[i][:count, count:], 0.0) for i in heads]
    inverses = unit_lower_inverse(systems, row, col)
    carried = [dot_fine(inverses[i], sources[i]) for i in heads]
    through = [
        dot_fine(jnp.where(upto, big[i][count:, :count], 0.0), carried[i]) for i in heads
    ]
    for i in heads:
        logits = (big[i][count:, count:] - through[i]) * 128 ** (-0.5)
        logits = jnp.where(allowed, logits, -1e30)
        highest = jnp.max(logits, axis=1, keepdims=True)
        weights = jnp.where(allowed, jnp.exp(logits - highest), 0.0)
        probs = weights / jnp.sum(weights, axis=1, keepdims=True)
        probs_ref[i] = probs
        carried_ref[i] = carried[i].astype(BF)
        inverse_ref[i] = inverses[i].astype(BF)
        att_ref[:, 128 * i : 128 * (i + 1)] = dot(probs.astype(BF), v[i]).astype(BF)


def attention_forward(tokens, length, attn):
    count, width = tokens.shape
    steps = width // 256
    cell = (PER_STEP, count, count)
    whole = lambda i, *_: (0, 0)
    column = lambda i, *_: (0, i)
    weight = lambda half, first: pl.BlockSpec(
        (width, 256), lambda i, *_: (half, first + i)
    )
    row_block = pl.BlockSpec((count, 256), column)
    cell_block = pl.BlockSpec(cell, lambda i, *_: (i, 0, 0))
    rows = jax.ShapeDtypeStruct((count, width), BF)
    cells = (2 * steps, count, count)
    return pl.pallas_call(
        attention_forward_kernel,
        grid_spec=pltpu.PrefetchScalarGridSpec(
            num_scalar_prefetch=1,
            grid=(steps,),
            in_specs=[
                pl.BlockSpec((count, width), whole),
                weight(0, 20),
                weight(0, 26),
                weight(1, 20),
                weight(1, 26),
                pl.BlockSpec((width, 128), lambda i, *_: (0, 6)),
            ],
            out_specs=[
                pl.BlockSpec((count, width), whole),
                row_block,
                row_block,
                row_block,
                row_block,
                row_block,
                cell_block,
                cell_block,
                cell_block,
                pl.BlockSpec((count, 128), whole),
            ],
        ),
        out_shape=[
            rows,
            rows,
            rows,
            rows,
            rows,
            rows,
            jax.ShapeDtypeStruct(cells, F32),
            jax.ShapeDtypeStruct(cells, BF),
            jax.ShapeDtypeStruct(cells, BF),
            jax.ShapeDtypeStruct((count, 128), F32),
        ],
        compiler_params=pltpu.CompilerParams(vmem_limit_bytes=VMEM_LIMIT),
        cost_estimate=pl.CostEstimate(
            flops=8 * count * width * width + 12 * 60 * 2 * 128**3,
            bytes_accessed=10 * width * width,
            transcendentals=0,
        ),
        name="attention_forward",
    )(length, tokens, attn, attn, attn, attn, attn)


FF_BLOCK = 512


def feedforward_kernel(
    length_ref,
    tokens_ref,
    att_ref,
    out_lo_ref,
    out_hi_ref,
    misc_ref,
    cot_ref,
    wg_ref,
    wu_ref,
    wd_lo_ref,
    wd_hi_ref,
    second_ref,
    acts_ref,
    mixed_ref,
    hidden_grad_ref,
    branch_ref,
    gain_grad_ref,
    hidden,
    feed,
    second_grad,
):
    at = pl.program_id(0)
    half = out_lo_ref.shape[1]

    @pl.when(at == 0)
    def _():
        att = att_ref[...]
        hidden[:, :half] = tokens_ref[:, :half].astype(F32) + dot(att, out_lo_ref[...])
        hidden[:, half:] = tokens_ref[:, half:].astype(F32) + dot(att, out_hi_ref[...])
        value = hidden[...]
        scale = lax.rsqrt(jnp.mean(value * value, axis=1, keepdims=True) + EPSILON)
        second_ref[...] = (value * scale * gain_row(misc_ref, 13)).astype(BF)
        feed[...] = jnp.zeros_like(feed)
        second_grad[...] = jnp.zeros_like(second_grad)

    second = second_ref[...]
    cot = cot_ref[...]
    gate = dot(second, wg_ref[...])
    upward = dot(second, wu_ref[...])
    sigma = jax.nn.sigmoid(gate)
    silu = gate * sigma
    product = (silu * upward).astype(BF)
    product_grad = dot_nt(cot[:, :half], wd_lo_ref[...]) + dot_nt(cot[:, half:], wd_hi_ref[...])
    gate_low = (product_grad * upward * (sigma * (1.0 + gate * (1.0 - sigma)))).astype(BF)
    up_low = (product_grad * silu).astype(BF)
    acts_ref[0] = product
    acts_ref[1] = gate_low
    acts_ref[2] = up_low
    feed[:, :half] += dot(product, wd_lo_ref[...])
    feed[:, half:] += dot(product, wd_hi_ref[...])
    second_grad[...] += dot_nt(gate_low, wg_ref[...]) + dot_nt(up_low, wu_ref[...])

    @pl.when(at == pl.num_programs(0) - 1)
    def _():
        value = hidden[...]
        valid = lax.broadcasted_iota(jnp.int32, value.shape, 0) < length_ref[0]
        mixed_ref[...] = jnp.where(valid, value + feed[...], 0.0).astype(BF)
        scale = lax.rsqrt(jnp.mean(value * value, axis=1, keepdims=True) + EPSILON)
        grad = second_grad[...]
        scaled = grad * gain_row(misc_ref, 13)
        along = jnp.mean(scaled * value, axis=1, keepdims=True)
        hidden_grad = (
            cot_ref[...].astype(F32) + scale * scaled - value * (scale * scale * scale * along)
        )
        hidden_grad_ref[...] = hidden_grad
        branch_ref[...] = hidden_grad.astype(BF)
        gain_grad_ref[...] = jnp.sum(grad * value * scale, axis=0, keepdims=True)


def feedforward(tokens, length, att, cot, attn, down):
    count, width = tokens.shape
    hidden_units = down.shape[0] // 2
    steps = hidden_units // FF_BLOCK
    half = width // 2
    whole = lambda i, *_: (0, 0)
    rows = pl.BlockSpec((count, width), whole)
    weight = lambda side: pl.BlockSpec(
        (width, FF_BLOCK), lambda i, *_: (side, 1024 // FF_BLOCK + i)
    )
    down_block = lambda side: pl.BlockSpec((FF_BLOCK, half), lambda i, *_: (side * steps + i, 0))
    return pl.pallas_call(
        feedforward_kernel,
        grid_spec=pltpu.PrefetchScalarGridSpec(
            num_scalar_prefetch=1,
            grid=(steps,),
            in_specs=[
                rows,
                rows,
                pl.BlockSpec((width, half), whole),
                pl.BlockSpec((width, half), lambda i, *_: (1, 0)),
                pl.BlockSpec((width, 128), lambda i, *_: (0, 6)),
                rows,
                weight(0),
                weight(1),
                down_block(0),
                down_block(1),
            ],
            out_specs=[
                rows,
                pl.BlockSpec((3, count, FF_BLOCK), lambda i, *_: (0, 0, i)),
                rows,
                rows,
                rows,
                pl.BlockSpec((1, width), whole),
            ],
            scratch_shapes=[
                pltpu.VMEM((count, width), F32),
                pltpu.VMEM((count, width), F32),
                pltpu.VMEM((count, width), F32),
            ],
        ),
        out_shape=[
            jax.ShapeDtypeStruct((count, width), BF),
            jax.ShapeDtypeStruct((3, count, hidden_units), BF),
            jax.ShapeDtypeStruct((count, width), BF),
            jax.ShapeDtypeStruct((count, width), F32),
            jax.ShapeDtypeStruct((count, width), BF),
            jax.ShapeDtypeStruct((1, width), F32),
        ],
        compiler_params=pltpu.CompilerParams(vmem_limit_bytes=VMEM_LIMIT),
        cost_estimate=pl.CostEstimate(
            flops=12 * count * width * hidden_units,
            bytes_accessed=6 * width * hidden_units,
            transcendentals=0,
        ),
        name="feedforward",
    )(length, tokens, att, attn, attn, attn, cot, attn, attn, down, down)


def attention_backward_kernel(
    tokens_ref,
    normed_ref,
    branch_ref,
    hidden_grad_ref,
    ffn_gain_ref,
    beta_ref,
    q_ref,
    k_ref,
    v_ref,
    h_ref,
    probs_ref,
    carried_ref,
    inverse_ref,
    wo_lo_ref,
    wo_hi_ref,
    wq_ref,
    wk_ref,
    wv_ref,
    wh_ref,
    misc_ref,
    grads_ref,
    grad_tokens_ref,
    misc_grad_ref,
    normed_grad,
    beta_grad,
):
    at = pl.program_id(0)
    half = wo_lo_ref.shape[1]

    @pl.when(at == 0)
    def _():
        normed_grad[...] = jnp.zeros_like(normed_grad)
        beta_grad[...] = jnp.zeros_like(beta_grad)

    att_grad_all = (
        dot_nt(branch_ref[:, :half], wo_lo_ref[...]) + dot_nt(branch_ref[:, half:], wo_hi_ref[...])
    ).astype(BF)
    count = att_grad_all.shape[0]
    row, col = triangles(count)
    strict = row > col
    upto = row >= col
    raw = beta_ref[...]
    lane = lax.broadcasted_iota(jnp.int32, raw.shape, 1)
    heads = range(PER_STEP)
    part = lambda ref: [ref[:, 128 * i : 128 * (i + 1)] for i in heads]
    q, k, v, h = part(q_ref), part(k_ref), part(v_ref), part(h_ref)
    att_grad = [att_grad_all[:, 128 * i : 128 * (i + 1)] for i in heads]
    big = [
        dot_nt(jnp.concatenate([h[i], q[i]], axis=0), jnp.concatenate([h[i], k[i]], axis=0))
        for i in heads
    ]
    probs = [probs_ref[i] for i in heads]
    carried = [carried_ref[i] for i in heads]
    inverse = [inverse_ref[i] for i in heads]
    probs_grad = [dot_nt(att_grad[i], v[i]) for i in heads]
    value_grad = [dot_tn(probs[i].astype(BF), att_grad[i]) for i in heads]
    logit_grad = []
    for i in heads:
        total = jnp.sum(probs_grad[i] * probs[i], axis=1, keepdims=True)
        logit_grad.append((probs[i] * (probs_grad[i] - total) * 128 ** (-0.5)).astype(BF))
    through_grad = [
        jnp.where(upto, -dot_nt(logit_grad[i], carried[i]), 0.0).astype(BF) for i in heads
    ]
    carried_grad = [
        -dot_tn(jnp.where(upto, big[i][count:, :count], 0.0).astype(BF), logit_grad[i])
        for i in heads
    ]
    solved = [dot_tn(inverse[i], carried_grad[i].astype(BF)) for i in heads]
    system_grad = [
        jnp.where(strict, -dot_nt(solved[i].astype(BF), carried[i]), 0.0) for i in heads
    ]
    source_grad = [jnp.where(strict, solved[i], 0.0) for i in heads]
    total_beta = jnp.zeros_like(raw)
    q_grads, k_grads, v_grads, h_grads = [], [], [], []
    for i in heads:
        house = h[i].astype(F32)
        inverse_square = 1.0 / (jnp.sum(house * house, axis=1, keepdims=True) + EPSILON)
        sigma = jax.nn.sigmoid(beta_of(raw, at * PER_STEP + i))
        strength = 2.0 * sigma * inverse_square
        key_part = (strength * source_grad[i]).astype(BF)
        self_part = (strength * system_grad[i]).astype(BF)
        strength_grad = jnp.sum(
            source_grad[i] * big[i][:count, count:] + system_grad[i] * big[i][:count, :count],
            axis=1,
            keepdims=True,
        )
        key_house = jnp.concatenate([k[i], h[i]], axis=0)
        query_house = jnp.concatenate([q[i], h[i]], axis=0)
        q_grads.append(
            dot(jnp.concatenate([logit_grad[i], through_grad[i]], axis=1), key_house).astype(BF)
        )
        k_grads.append(
            dot_tn(jnp.concatenate([logit_grad[i], key_part], axis=0), query_house).astype(BF)
        )
        house_grad = (
            dot_tn(jnp.concatenate([through_grad[i], self_part], axis=0), query_house)
            + dot(jnp.concatenate([key_part, self_part], axis=1), key_house)
            - (2.0 * strength_grad * strength * inverse_square) * house
        )
        h_grads.append(house_grad.astype(BF))
        v_grads.append(value_grad[i].astype(BF))
        raw_grad = strength_grad * inverse_square * (2.0 * sigma * (1.0 - sigma))
        total_beta += jnp.where(lane == at * PER_STEP + i, raw_grad, 0.0)
    beta_grad[...] += total_beta
    update = None
    for index, (pieces, weight_ref) in enumerate(
        ((q_grads, wq_ref), (k_grads, wk_ref), (v_grads, wv_ref), (h_grads, wh_ref))
    ):
        joined = jnp.concatenate(pieces, axis=1)
        grads_ref[index] = joined
        term = dot_nt(joined, weight_ref[...])
        update = term if update is None else update + term
    normed_grad[...] += update

    @pl.when(at == pl.num_programs(0) - 1)
    def _():
        beta_low = beta_grad[...].astype(BF)
        grad = normed_grad[...] + dot_nt(beta_low, misc_ref[...])
        value = tokens_ref[...].astype(F32)
        scale = lax.rsqrt(jnp.mean(value * value, axis=1, keepdims=True) + EPSILON)
        scaled = grad * gain_row(misc_ref, 12)
        along = jnp.mean(scaled * value, axis=1, keepdims=True)
        grad_tokens_ref[...] = (
            hidden_grad_ref[...] + scale * scaled - value * (scale * scale * scale * along)
        )
        attn_gain = jnp.sum(grad * value * scale, axis=0, keepdims=True)
        attn_high, attn_low = two_parts(attn_gain)
        ffn_high, ffn_low = two_parts(ffn_gain_ref[...])
        gains = jnp.concatenate(
            [
                attn_high.astype(F32),
                attn_low.astype(F32),
                ffn_high.astype(F32),
                ffn_low.astype(F32),
                jnp.zeros((4, attn_gain.shape[1]), F32),
            ],
            axis=0,
        )
        place = lax.broadcasted_iota(jnp.int32, (8, 128), 0)
        lanes = lax.broadcasted_iota(jnp.int32, (8, 128), 1)
        pick = ((place < 4) & (lanes == 12 + place // 2)).astype(F32)
        misc_grad = dot_tn(normed_ref[...], beta_low) + dot_tn(
            gains.astype(BF), pick.astype(BF)
        )
        misc_grad_ref[...] = misc_grad.astype(BF)


def attention_backward(tokens, normed, branch, hidden_grad, ffn_gain, saved, attn):
    q, k, v, h, probs, carried, inverse, beta = saved
    count, width = tokens.shape
    steps = width // 256
    half = width // 2
    whole = lambda i: (0, 0)
    rows = pl.BlockSpec((count, width), whole)
    row_block = pl.BlockSpec((count, 256), lambda i: (0, i))
    cell_block = pl.BlockSpec((PER_STEP, count, count), lambda i: (i, 0, 0))
    weight = lambda side, first: pl.BlockSpec((width, 256), lambda i: (side, first + i))
    out_rows = lambda side: pl.BlockSpec((256, half), lambda i: (side * steps + i, 0))
    return pl.pallas_call(
        attention_backward_kernel,
        grid=(steps,),
        in_specs=[
            rows,
            rows,
            rows,
            rows,
            pl.BlockSpec((1, width), whole),
            pl.BlockSpec((count, 128), whole),
            row_block,
            row_block,
            row_block,
            row_block,
            cell_block,
            cell_block,
            cell_block,
            out_rows(0),
            out_rows(1),
            weight(0, 20),
            weight(0, 26),
            weight(1, 20),
            weight(1, 26),
            pl.BlockSpec((width, 128), lambda i: (0, 6)),
        ],
        out_specs=[
            pl.BlockSpec((4, count, 256), lambda i: (0, 0, i)),
            rows,
            pl.BlockSpec((width, 128), whole),
        ],
        out_shape=[
            jax.ShapeDtypeStruct((4, count, width), BF),
            jax.ShapeDtypeStruct((count, width), F32),
            jax.ShapeDtypeStruct((width, 128), BF),
        ],
        scratch_shapes=[pltpu.VMEM((count, width), F32), pltpu.VMEM((count, 128), F32)],
        compiler_params=pltpu.CompilerParams(vmem_limit_bytes=VMEM_LIMIT),
        cost_estimate=pl.CostEstimate(
            flops=10 * count * width * width + 12 * 40 * 2 * 128**3,
            bytes_accessed=12 * width * width,
            transcendentals=0,
        ),
        name="attention_backward",
    )(
        tokens,
        normed,
        branch,
        hidden_grad,
        ffn_gain,
        beta,
        q,
        k,
        v,
        h,
        probs,
        carried,
        inverse,
        attn,
        attn,
        attn,
        attn,
        attn,
        attn,
        attn,
    )


def weight_gradient_kernel(place_ref, core_ref, mine_x, other_x, mine_y, other_y, keep, send, xt, hold):
    @pl.when(pl.program_id(0) == 0)
    def _():
        xt[:, :128] = mine_x[...].T
        xt[:, 128:] = other_x[...].T

    height = hold.shape[1]
    chips = hold.shape[0]
    y = jnp.concatenate([mine_y[...], other_y[...]], axis=0)
    group = 8 if height == 24 else 4
    for first in range(0, chips, group):
        part = dot(xt[first * height : (first + group) * height], y)
        for chip in range(group):
            hold[first + chip] = part[chip * height : (chip + 1) * height].astype(BF)
    for place in range(chips // 2):
        keep[place] = hold[place_ref[place]]
        send[place] = hold[place_ref[place + chips // 2]]


def weight_gradient(places, core, mine_x, other_x, mine_y, other_y, height, tile, y_index, tiles):
    x_spec, mine_x, other_x = x_operand(mine_x, other_x)
    width = mine_x.shape[-1]
    count = mine_x.shape[-2]
    chips = width // height
    y_spec = pl.BlockSpec((None, count, tile), y_index)
    out = pl.BlockSpec((chips // 2, height, tile), lambda i, *_: (0, 0, i))
    shape = jax.ShapeDtypeStruct((chips // 2, height, tile * tiles), BF)
    return pl.pallas_call(
        weight_gradient_kernel,
        grid_spec=pltpu.PrefetchScalarGridSpec(
            num_scalar_prefetch=2,
            grid=(tiles,),
            in_specs=[x_spec, x_spec, y_spec, y_spec],
            out_specs=[out, out],
            scratch_shapes=[
                pltpu.VMEM((width, 2 * count), BF),
                pltpu.VMEM((chips, height, tile), BF),
            ],
        ),
        out_shape=[shape, shape],
        compiler_params=pltpu.CompilerParams(vmem_limit_bytes=VMEM_LIMIT),
        cost_estimate=pl.CostEstimate(
            flops=4 * count * width * tile * tiles,
            bytes_accessed=2 * width * tile * tiles,
            transcendentals=0,
        ),
        name="weight_gradient",
    )(places, core, mine_x, other_x, mine_y, other_y)


def x_operand(mine, other):
    if mine.ndim == 3:
        return pl.BlockSpec((None,) + mine.shape[1:], lambda i, *_: (0, 0, 0)), mine, other
    return pl.BlockSpec(mine.shape, lambda i, *_: (0, 0)), mine, other


def add_kernel(*refs):
    n = len(refs) // 6
    ins, outs = refs[: 4 * n], refs[4 * n :]
    for s in range(n):
        keep_lo, keep_hi, got_lo, got_hi = ins[4 * s : 4 * s + 4]
        outs[2 * s][...] = keep_lo[...] + got_lo[...]
        outs[2 * s + 1][...] = keep_hi[...] + got_hi[...]


def add_halves(keeps, gots):
    rows = keeps[0].shape[0] // 2
    grid = max(1, rows // 2)
    block = rows // grid
    operands, in_specs, out_specs, shapes = [], [], [], []
    for keep, got in zip(keeps, gots):
        shape = (block,) + keep.shape[1:]
        low = pl.BlockSpec(shape, lambda i: (i, 0, 0))
        high = pl.BlockSpec(shape, lambda i: (i + grid, 0, 0))
        operands += [keep, keep, got, got]
        in_specs += [low, high, low, high]
        out_specs += [low, low]
        shapes += [jax.ShapeDtypeStruct((rows,) + keep.shape[1:], BF)] * 2
    size = sum(int(np.prod(k.shape)) for k in keeps)
    outs = pl.pallas_call(
        add_kernel,
        grid=(grid,),
        in_specs=in_specs,
        out_specs=out_specs,
        out_shape=shapes,
        compiler_params=pltpu.CompilerParams(vmem_limit_bytes=VMEM_LIMIT),
        cost_estimate=pl.CostEstimate(flops=size, bytes_accessed=6 * size, transcendentals=0),
        name="add_halves",
    )(*operands)
    return outs[0::2], outs[1::2]


def send_step(value, stream, step):
    count = lax.axis_size("fsdp")
    pairs = [(d, d ^ (2 * MASKS[stream][d & 1][step])) for d in range(count)]
    return lax.ppermute(value, "fsdp", pairs)


def reduce_streams(keeps, sends):
    for step in range(6):
        gots = [send_step(send, stream, step) for stream, send in enumerate(sends)]
        if step == 5:
            return [(keep + got)[0] for keep, got in zip(keeps, gots)]
        keeps, sends = add_halves(keeps, gots)


def own_rows(block, core):
    rows = block.shape[0] // 2
    first = jnp.where(core == 0, block[:rows], block[rows:])
    second = jnp.where(core == 0, block[rows:], block[:rows])
    return first, swap(second)


def both_halves(mine, other, core):
    left = jnp.where(core == 0, mine, other)
    right = jnp.where(core == 0, other, mine)
    return jnp.concatenate([left, right], axis=1).astype(F32)


def body(
    tokens,
    lengths,
    gain_attn,
    w_query,
    w_key,
    w_value,
    w_house,
    w_beta,
    w_out,
    gain_ffn,
    w_gate,
    w_up,
    w_down,
    cotangent,
):
    seqs, count, width = tokens.shape
    heads = w_beta.shape[1]
    hidden_units = w_gate.shape[1]
    half = width // 2
    devices = lax.axis_size("fsdp")
    me = lax.axis_index("fsdp")
    core, chip = me % 2, me // 2
    offsets = jnp.asarray(owner_offsets())
    places = jnp.where(core == 0, offsets[0], offsets[1]) ^ chip
    core_at = core.astype(jnp.int32)[None]

    misc = jnp.concatenate(
        [
            w_beta,
            gain_attn[:, None],
            gain_ffn[:, None],
            jnp.zeros((w_beta.shape[0], 256 - heads - 2), BF),
        ],
        axis=1,
    )
    pack_a = jnp.concatenate([w_out[:, :half], misc, w_gate, w_query, w_key], axis=1)
    pack_b = jnp.concatenate([w_out[:, half:], misc, w_up, w_value, w_house], axis=1)
    mine = jnp.where(core == 0, pack_a, pack_b)
    theirs = swap(jnp.where(core == 0, pack_b, pack_a))
    slab = jnp.where(
        core == 0,
        jnp.concatenate([mine, theirs], axis=0),
        jnp.concatenate([theirs, mine], axis=0),
    )
    mine = jnp.where(core == 0, w_down[:, :half], w_down[:, half:])
    theirs = swap(jnp.where(core == 0, w_down[:, half:], w_down[:, :half]))
    slab_down = jnp.where(
        core == 0,
        jnp.concatenate([mine, theirs], axis=0),
        jnp.concatenate([theirs, mine], axis=0),
    )
    by_core = [[*range(0, devices, 2), *range(1, devices, 2)]]
    attn = lax.all_gather(slab, "fsdp", axis=0, tiled=True, axis_index_groups=by_core)
    down = lax.all_gather(slab_down, "fsdp", axis=0, tiled=True, axis_index_groups=by_core)

    flat = tokens.reshape(count, width)
    valid = lax.broadcasted_iota(jnp.int32, (count, 1), 0) < lengths[0]
    cot = jnp.where(valid, cotangent.reshape(count, width), jnp.zeros((), BF))
    cot_other = swap(cot)

    normed, q, k, v, h, att, probs, carried, inverse, beta = attention_forward(flat, lengths, attn)
    normed_other, att_other = swap(normed), swap(att)
    second, acts, mixed, hidden_grad, branch, ffn_gain = feedforward(
        flat, lengths, att, cot, attn, down
    )
    second_other, acts_other, branch_other = swap(second), swap(acts), swap(branch)

    unit = hidden_units // 2 // 512
    pairs = [
        weight_gradient(
            places[0],
            core_at,
            second,
            second_other,
            acts,
            acts_other,
            24,
            512,
            lambda i, _, c: (1, 0, unit * c[0] + i),
            unit,
        ),
        weight_gradient(
            places[1],
            core_at,
            second,
            second_other,
            acts,
            acts_other,
            24,
            512,
            lambda i, _, c: (2, 0, unit * c[0] + i),
            unit,
        ),
        weight_gradient(
            places[2],
            core_at,
            acts,
            acts_other,
            cot[None],
            cot_other[None],
            64,
            256,
            lambda i, _, c: (0, 0, 3 * c[0] + i),
            3,
        ),
    ]
    gate_sum, up_sum, down_sum = reduce_streams([p[0] for p in pairs], [p[1] for p in pairs])

    grads, grad_tokens, misc_grad = attention_backward(
        flat, normed, branch, hidden_grad, ffn_gain, (q, k, v, h, probs, carried, inverse, beta), attn
    )
    grads_other = swap(grads)
    tile_index = lambda first: lambda i, _, c: ((first + i) // 3, 0, 3 * c[0] + (first + i) % 3)
    qkvh = lambda stream, first, tiles: weight_gradient(
        places[stream],
        core_at,
        normed,
        normed_other,
        grads,
        grads_other,
        24,
        256,
        tile_index(first),
        tiles,
    )
    out_pair = weight_gradient(
        places[2],
        core_at,
        att,
        att_other,
        branch[None],
        branch_other[None],
        24,
        256,
        lambda i, _, c: (0, 0, 3 * c[0] + i),
        3,
    )
    misc_blocks = misc_grad.reshape(-1, 24, 128)[places[2]]
    last_pair = qkvh(2, 10, 2)
    cut = misc_blocks.shape[0] // 2
    pairs = [
        qkvh(0, 0, 5),
        qkvh(1, 5, 5),
        [
            jnp.concatenate([last_pair[0], out_pair[0], misc_blocks[:cut]], axis=2),
            jnp.concatenate([last_pair[1], out_pair[1], misc_blocks[cut:]], axis=2),
        ],
    ]
    sums = reduce_streams([p[0] for p in pairs], [p[1] for p in pairs])

    gate_up = jnp.concatenate([gate_sum, up_sum], axis=1)
    mine, other = own_rows(gate_up, core)
    part = hidden_units // 2
    grad_gate = both_halves(mine[:, :part], other[:, :part], core)
    grad_up = both_halves(mine[:, part:], other[:, part:], core)
    mine, other = own_rows(down_sum, core)
    grad_down = both_halves(mine, other, core)
    joined = jnp.concatenate(sums, axis=1)
    mine, other = own_rows(joined, core)
    small = [
        both_halves(mine[:, half * i : half * (i + 1)], other[:, half * i : half * (i + 1)], core)
        for i in range(5)
    ]
    misc_sum = mine[:, 5 * half :].astype(F32) + other[:, 5 * half :].astype(F32)
    return (
        mixed.reshape(seqs, count, width),
        grad_tokens.reshape(seqs, count, width),
        misc_sum[:, heads],
        small[0],
        small[1],
        small[2],
        small[3],
        misc_sum[:, :heads],
        small[4],
        misc_sum[:, heads + 1],
        grad_gate,
        grad_up,
        grad_down,
    )


def solution(mesh):
    rows = P("fsdp", None)
    line = P("fsdp")
    cube = P("fsdp", None, None)
    in_specs = (cube, line, line, rows, rows, rows, rows, rows, rows, line, rows, rows, rows, cube)
    out_specs = (cube, cube, line, rows, rows, rows, rows, rows, rows, line, rows, rows, rows)
    return jax.shard_map(body, mesh=mesh, in_specs=in_specs, out_specs=out_specs, check_vma=False)
```

time: 1870 us -> 580 us (0.31)
  waiting for transfers between devices: 993 us -> 309 us
  other arithmetic: 301 us -> 15.6 us
  local copies, waits for them, and re-layouts: 191 us -> 21.8 us
  Pallas kernels: 0 us -> 161 us
  matrix products: 140 us -> 0 us
  blocking collectives: 104 us -> 0 us
  starting transfers between devices: 104 us -> 56.4 us
    all_to_all x11 -> x0, waiting for transfers between devices: 860 us -> none  [the longest x1 208 us: body(): lax.all_to_all(stacked(grad_up, owners).astype(jnp.bfloat16), 'fsdp', spl...]
    another operation x5 -> x0, other arithmetic: 243 us -> none  [reflector_probabilities(): lax.linalg.triangular_solve(system, source, left_side=True, lower=True, u...]
    pallas_call x0 -> x20, Pallas kernels: none -> 161 us  [the longest x10 47.4 us: add_halves(): pl.pallas_call(add_kernel, grid=(grid,), in_specs=in_specs, out_specs=out...]
    dot_general x46 -> x0, matrix products: 133 us -> none  [the longest x9 39.4 us: matmul_nt(): lax.dot_general(left, right, (((1,), (1,)), ((), ())), preferred_element_...]
    ppermute x0 -> x48, waiting for transfers between devices: none -> 121 us  [the longest x36 117 us: send_step(): return lax.ppermute(value, 'fsdp', pairs)]
    all_to_all x11 -> x0, starting transfers between devices: 104 us -> none  [the longest x1 15.9 us: body(): lax.all_to_all(stacked(grad_up, owners).astype(jnp.bfloat16), 'fsdp', spl...]
    convert_element_type x16 -> x0, local copies, waits for them, and re-layouts: 98.5 us -> none  [the longest x1 27.5 us: body(): stacked(grad_down, owners).astype(jnp.bfloat16)]
    unnamed x166 -> x86, local copies, waits for them, and re-layouts: 84.1 us -> 12.8 us
  transfers between devices with their start and end apart: 19 -> 50, of which waited for: 13 -> 29; matrix products, arithmetic and copies ran while one was open for 31% -> 3% of each run, Pallas kernels for 0% -> 17%
where the time goes in v1:
time: 580 us; the launch traced here: 578 us
  waiting for transfers between devices  309 us (53%)
  Pallas kernels  161 us (28%)
  starting transfers between devices  56.4 us (10%)
  local copies, waits for them, and re-layouts  21.8 us (4%)
  other arithmetic  15.6 us (3%)
  between operations  15.2 us (3%)
    all_gather x1, waiting for transfers between devices, body(): lax.all_gather(slab, 'fsdp', axis=0, tiled=True, axis_index_groups=by_core)  133 us
    ppermute x36, waiting for transfers between devices, send_step(): return lax.ppermute(value, 'fsdp', pairs)  117 us
    all_gather x1, waiting for transfers between devices, body(): lax.all_gather(slab_down, 'fsdp', axis=0, tiled=True, axis_index_groups=b...  54.7 us
    pallas_call x10, Pallas kernels, add_halves(): pl.pallas_call(add_kernel, grid=(grid,), in_specs=in_specs, out_specs=out...  47.4 us
    pallas_call x7, Pallas kernels, weight_gradient(): pl.pallas_call(weight_gradient_kernel, grid_spec=pltpu.PrefetchScalarGrid...  43.6 us
    ppermute x36, starting transfers between devices, send_step(): return lax.ppermute(value, 'fsdp', pairs)  29.7 us
    pallas_call x1, Pallas kernels, feedforward(): pl.pallas_call(feedforward_kernel, grid_spec=pltpu.PrefetchScalarGridSpec...  27 us
    ppermute x12, starting transfers between devices, swap(): return lax.ppermute(value, 'fsdp', [(d, d ^ 1) for d in range(count)])  26.6 us
  transfers between devices with their start and end apart: 50, of which 29 were waited for; matrix products, arithmetic and copies ran while one was open for 3% of the time, Pallas kernels for 17%

profile of v1, /device:TPU:1, one launch (start us, length us, event | category | flops | bytes accessed | tf_op | source)
XLA Modules:
  0.0 578.4 jit_solution(10870885429347163466)
XLA Ops:
  19.4 133.4 %all-gather.3.cloned.1.call-done.wq_ref.wk_ref.wv_ref.wh_ref.misc_ref.out_lo_ref.out_hi_ref.wg_ref.wu_ref.wo_lo_ref.wo_hi_ref = bf16[3072,8192]{1,0:T(8,128)(2,1)} async-done(((bf16[24,8192]{1,0:T(8,128)(2,1)}), bf16[3072,8192]{1,0:T(8,128)(2,1)}) %all-gather.3.cloned.1.call-update) | async-done | bytes 50331664 | tf_op jit(solution)/shard_map/all_gather | solution.py:777
  152.7 21.6 %attention_forward.1 = (bf16[128,1536]{1,0:T(8,128)(2,1)}, bf16[128,1536]{1,0:T(8,128)(2,1)}, bf16[128,1536]{1,0:T(8,128)(2,1)}, bf16[128,1536]{1,0:T(8,128)(2,1...) custom-call(s32[1]{0:T(128)} %copy.36.length_ref, ...), custom_call_target="tpu_custom_call" | custom-call | flops 5435817984 | bytes 23592960 | tf_op jit(solution)/shard_map/attention_forward/pallas_call | solution.py:198
  174.4 54.7 %all-gather.5.cloned.1.call-done.wd_lo_ref.wd_hi_ref = bf16[8192,768]{1,0:T(8,128)(2,1)} async-done(((bf16[64,768]{1,0:T(8,128)(2,1)}), bf16[8192,768]{1,0:T(8,128)(2,1)}) %all-gather.5.cloned.1.call-update) | async-done | bytes 12582928 | tf_op jit(solution)/shard_map/all_gather | solution.py:778
  229.0 27.0 %feedforward.1 = (bf16[128,1536]{1,0:T(8,128)(2,1)}, bf16[3,128,4096]{2,1,0:T(8,128)(2,1)}, bf16[128,1536]{1,0:T(8,128)(2,1)}, f32[128,1536]{1,0:T(8,128)}, bf16...) custom-call(s32[1]{0:T(128)} %copy.36.length_ref, bf16[128,1536]{1,0:T(8,128)(2,1)} %bitcast.41, ...), custom_call_target="tpu_custom_call" | custom-call | flops 9663676416 | bytes 37748736 | tf_op jit(solution)/shard_map/feedforward/pallas_call | solution.py:330
  256.1 20.9 %attention_backward.1 = (bf16[4,128,1536]{2,1,0:T(8,128)(2,1)}, f32[128,1536]{1,0:T(8,128)}, bf16[1536,128]{1,0:T(8,128)(2,1)}) custom-call(bf16[128,1536]{1,0:T(8,128)(2,1)} %bitcast.42, bf16[128,1536]{1,0:T(8,128)(2,1)} %get-tuple-element.108.normed_ref.mine_x, bf16[128,1536]{1,0:T(8,128)(2,1)} %get-tuple-element.109.branch_ref, ...), custom_call_target="tpu_custom_call" | custom-call | flops 5033164800 | bytes 28311552 | tf_op jit(solution)/shard_map/attention_backward/pallas_call | solution.py:538
  283.1 5.0 weight_gradient.10
  288.2 4.1 weight_gradient.9
  297.4 6.5 %weight_gradient.7 = (bf16[32,24,1280]{2,1,0:T(8,128)(2,1)}, bf16[32,24,1280]{2,1,0:T(8,128)(2,1)}) custom-call(s32[64]{0:T(128)} %get-tuple-element.230.place_ref, s32[1]{0:T(128)} %bitcast.8.core_ref, bf16[128,1536]{1,0:T(8,128)(2,1)} %get-tuple-element.108.normed_ref.mine_x, bf16[128,1536]{1,0:T(8,128)(2,1)} %collective-permute-done.2.other_x, ...), custom_call_target="tpu_custom_call" | custom-call | flops 1006632960 | bytes 3932160 | tf_op jit(solution)/shard_map/weight_gradient/pallas_call | solution.py:632
  306.3 6.5 %weight_gradient.8 = (bf16[32,24,1280]{2,1,0:T(8,128)(2,1)}, bf16[32,24,1280]{2,1,0:T(8,128)(2,1)}) custom-call(s32[64]{0:T(128)} %get-tuple-element.229.place_ref, s32[1]{0:T(128)} %bitcast.8.core_ref, bf16[128,1536]{1,0:T(8,128)(2,1)} %get-tuple-element.108.normed_ref.mine_x, bf16[128,1536]{1,0:T(8,128)(2,1)} %collective-permute-done.2.other_x, ...), custom_call_target="tpu_custom_call" | custom-call | flops 1006632960 | bytes 3932160 | tf_op jit(solution)/shard_map/weight_gradient/pallas_call | solution.py:632
  313.3 3.0 pad_maximum_fusion.refs_8_.refs_9_
  316.4 12.4 %collective-permute-done.4.refs_2_.refs_3_ = bf16[32,24,1280]{2,1,0:T(8,128)(2,1)S(1)} collective-permute-done((bf16[32,24,1280]{2,1,0:T(8,128)(2,1)}, bf16[32,24,1280]{2,1,0:T(8,128)(2,1)S(1)}, u32[]{:S(2)}, u32[]{:S(2)}) %collective-permute-start.4) | collective-permute-done | bytes 1966112 | tf_op jit(solution)/shard_map/ppermute | solution.py:700
  328.8 8.9 %collective-permute-done.5.refs_6_.refs_7_ = bf16[32,24,1280]{2,1,0:T(8,128)(2,1)S(1)} collective-permute-done((bf16[32,24,1280]{2,1,0:T(8,128)(2,1)}, bf16[32,24,1280]{2,1,0:T(8,128)(2,1)S(1)}, u32[]{:S(2)}, u32[]{:S(2)}) %collective-permute-start.5) | collective-permute-done | bytes 1966112 | tf_op jit(solution)/shard_map/ppermute | solution.py:700
  340.3 9.1 %add_halves.10 = (bf16[16,24,1280]{2,1,0:T(8,128)(2,1)}, bf16[16,24,1280]{2,1,0:T(8,128)(2,1)}, bf16[16,24,1280]{2,1,0:T(8,128)(2,1)}, bf16[16,24,1280]{2,1,0:T(...) custom-call(bf16[32,24,1280]{2,1,0:T(8,128)(2,1)} %get-tuple-element.122.refs_0_.refs_1_, ...), custom_call_target="tpu_custom_call" | custom-call | flops 3047424 | bytes 18284544 | tf_op jit(solution)/shard_map/add_halves/pallas_call | solution.py:684
  350.4 6.9 %weight_gradient.11 = (bf16[32,24,2048]{2,1,0:T(8,128)(2,1)}, bf16[32,24,2048]{2,1,0:T(8,128)(2,1)}) custom-call(s32[64]{0:T(128)} %get-tuple-element.230.place_ref, s32[1]{0:T(128)} %bitcast.8.core_ref, bf16[128,1536]{1,0:T(8,128)(2,1)} %get-tuple-element.161.mine_x, bf16[128,1536]{1,0:T(8,128)(2,1)} %collective-permute-done.25.other_x, ...), custom_call_target="tpu_custom_call" | custom-call | flops 1610612736 | bytes 6291456 | tf_op jit(solution)/shard_map/weight_gradient/pallas_call | solution.py:632
  358.2 6.9 %weight_gradient.12 = (bf16[32,24,2048]{2,1,0:T(8,128)(2,1)}, bf16[32,24,2048]{2,1,0:T(8,128)(2,1)}) custom-call(s32[64]{0:T(128)} %get-tuple-element.229.place_ref, s32[1]{0:T(128)} %bitcast.8.core_ref, bf16[128,1536]{1,0:T(8,128)(2,1)} %get-tuple-element.161.mine_x, bf16[128,1536]{1,0:T(8,128)(2,1)} %collective-permute-done.25.other_x, ...), custom_call_target="tpu_custom_call" | custom-call | flops 1610612736 | bytes 6291456 | tf_op jit(solution)/shard_map/weight_gradient/pallas_call | solution.py:632
  366.8 7.5 %weight_gradient.13 = (bf16[32,64,768]{2,1,0:T(8,128)(2,1)}, bf16[32,64,768]{2,1,0:T(8,128)(2,1)}) custom-call(s32[64]{0:T(128)} %get-tuple-element.228.place_ref, s32[1]{0:T(128)} %bitcast.8.core_ref, bf16[3,128,4096]{2,1,0:T(8,128)(2,1)} %get-tuple-element.162.mine_y.mine_x, bf16[3,128,4096]{2,1,0:T(8,128)(2,1)} %collective-permute-done.26.other_y.other_x, ...), custom_call_target="tpu_custom_call" | custom-call | flops 1610612736 | bytes 6291456 | tf_op jit(solution)/shard_map/weight_gradient/pallas_call | solution.py:632
  375.0 24.1 %collective-permute-done.10.refs_6_.refs_7_ = bf16[16,24,1280]{2,1,0:T(8,128)(2,1)S(1)} collective-permute-done((bf16[16,24,1280]{2,1,0:T(8,128)(2,1)}, bf16[16,24,1280]{2,1,0:T(8,128)(2,1)S(1)}, u32[]{:S(2)}, u32[]{:S(2)}) %collective-permute-start.10) | collective-permute-done | bytes 983072 | tf_op jit(solution)/shard_map/ppermute | solution.py:700
  402.3 5.0 add_halves.11
  409.7 8.8 %collective-permute-done.12.refs_2_.refs_3_ = bf16[8,24,1280]{2,1,0:T(8,128)(2,1)S(1)} collective-permute-done((bf16[8,24,1280]{2,1,0:T(8,128)(2,1)}, bf16[8,24,1280]{2,1,0:T(8,128)(2,1)S(1)}, u32[]{:S(2)}, u32[]{:S(2)}) %collective-permute-start.12) | collective-permute-done | bytes 491552 | tf_op jit(solution)/shard_map/ppermute | solution.py:700
  418.7 10.0 %collective-permute-done.13.refs_6_.refs_7_ = bf16[8,24,1280]{2,1,0:T(8,128)(2,1)S(1)} collective-permute-done((bf16[8,24,1280]{2,1,0:T(8,128)(2,1)}, bf16[8,24,1280]{2,1,0:T(8,128)(2,1)S(1)}, u32[]{:S(2)}, u32[]{:S(2)}) %collective-permute-start.13) | collective-permute-done | bytes 491552 | tf_op jit(solution)/shard_map/ppermute | solution.py:700
  429.7 2.9 add_halves.12
  433.6 4.6 collective-permute-done.15.refs_2_.refs_3_
  438.2 5.5 collective-permute-done.16.refs_6_.refs_7_
  448.1 4.2 collective-permute-done.18.refs_2_.refs_3_
  452.8 4.7 collective-permute-done.19.refs_6_.refs_7_
  462.8 11.6 %add_halves.15 = (bf16[16,24,2048]{2,1,0:T(8,128)(2,1)}, bf16[16,24,2048]{2,1,0:T(8,128)(2,1)}, bf16[16,24,2048]{2,1,0:T(8,128)(2,1)}, bf16[16,24,2048]{2,1,0:T(...) custom-call(bf16[32,24,2048]{2,1,0:T(8,128)(2,1)} %get-tuple-element.163.refs_0_.refs_1_, ...), custom_call_target="tpu_custom_call" | custom-call | flops 4718592 | bytes 28311552 | tf_op jit(solution)/shard_map/add_halves/pallas_call | solution.py:684
  478.0 16.3 %collective-permute-done.31.refs_2_.refs_3_ = bf16[16,24,2048]{2,1,0:T(8,128)(2,1)S(1)} collective-permute-done((bf16[16,24,2048]{2,1,0:T(8,128)(2,1)}, bf16[16,24,2048]{2,1,0:T(8,128)(2,1)S(1)}, u32[]{:S(2)}, u32[]{:S(2)}) %collective-permute-start.31) | collective-permute-done | bytes 1572896 | tf_op jit(solution)/shard_map/ppermute | solution.py:700
  498.3 6.2 %add_halves.16 = (bf16[8,24,2048]{2,1,0:T(8,128)(2,1)}, bf16[8,24,2048]{2,1,0:T(8,128)(2,1)}, bf16[8,24,2048]{2,1,0:T(8,128)(2,1)}, bf16[8,24,2048]{2,1,0:T(8,12...) custom-call(bf16[16,24,2048]{2,1,0:T(8,128)(2,1)} %get-tuple-element.169.refs_0_.refs_1_, ...), custom_call_target="tpu_custom_call" | custom-call | flops 2359296 | bytes 14155776 | tf_op jit(solution)/shard_map/add_halves/pallas_call | solution.py:684
  507.5 7.2 %collective-permute-start.24 = (bf16[12,3968]{1,0:T(8,128)(2,1)S(1)}, bf16[12,3968]{1,0:T(8,128)(2,1)S(1)}, u32[]{:S(2)}, u32[]{:S(2)}) collective-permute-start(bf16[12,3968]{1,0:T(8,128)(2,1)S(1)} %get-tuple-element.221), channel_id=1, source_target_pairs={{0,1},{1,0},{2,3},{3,2},{4,5},{5,4},{6,7},{7,6},{8,9},{9,8},{10,11... | collective-permute-start | bytes 285704 | tf_op jit(solution)/shard_map/ppermute | solution.py:70
  518.7 3.6 add_halves.17
  539.1 4.5 collective-permute-done.40.refs_2_.refs_3_
  552.0 14.0 %collective-permute-start.47 = (bf16[32,768]{1,0:T(8,128)(2,1)S(1)}, bf16[32,768]{1,0:T(8,128)(2,1)S(1)}, u32[]{:S(2)}, u32[]{:S(2)}) collective-permute-start(bf16[32,768]{1,0:T(8,128)(2,1)S(1)} %select_bitcast_fusion), channel_id=1, source_target_pairs={{0,1},{1,0},{2,3},{3,2},{4,5},{5,4},{6,7},{7,6},{8,9},{9,8},{10,11... | collective-permute-start | bytes 147464 | tf_op jit(solution)/shard_map/ppermute | solution.py:70
  (218 shorter events, 95.2 us)
Async XLA Ops:
  7.2 145.5 %all-gather.3.cloned.1.call-start = ((), (), s32[]{:S(2)}) async-start(), calls=%async_computation | async-start | bytes 50724864 | tf_op jit(solution)/shard_map/all_gather | solution.py:777
  15.3 213.8 %all-gather.5.cloned.1.call-start = ((), (), s32[]{:S(2)}) async-start(), calls=%async_computation.1 | async-start | bytes 12681216 | tf_op jit(solution)/shard_map/all_gather | solution.py:778
  277.0 11.1 %collective-permute-start.3 = (bf16[4,128,1536]{2,1,0:T(8,128)(2,1)}, bf16[4,128,1536]{2,1,0:T(8,128)(2,1)}, u32[]{:S(2)}, u32[]{:S(2)}) collective-permute-start(bf16[4,128,1536]{2,1,0:T(8,128)(2,1)} %get-tuple-element.121.mine_y), channel_id=1, source_target_pairs={{0,1},{1,0},{2,3},{3,2},{4,5},{5,4},{6,7},{7,6},{8,9},{9,8},{10,11... | collective-permute-start | bytes 4718600 | tf_op jit(solution)/shard_map/ppermute | solution.py:70
  278.7 71.7 %collective-permute-start.26 = (bf16[3,128,4096]{2,1,0:T(8,128)(2,1)S(1)}, bf16[3,128,4096]{2,1,0:T(8,128)(2,1)}, u32[]{:S(2)}, u32[]{:S(2)}) collective-permute-start(bf16[3,128,4096]{2,1,0:T(8,128)(2,1)S(1)} %copy-done), channel_id=1, source_target_pairs={{0,1},{1,0},{2,3},{3,2},{4,5},{5,4},{6,7},{7,6},{8,9},{9,8},{10,11... | collective-permute-start | bytes 9437192 | tf_op jit(solution)/shard_map/ppermute | solution.py:70
  294.9 42.8 %collective-permute-start.8 = (bf16[32,24,1408]{2,1,0:T(8,128)(2,1)}, bf16[32,24,1408]{2,1,0:T(8,128)(2,1)S(1)}, u32[]{:S(2)}, u32[]{:S(2)}) collective-permute-start(bf16[32,24,1408]{2,1,0:T(8,128)(2,1)} %pad_maximum_fusion.1), channel_id=1, source_target_pairs={{0,2},{1,7},{2,0},{3,5},{4,6},{5,3},{6,4},{7,1},{8,10},{9,15},{10,... | collective-permute-start | bytes 6488072 | tf_op jit(solution)/shard_map/ppermute | solution.py:700
  303.9 24.9 %collective-permute-start.4 = (bf16[32,24,1280]{2,1,0:T(8,128)(2,1)}, bf16[32,24,1280]{2,1,0:T(8,128)(2,1)S(1)}, u32[]{:S(2)}, u32[]{:S(2)}) collective-permute-start(bf16[32,24,1280]{2,1,0:T(8,128)(2,1)} %get-tuple-element.123), channel_id=1, source_target_pairs={{0,32},{1,97},{2,34},{3,99},{4,36},{5,101},{6,38},{7,103},{8,40},{... | collective-permute-start | bytes 5898248 | tf_op jit(solution)/shard_map/ppermute | solution.py:700
  312.8 24.9 %collective-permute-start.5 = (bf16[32,24,1280]{2,1,0:T(8,128)(2,1)}, bf16[32,24,1280]{2,1,0:T(8,128)(2,1)S(1)}, u32[]{:S(2)}, u32[]{:S(2)}) collective-permute-start(bf16[32,24,1280]{2,1,0:T(8,128)(2,1)} %get-tuple-element.125), channel_id=1, source_target_pairs={{0,8},{1,25},{2,10},{3,27},{4,12},{5,29},{6,14},{7,31},{8,0},{9,17... | collective-permute-start | bytes 5898248 | tf_op jit(solution)/shard_map/ppermute | solution.py:700
  313.3 53.5 %collective-permute-start.29 = (bf16[128,1536]{1,0:T(8,128)(2,1)}, bf16[128,1536]{1,0:T(8,128)(2,1)}, u32[]{:S(2)}, u32[]{:S(2)}) collective-permute-start(bf16[128,1536]{1,0:T(8,128)(2,1)} %bitcast_select_fusion.cot_ref), channel_id=1, source_target_pairs={{0,1},{1,0},{2,3},{3,2},{4,5},{5,4},{6,7},{7,6},{8,9},{9,8},{10,11... | collective-permute-start | bytes 1179656 | tf_op jit(solution)/shard_map/ppermute | solution.py:70
  328.8 21.6 %collective-permute-start.25 = (bf16[128,1536]{1,0:T(8,128)(2,1)S(1)}, bf16[128,1536]{1,0:T(8,128)(2,1)}, u32[]{:S(2)}, u32[]{:S(2)}) collective-permute-start(bf16[128,1536]{1,0:T(8,128)(2,1)S(1)} %copy-done.23), channel_id=1, source_target_pairs={{0,1},{1,0},{2,3},{3,2},{4,5},{5,4},{6,7},{7,6},{8,9},{9,8},{10,11... | collective-permute-start | bytes 1179656 | tf_op jit(solution)/shard_map/ppermute | solution.py:70
  349.4 25.6 %collective-permute-start.9 = (bf16[16,24,1280]{2,1,0:T(8,128)(2,1)}, bf16[16,24,1280]{2,1,0:T(8,128)(2,1)}, u32[]{:S(2)}, u32[]{:S(2)}) collective-permute-start(bf16[16,24,1280]{2,1,0:T(8,128)(2,1)} %get-tuple-element.132), channel_id=1, source_target_pairs={{0,96},{1,33},{2,98},{3,35},{4,100},{5,37},{6,102},{7,39},{8,104},... | collective-permute-start | bytes 2949128 | tf_op jit(solution)/shard_map/ppermute | solution.py:700
  357.3 102.9 %collective-permute-start.27 = (bf16[32,24,2048]{2,1,0:T(8,128)(2,1)}, bf16[32,24,2048]{2,1,0:T(8,128)(2,1)S(1)}, u32[]{:S(2)}, u32[]{:S(2)}) collective-permute-start(bf16[32,24,2048]{2,1,0:T(8,128)(2,1)} %get-tuple-element.164), channel_id=1, source_target_pairs={{0,32},{1,97},{2,34},{3,99},{4,36},{5,101},{6,38},{7,103},{8,40},{... | collective-permute-start | bytes 9437192 | tf_op jit(solution)/shard_map/ppermute | solution.py:700
  365.1 95.3 %collective-permute-start.28 = (bf16[32,24,2048]{2,1,0:T(8,128)(2,1)}, bf16[32,24,2048]{2,1,0:T(8,128)(2,1)S(1)}, u32[]{:S(2)}, u32[]{:S(2)}) collective-permute-start(bf16[32,24,2048]{2,1,0:T(8,128)(2,1)} %get-tuple-element.166), channel_id=1, source_target_pairs={{0,8},{1,25},{2,10},{3,27},{4,12},{5,29},{6,14},{7,31},{8,0},{9,17... | collective-permute-start | bytes 9437192 | tf_op jit(solution)/shard_map/ppermute | solution.py:700
  374.3 86.1 %collective-permute-start.30 = (bf16[32,64,768]{2,1,0:T(8,128)(2,1)}, bf16[32,64,768]{2,1,0:T(8,128)(2,1)}, u32[]{:S(2)}, u32[]{:S(2)}) collective-permute-start(bf16[32,64,768]{2,1,0:T(8,128)(2,1)} %get-tuple-element.168), channel_id=1, source_target_pairs={{0,2},{1,7},{2,0},{3,5},{4,6},{5,3},{6,4},{7,1},{8,10},{9,15},{10,... | collective-permute-start | bytes 9437192 | tf_op jit(solution)/shard_map/ppermute | solution.py:700
  375.0 26.3 %collective-permute-start.11 = (bf16[16,24,1408]{2,1,0:T(8,128)(2,1)}, bf16[16,24,1408]{2,1,0:T(8,128)(2,1)S(1)}, u32[]{:S(2)}, u32[]{:S(2)}) collective-permute-start(bf16[16,24,1408]{2,1,0:T(8,128)(2,1)} %get-tuple-element.136), channel_id=1, source_target_pairs={{0,6},{1,3},{2,4},{3,1},{4,2},{5,7},{6,0},{7,5},{8,14},{9,11},{10,... | collective-permute-start | bytes 3244040 | tf_op jit(solution)/shard_map/ppermute | solution.py:700
  375.0 24.2 %collective-permute-start.10 = (bf16[16,24,1280]{2,1,0:T(8,128)(2,1)}, bf16[16,24,1280]{2,1,0:T(8,128)(2,1)S(1)}, u32[]{:S(2)}, u32[]{:S(2)}) collective-permute-start(bf16[16,24,1280]{2,1,0:T(8,128)(2,1)} %get-tuple-element.134), channel_id=1, source_target_pairs={{0,24},{1,9},{2,26},{3,11},{4,28},{5,13},{6,30},{7,15},{8,16},{9,1... | collective-permute-start | bytes 2949128 | tf_op jit(solution)/shard_map/ppermute | solution.py:700
  407.3 11.2 %collective-permute-start.12 = (bf16[8,24,1280]{2,1,0:T(8,128)(2,1)}, bf16[8,24,1280]{2,1,0:T(8,128)(2,1)S(1)}, u32[]{:S(2)}, u32[]{:S(2)}) collective-permute-start(bf16[8,24,1280]{2,1,0:T(8,128)(2,1)} %get-tuple-element.138), channel_id=1, source_target_pairs={{0,8},{1,25},{2,10},{3,27},{4,12},{5,29},{6,14},{7,31},{8,0},{9,17... | collective-permute-start | bytes 1474568 | tf_op jit(solution)/shard_map/ppermute | solution.py:700
  407.8 20.9 %collective-permute-start.14 = (bf16[8,24,1408]{2,1,0:T(8,128)(2,1)}, bf16[8,24,1408]{2,1,0:T(8,128)(2,1)S(1)}, u32[]{:S(2)}, u32[]{:S(2)}) collective-permute-start(bf16[8,24,1408]{2,1,0:T(8,128)(2,1)} %get-tuple-element.142), channel_id=1, source_target_pairs={{0,32},{1,97},{2,34},{3,99},{4,36},{5,101},{6,38},{7,103},{8,40},{... | collective-permute-start | bytes 1622024 | tf_op jit(solution)/shard_map/ppermute | solution.py:700
  418.4 10.3 %collective-permute-start.13 = (bf16[8,24,1280]{2,1,0:T(8,128)(2,1)}, bf16[8,24,1280]{2,1,0:T(8,128)(2,1)S(1)}, u32[]{:S(2)}, u32[]{:S(2)}) collective-permute-start(bf16[8,24,1280]{2,1,0:T(8,128)(2,1)} %get-tuple-element.140), channel_id=1, source_target_pairs={{0,2},{1,7},{2,0},{3,5},{4,6},{5,3},{6,4},{7,1},{8,10},{9,15},{10,... | collective-permute-start | bytes 1474568 | tf_op jit(solution)/shard_map/ppermute | solution.py:700
  432.7 11.1 %collective-permute-start.17 = (bf16[4,24,1408]{2,1,0:T(8,128)(2,1)}, bf16[4,24,1408]{2,1,0:T(8,128)(2,1)S(1)}, u32[]{:S(2)}, u32[]{:S(2)}) collective-permute-start(bf16[4,24,1408]{2,1,0:T(8,128)(2,1)} %get-tuple-element.148), channel_id=1, source_target_pairs={{0,96},{1,33},{2,98},{3,35},{4,100},{5,37},{6,102},{7,39},{8,104},... | collective-permute-start | bytes 811016 | tf_op jit(solution)/shard_map/ppermute | solution.py:700
  447.5 9.9 %collective-permute-start.20 = (bf16[2,24,1408]{2,1,0:T(8,128)(2,1)}, bf16[2,24,1408]{2,1,0:T(8,128)(2,1)S(1)}, u32[]{:S(2)}, u32[]{:S(2)}) collective-permute-start(bf16[2,24,1408]{2,1,0:T(8,128)(2,1)} %get-tuple-element.154), channel_id=1, source_target_pairs={{0,8},{1,25},{2,10},{3,27},{4,12},{5,29},{6,14},{7,31},{8,0},{9,17... | collective-permute-start | bytes 405512 | tf_op jit(solution)/shard_map/ppermute | solution.py:700
  460.1 17.2 %collective-permute-start.22 = (bf16[1,24,1280]{2,1,0:T(8,128)(2,1)}, bf16[1,24,1280]{2,1,0:T(8,128)(2,1)S(1)}, u32[]{:S(2)}, u32[]{:S(2)}) collective-permute-start(bf16[1,24,1280]{2,1,0:T(8,128)(2,1)} %get-tuple-element.158), channel_id=1, source_target_pairs={{0,96},{1,33},{2,98},{3,35},{4,100},{5,37},{6,102},{7,39},{8,104},... | collective-permute-start | bytes 184328 | tf_op jit(solution)/shard_map/ppermute | solution.py:700
  460.2 17.8 %collective-permute-start.23 = (bf16[1,24,1408]{2,1,0:T(8,128)(2,1)}, bf16[1,24,1408]{2,1,0:T(8,128)(2,1)S(1)}, u32[]{:S(2)}, u32[]{:S(2)}) collective-permute-start(bf16[1,24,1408]{2,1,0:T(8,128)(2,1)} %get-tuple-element.160), channel_id=1, source_target_pairs={{0,24},{1,9},{2,26},{3,11},{4,28},{5,13},{6,30},{7,15},{8,16},{9,1... | collective-permute-start | bytes 202760 | tf_op jit(solution)/shard_map/ppermute | solution.py:700
  460.3 17.6 %collective-permute-start.21 = (bf16[1,24,1280]{2,1,0:T(8,128)(2,1)}, bf16[1,24,1280]{2,1,0:T(8,128)(2,1)S(1)}, u32[]{:S(2)}, u32[]{:S(2)}) collective-permute-start(bf16[1,24,1280]{2,1,0:T(8,128)(2,1)} %get-tuple-element.156), channel_id=1, source_target_pairs={{0,6},{1,3},{2,4},{3,1},{4,2},{5,7},{6,0},{7,5},{8,14},{9,11},{10,... | collective-permute-start | bytes 184328 | tf_op jit(solution)/shard_map/ppermute | solution.py:700
  474.4 19.9 %collective-permute-start.31 = (bf16[16,24,2048]{2,1,0:T(8,128)(2,1)}, bf16[16,24,2048]{2,1,0:T(8,128)(2,1)S(1)}, u32[]{:S(2)}, u32[]{:S(2)}) collective-permute-start(bf16[16,24,2048]{2,1,0:T(8,128)(2,1)} %get-tuple-element.170), channel_id=1, source_target_pairs={{0,96},{1,33},{2,98},{3,35},{4,100},{5,37},{6,102},{7,39},{8,104},... | collective-permute-start | bytes 4718600 | tf_op jit(solution)/shard_map/ppermute | solution.py:700
  475.9 19.8 %collective-permute-start.32 = (bf16[16,24,2048]{2,1,0:T(8,128)(2,1)}, bf16[16,24,2048]{2,1,0:T(8,128)(2,1)S(1)}, u32[]{:S(2)}, u32[]{:S(2)}) collective-permute-start(bf16[16,24,2048]{2,1,0:T(8,128)(2,1)} %get-tuple-element.172), channel_id=1, source_target_pairs={{0,24},{1,9},{2,26},{3,11},{4,28},{5,13},{6,30},{7,15},{8,16},{9,1... | collective-permute-start | bytes 4718600 | tf_op jit(solution)/shard_map/ppermute | solution.py:700
  477.3 19.8 %collective-permute-start.33 = (bf16[16,64,768]{2,1,0:T(8,128)(2,1)}, bf16[16,64,768]{2,1,0:T(8,128)(2,1)S(1)}, u32[]{:S(2)}, u32[]{:S(2)}) collective-permute-start(bf16[16,64,768]{2,1,0:T(8,128)(2,1)} %get-tuple-element.174), channel_id=1, source_target_pairs={{0,6},{1,3},{2,4},{3,1},{4,2},{5,7},{6,0},{7,5},{8,14},{9,11},{10,... | collective-permute-start | bytes 4718600 | tf_op jit(solution)/shard_map/ppermute | solution.py:700
  504.5 12.3 %collective-permute-start.34 = (bf16[8,24,2048]{2,1,0:T(8,128)(2,1)}, bf16[8,24,2048]{2,1,0:T(8,128)(2,1)S(1)}, u32[]{:S(2)}, u32[]{:S(2)}) collective-permute-start(bf16[8,24,2048]{2,1,0:T(8,128)(2,1)} %get-tuple-element.176), channel_id=1, source_target_pairs={{0,8},{1,25},{2,10},{3,27},{4,12},{5,29},{6,14},{7,31},{8,0},{9,17... | collective-permute-start | bytes 2359304 | tf_op jit(solution)/shard_map/ppermute | solution.py:700
  505.3 12.3 %collective-permute-start.35 = (bf16[8,24,2048]{2,1,0:T(8,128)(2,1)}, bf16[8,24,2048]{2,1,0:T(8,128)(2,1)S(1)}, u32[]{:S(2)}, u32[]{:S(2)}) collective-permute-start(bf16[8,24,2048]{2,1,0:T(8,128)(2,1)} %get-tuple-element.178), channel_id=1, source_target_pairs={{0,2},{1,7},{2,0},{3,5},{4,6},{5,3},{6,4},{7,1},{8,10},{9,15},{10,... | collective-permute-start | bytes 2359304 | tf_op jit(solution)/shard_map/ppermute | solution.py:700
  505.5 12.3 %collective-permute-start.36 = (bf16[8,64,768]{2,1,0:T(8,128)(2,1)}, bf16[8,64,768]{2,1,0:T(8,128)(2,1)S(1)}, u32[]{:S(2)}, u32[]{:S(2)}) collective-permute-start(bf16[8,64,768]{2,1,0:T(8,128)(2,1)} %get-tuple-element.180), channel_id=1, source_target_pairs={{0,32},{1,97},{2,34},{3,99},{4,36},{5,101},{6,38},{7,103},{8,40},{... | collective-permute-start | bytes 2359304 | tf_op jit(solution)/shard_map/ppermute | solution.py:700
  548.7 17.3 %collective-permute-start.44 = (bf16[1,24,2048]{2,1,0:T(8,128)(2,1)}, bf16[1,24,2048]{2,1,0:T(8,128)(2,1)S(1)}, u32[]{:S(2)}, u32[]{:S(2)}) collective-permute-start(bf16[1,24,2048]{2,1,0:T(8,128)(2,1)} %get-tuple-element.196), channel_id=1, source_target_pairs={{0,96},{1,33},{2,98},{3,35},{4,100},{5,37},{6,102},{7,39},{8,104},... | collective-permute-start | bytes 294920 | tf_op jit(solution)/shard_map/ppermute | solution.py:700
  548.7 18.2 %collective-permute-start.43 = (bf16[1,24,2048]{2,1,0:T(8,128)(2,1)}, bf16[1,24,2048]{2,1,0:T(8,128)(2,1)S(1)}, u32[]{:S(2)}, u32[]{:S(2)}) collective-permute-start(bf16[1,24,2048]{2,1,0:T(8,128)(2,1)} %get-tuple-element.194), channel_id=1, source_target_pairs={{0,6},{1,3},{2,4},{3,1},{4,2},{5,7},{6,0},{7,5},{8,14},{9,11},{10,... | collective-permute-start | bytes 294920 | tf_op jit(solution)/shard_map/ppermute | solution.py:700
  552.0 17.7 %collective-permute-start.47 = (bf16[32,768]{1,0:T(8,128)(2,1)S(1)}, bf16[32,768]{1,0:T(8,128)(2,1)S(1)}, u32[]{:S(2)}, u32[]{:S(2)}) collective-permute-start(bf16[32,768]{1,0:T(8,128)(2,1)S(1)} %select_bitcast_fusion), channel_id=1, source_target_pairs={{0,1},{1,0},{2,3},{3,2},{4,5},{5,4},{6,7},{7,6},{8,9},{9,8},{10,11... | collective-permute-start | bytes 147464 | tf_op jit(solution)/shard_map/ppermute | solution.py:70
  (61 other events, 388.8 us)
Sparse Core Ops, SparseCore 0:
  15.4 137.3 all-gather.2
  156.4 72.5 all-gather.4

commit v2 on v1

--- a/solution.py
+++ b/solution.py
@@ -11,7 +11,8 @@
 EPSILON = 1e-06
 BF = jnp.bfloat16
 F32 = jnp.float32
-VMEM_LIMIT = 56 * 1024 * 1024
+MIB = 1024 * 1024
+SHORT = pl.CostEstimate(flops=1, bytes_accessed=1, transcendentals=0)
 AXIS_UNIT = {"x": 16, "z": 4, "y": 1}
 ORDERS = ("xzy", "zyx", "yxz")
 
@@ -114,16 +115,18 @@
     wv_ref,
     wh_ref,
     misc_ref,
-    normed_ref,
+    normed_t_ref,
     q_ref,
     k_ref,
     v_ref,
     h_ref,
     att_ref,
+    att_t_ref,
     probs_ref,
     carried_ref,
     inverse_ref,
     beta_ref,
+    normed_ref,
 ):
     at = pl.program_id(0)
 
@@ -131,7 +134,9 @@
     def _():
         tokens = tokens_ref[...].astype(F32)
         scale = lax.rsqrt(jnp.mean(tokens * tokens, axis=1, keepdims=True) + EPSILON)
-        normed_ref[...] = (tokens * scale * gain_row(misc_ref, 12)).astype(BF)
+        value = tokens * scale * gain_row(misc_ref, 12)
+        normed_ref[...] = value.astype(BF)
+        normed_t_ref[...] = value.T.astype(BF)
         beta_ref[...] = dot(normed_ref[...], misc_ref[...])
 
     normed = normed_ref[...]
@@ -179,7 +184,9 @@
         probs_ref[i] = probs
         carried_ref[i] = carried[i].astype(BF)
         inverse_ref[i] = inverses[i].astype(BF)
-        att_ref[:, 128 * i : 128 * (i + 1)] = dot(probs.astype(BF), v[i]).astype(BF)
+        att = dot(probs.astype(BF), v[i])
+        att_ref[:, 128 * i : 128 * (i + 1)] = att.astype(BF)
+        att_t_ref[128 * i : 128 * (i + 1), :] = att.T.astype(BF)
 
 
 def attention_forward(tokens, length, attn):
@@ -194,6 +201,7 @@
     row_block = pl.BlockSpec((count, 256), column)
     cell_block = pl.BlockSpec(cell, lambda i, *_: (i, 0, 0))
     rows = jax.ShapeDtypeStruct((count, width), BF)
+    turned = jax.ShapeDtypeStruct((width, count), BF)
     cells = (2 * steps, count, count)
     return pl.pallas_call(
         attention_forward_kernel,
@@ -209,31 +217,34 @@
                 pl.BlockSpec((width, 128), lambda i, *_: (0, 6)),
             ],
             out_specs=[
-                pl.BlockSpec((count, width), whole),
+                pl.BlockSpec((width, count), whole),
                 row_block,
                 row_block,
                 row_block,
                 row_block,
                 row_block,
+                pl.BlockSpec((256, count), lambda i, *_: (i, 0)),
                 cell_block,
                 cell_block,
                 cell_block,
                 pl.BlockSpec((count, 128), whole),
             ],
+            scratch_shapes=[pltpu.VMEM((count, width), BF)],
         ),
         out_shape=[
+            turned,
             rows,
             rows,
             rows,
             rows,
             rows,
-            rows,
+            turned,
             jax.ShapeDtypeStruct(cells, F32),
             jax.ShapeDtypeStruct(cells, BF),
             jax.ShapeDtypeStruct(cells, BF),
             jax.ShapeDtypeStruct((count, 128), F32),
         ],
-        compiler_params=pltpu.CompilerParams(vmem_limit_bytes=VMEM_LIMIT),
+        compiler_params=pltpu.CompilerParams(vmem_limit_bytes=32 * MIB),
         cost_estimate=pl.CostEstimate(
             flops=8 * count * width * width + 12 * 60 * 2 * 128**3,
             bytes_accessed=10 * width * width,
@@ -248,17 +259,21 @@
 
 def feedforward_kernel(
     length_ref,
+    core_ref,
     tokens_ref,
     att_ref,
     out_lo_ref,
     out_hi_ref,
     misc_ref,
     cot_ref,
+    cot_own_ref,
+    cot_other_ref,
     wg_ref,
     wu_ref,
-    wd_lo_ref,
-    wd_hi_ref,
-    second_ref,
+    down_own_ref,
+    down_other_ref,
+    second_t_ref,
+    product_t_ref,
     acts_ref,
     mixed_ref,
     hidden_grad_ref,
@@ -267,6 +282,7 @@
     hidden,
     feed,
     second_grad,
+    second_ref,
 ):
     at = pl.program_id(0)
     half = out_lo_ref.shape[1]
@@ -278,32 +294,37 @@
         hidden[:, half:] = tokens_ref[:, half:].astype(F32) + dot(att, out_hi_ref[...])
         value = hidden[...]
         scale = lax.rsqrt(jnp.mean(value * value, axis=1, keepdims=True) + EPSILON)
-        second_ref[...] = (value * scale * gain_row(misc_ref, 13)).astype(BF)
+        value = value * scale * gain_row(misc_ref, 13)
+        second_ref[...] = value.astype(BF)
+        second_t_ref[...] = value.T.astype(BF)
         feed[...] = jnp.zeros_like(feed)
         second_grad[...] = jnp.zeros_like(second_grad)
 
     second = second_ref[...]
-    cot = cot_ref[...]
     gate = dot(second, wg_ref[...])
     upward = dot(second, wu_ref[...])
     sigma = jax.nn.sigmoid(gate)
     silu = gate * sigma
-    product = (silu * upward).astype(BF)
-    product_grad = dot_nt(cot[:, :half], wd_lo_ref[...]) + dot_nt(cot[:, half:], wd_hi_ref[...])
+    product = silu * upward
+    product_t_ref[...] = product.T.astype(BF)
+    product = product.astype(BF)
+    product_grad = dot_nt(cot_own_ref[...], down_own_ref[...]) + dot_nt(
+        cot_other_ref[...], down_other_ref[...]
+    )
     gate_low = (product_grad * upward * (sigma * (1.0 + gate * (1.0 - sigma)))).astype(BF)
     up_low = (product_grad * silu).astype(BF)
-    acts_ref[0] = product
-    acts_ref[1] = gate_low
-    acts_ref[2] = up_low
-    feed[:, :half] += dot(product, wd_lo_ref[...])
-    feed[:, half:] += dot(product, wd_hi_ref[...])
+    acts_ref[0] = gate_low
+    acts_ref[1] = up_low
+    feed[0] += dot(product, down_own_ref[...])
+    feed[1] += dot(product, down_other_ref[...])
     second_grad[...] += dot_nt(gate_low, wg_ref[...]) + dot_nt(up_low, wu_ref[...])
 
     @pl.when(at == pl.num_programs(0) - 1)
     def _():
         value = hidden[...]
         valid = lax.broadcasted_iota(jnp.int32, value.shape, 0) < length_ref[0]
-        mixed_ref[...] = jnp.where(valid, value + feed[...], 0.0).astype(BF)
+        fed = jnp.concatenate([feed[core_ref[0]], feed[1 - core_ref[0]]], axis=1)
+        mixed_ref[...] = jnp.where(valid, value + fed, 0.0).astype(BF)
         scale = lax.rsqrt(jnp.mean(value * value, axis=1, keepdims=True) + EPSILON)
         grad = second_grad[...]
         scaled = grad * gain_row(misc_ref, 13)
@@ -316,9 +337,9 @@
         gain_grad_ref[...] = jnp.sum(grad * value * scale, axis=0, keepdims=True)
 
 
-def feedforward(tokens, length, att, cot, attn, down):
+def feedforward(tokens, length, core, att, cots, attn, downs):
     count, width = tokens.shape
-    hidden_units = down.shape[0] // 2
+    hidden_units = downs[0].shape[0]
     steps = hidden_units // FF_BLOCK
     half = width // 2
     whole = lambda i, *_: (0, 0)
@@ -326,11 +347,11 @@
     weight = lambda side: pl.BlockSpec(
         (width, FF_BLOCK), lambda i, *_: (side, 1024 // FF_BLOCK + i)
     )
-    down_block = lambda side: pl.BlockSpec((FF_BLOCK, half), lambda i, *_: (side * steps + i, 0))
+    down_block = pl.BlockSpec((FF_BLOCK, half), lambda i, *_: (i, 0))
     return pl.pallas_call(
         feedforward_kernel,
         grid_spec=pltpu.PrefetchScalarGridSpec(
-            num_scalar_prefetch=1,
+            num_scalar_prefetch=2,
             grid=(steps,),
             in_specs=[
                 rows,
@@ -339,14 +360,17 @@
                 pl.BlockSpec((width, half), lambda i, *_: (1, 0)),
                 pl.BlockSpec((width, 128), lambda i, *_: (0, 6)),
                 rows,
+                pl.BlockSpec((count, half), whole),
+                pl.BlockSpec((count, half), whole),
                 weight(0),
                 weight(1),
-                down_block(0),
-                down_block(1),
+                down_block,
+                down_block,
             ],
             out_specs=[
-                rows,
-                pl.BlockSpec((3, count, FF_BLOCK), lambda i, *_: (0, 0, i)),
+                pl.BlockSpec((width, count), whole),
+                pl.BlockSpec((FF_BLOCK, count), lambda i, *_: (i, 0)),
+                pl.BlockSpec((2, count, FF_BLOCK), lambda i, *_: (0, 0, i)),
                 rows,
                 rows,
                 rows,
@@ -354,31 +378,33 @@
             ],
             scratch_shapes=[
                 pltpu.VMEM((count, width), F32),
+                pltpu.VMEM((2, count, half), F32),
                 pltpu.VMEM((count, width), F32),
-                pltpu.VMEM((count, width), F32),
+                pltpu.VMEM((count, width), BF),
             ],
         ),
         out_shape=[
-            jax.ShapeDtypeStruct((count, width), BF),
-            jax.ShapeDtypeStruct((3, count, hidden_units), BF),
+            jax.ShapeDtypeStruct((width, count), BF),
+            jax.ShapeDtypeStruct((hidden_units, count), BF),
+            jax.ShapeDtypeStruct((2, count, hidden_units), BF),
             jax.ShapeDtypeStruct((count, width), BF),
             jax.ShapeDtypeStruct((count, width), F32),
             jax.ShapeDtypeStruct((count, width), BF),
             jax.ShapeDtypeStruct((1, width), F32),
         ],
-        compiler_params=pltpu.CompilerParams(vmem_limit_bytes=VMEM_LIMIT),
+        compiler_params=pltpu.CompilerParams(vmem_limit_bytes=48 * MIB),
         cost_estimate=pl.CostEstimate(
             flops=12 * count * width * hidden_units,
             bytes_accessed=6 * width * hidden_units,
             transcendentals=0,
         ),
         name="feedforward",
-    )(length, tokens, att, attn, attn, attn, cot, attn, attn, down, down)
+    )(length, core, tokens, att, attn, attn, attn, *cots, attn, attn, *downs)
 
 
 def attention_backward_kernel(
     tokens_ref,
-    normed_ref,
+    normed_t_ref,
     branch_ref,
     hidden_grad_ref,
     ffn_gain_ref,
@@ -518,13 +544,13 @@
         place = lax.broadcasted_iota(jnp.int32, (8, 128), 0)
         lanes = lax.broadcasted_iota(jnp.int32, (8, 128), 1)
         pick = ((place < 4) & (lanes == 12 + place // 2)).astype(F32)
-        misc_grad = dot_tn(normed_ref[...], beta_low) + dot_tn(
+        misc_grad = dot(normed_t_ref[...], beta_low) + dot_tn(
             gains.astype(BF), pick.astype(BF)
         )
         misc_grad_ref[...] = misc_grad.astype(BF)
 
 
-def attention_backward(tokens, normed, branch, hidden_grad, ffn_gain, saved, attn):
+def attention_backward(tokens, normed_t, branch, hidden_grad, ffn_gain, saved, attn):
     q, k, v, h, probs, carried, inverse, beta = saved
     count, width = tokens.shape
     steps = width // 256
@@ -540,7 +566,7 @@
         grid=(steps,),
         in_specs=[
             rows,
-            rows,
+            pl.BlockSpec((width, count), whole),
             rows,
             rows,
             pl.BlockSpec((1, width), whole),
@@ -571,16 +597,12 @@
             jax.ShapeDtypeStruct((width, 128), BF),
         ],
         scratch_shapes=[pltpu.VMEM((count, width), F32), pltpu.VMEM((count, 128), F32)],
-        compiler_params=pltpu.CompilerParams(vmem_limit_bytes=VMEM_LIMIT),
-        cost_estimate=pl.CostEstimate(
-            flops=10 * count * width * width + 12 * 40 * 2 * 128**3,
-            bytes_accessed=12 * width * width,
-            transcendentals=0,
-        ),
+        compiler_params=pltpu.CompilerParams(vmem_limit_bytes=40 * MIB),
+        cost_estimate=SHORT,
         name="attention_backward",
     )(
         tokens,
-        normed,
+        normed_t,
         branch,
         hidden_grad,
         ffn_gain,
@@ -602,96 +624,223 @@
     )
 
 
-def weight_gradient_kernel(place_ref, core_ref, mine_x, other_x, mine_y, other_y, keep, send, xt, hold):
-    @pl.when(pl.program_id(0) == 0)
-    def _():
-        xt[:, :128] = mine_x[...].T
-        xt[:, 128:] = other_x[...].T
-
-    height = hold.shape[1]
-    chips = hold.shape[0]
-    y = jnp.concatenate([mine_y[...], other_y[...]], axis=0)
-    group = 8 if height == 24 else 4
-    for first in range(0, chips, group):
-        part = dot(xt[first * height : (first + group) * height], y)
-        for chip in range(group):
-            hold[first + chip] = part[chip * height : (chip + 1) * height].astype(BF)
-    for place in range(chips // 2):
-        keep[place] = hold[place_ref[place]]
-        send[place] = hold[place_ref[place + chips // 2]]
-
-
-def weight_gradient(places, core, mine_x, other_x, mine_y, other_y, height, tile, y_index, tiles):
-    x_spec, mine_x, other_x = x_operand(mine_x, other_x)
-    width = mine_x.shape[-1]
-    count = mine_x.shape[-2]
-    chips = width // height
-    y_spec = pl.BlockSpec((None, count, tile), y_index)
-    out = pl.BlockSpec((chips // 2, height, tile), lambda i, *_: (0, 0, i))
-    shape = jax.ShapeDtypeStruct((chips // 2, height, tile * tiles), BF)
+def weight_gradient_kernel(segments, n_x, n_y, has_misc, second_half, *refs):
+    place_ref, refs = refs[0], refs[2:]
+    xs = [(refs[2 * i], refs[2 * i + 1]) for i in range(n_x)]
+    refs = refs[2 * n_x :]
+    ys = [(refs[2 * i], refs[2 * i + 1]) for i in range(n_y)]
+    refs = refs[2 * n_y :]
+    misc_ref = None
+    if has_misc:
+        misc_ref, refs = refs[0], refs[1:]
+    at = pl.program_id(0)
+    chips, height = xs[0][0].shape[0], xs[0][0].shape[1]
+    if second_half:
+        spots = [(refs[0], None, i, chips // 2 + 8 * at + i) for i in range(8)]
+    else:
+        got_lo, got_hi, keep, send = refs
+        spots = [(keep, got_lo, i, 4 * at + i) for i in range(4)]
+        spots += [(send, got_hi, i, chips // 4 + 4 * at + i) for i in range(4)]
+    owners = [place_ref[spot[3]] for spot in spots]
+    lefts = []
+    for mine, other in xs:
+        rows = [
+            jnp.concatenate([mine[owner].astype(F32), other[owner].astype(F32)], axis=1)
+            for owner in owners
+        ]
+        lefts.append(jnp.concatenate(rows, axis=0).astype(BF))
+    done = 0
+    for x_at, y_at, matrix, start, size in segments:
+        mine, other = ys[y_at]
+        columns = slice(start, start + size)
+        part = dot(
+            lefts[x_at],
+            jnp.concatenate([mine[matrix, :, columns], other[matrix, :, columns]], axis=0),
+        )
+        for index, (out, got, i, _) in enumerate(spots):
+            value = part[index * height : (index + 1) * height]
+            if got is not None:
+                value = value + got[i, :, done : done + size].astype(F32)
+            out[i, :, done : done + size] = value.astype(BF)
+        done += size
+    if has_misc:
+        for (out, got, i, _), owner in zip(spots, owners):
+            value = misc_ref[owner].astype(F32)
+            if got is not None:
+                value = value + got[i, :, done:].astype(F32)
+            out[i, :, done:] = value.astype(BF)
+
+
+def weight_gradient(places, core, xs, ys, segments, misc=None, got=None):
+    chips, height, count = xs[0][0].shape
+    columns = sum(segment[4] for segment in segments) + (128 if misc is not None else 0)
+    operands, in_specs = [], []
+    for mine, other in xs:
+        operands += [mine, other]
+        in_specs += [pl.BlockSpec(mine.shape, lambda i, *_: (0, 0, 0))] * 2
+    for mine, other in ys:
+        operands += [mine, other]
+        half = (mine.shape[0], mine.shape[1], mine.shape[2] // 2)
+        in_specs += [pl.BlockSpec(half, lambda i, _, c: (0, 0, c[0]))] * 2
+    if misc is not None:
+        operands.append(misc)
+        in_specs.append(pl.BlockSpec(misc.shape, lambda i, *_: (0, 0, 0)))
+    steps = chips // 16
+    if got is None:
+        out_specs = [pl.BlockSpec((8, height, columns), lambda i, *_: (i, 0, 0))]
+        out_shape = [jax.ShapeDtypeStruct((chips // 2, height, columns), BF)]
+    else:
+        block = (4, height, columns)
+        operands += [got, got]
+        in_specs += [
+            pl.BlockSpec(block, lambda i, *_: (i, 0, 0)),
+            pl.BlockSpec(block, lambda i, *_: (steps + i, 0, 0)),
+        ]
+        out_specs = [pl.BlockSpec(block, lambda i, *_: (i, 0, 0))] * 2
+        out_shape = [jax.ShapeDtypeStruct((chips // 4, height, columns), BF)] * 2
     return pl.pallas_call(
-        weight_gradient_kernel,
+        functools.partial(
+            weight_gradient_kernel, segments, len(xs), len(ys), misc is not None, got is None
+        ),
         grid_spec=pltpu.PrefetchScalarGridSpec(
-            num_scalar_prefetch=2,
-            grid=(tiles,),
-            in_specs=[x_spec, x_spec, y_spec, y_spec],
-            out_specs=[out, out],
-            scratch_shapes=[
-                pltpu.VMEM((width, 2 * count), BF),
-                pltpu.VMEM((chips, height, tile), BF),
-            ],
+            num_scalar_prefetch=2, grid=(steps,), in_specs=in_specs, out_specs=out_specs
         ),
-        out_shape=[shape, shape],
-        compiler_params=pltpu.CompilerParams(vmem_limit_bytes=VMEM_LIMIT),
-        cost_estimate=pl.CostEstimate(
-            flops=4 * count * width * tile * tiles,
-            bytes_accessed=2 * width * tile * tiles,
-            transcendentals=0,
-        ),
-        name="weight_gradient",
-    )(places, core, mine_x, other_x, mine_y, other_y)
-
-
-def x_operand(mine, other):
-    if mine.ndim == 3:
-        return pl.BlockSpec((None,) + mine.shape[1:], lambda i, *_: (0, 0, 0)), mine, other
-    return pl.BlockSpec(mine.shape, lambda i, *_: (0, 0)), mine, other
-
-
-def add_kernel(*refs):
-    n = len(refs) // 6
-    ins, outs = refs[: 4 * n], refs[4 * n :]
-    for s in range(n):
-        keep_lo, keep_hi, got_lo, got_hi = ins[4 * s : 4 * s + 4]
-        outs[2 * s][...] = keep_lo[...] + got_lo[...]
-        outs[2 * s + 1][...] = keep_hi[...] + got_hi[...]
-
-
-def add_halves(keeps, gots):
-    rows = keeps[0].shape[0] // 2
+        out_shape=out_shape,
+        compiler_params=pltpu.CompilerParams(vmem_limit_bytes=32 * MIB),
+        cost_estimate=SHORT,
+        name="weight_gradient" if got is None else "weight_gradient_add",
+    )(places, core, *operands)
+
+
+def add_kernel(widths, *refs):
+    total = sum(len(group) for group in widths)
+    ins, outs = refs[: 4 * total], refs[4 * total :]
+    at = 0
+    for index, group in enumerate(widths):
+        start = 0
+        for width in group:
+            keep_lo, keep_hi, got_lo, got_hi = ins[4 * at : 4 * at + 4]
+            columns = slice(start, start + width)
+            outs[2 * index][:, :, columns] = keep_lo[...] + got_lo[...]
+            outs[2 * index + 1][:, :, columns] = keep_hi[...] + got_hi[...]
+            start += width
+            at += 1
+
+
+def add_halves(groups):
+    rows = groups[0][0][0].shape[0] // 2
     grid = max(1, rows // 2)
     block = rows // grid
-    operands, in_specs, out_specs, shapes = [], [], [], []
-    for keep, got in zip(keeps, gots):
-        shape = (block,) + keep.shape[1:]
-        low = pl.BlockSpec(shape, lambda i: (i, 0, 0))
-        high = pl.BlockSpec(shape, lambda i: (i + grid, 0, 0))
-        operands += [keep, keep, got, got]
-        in_specs += [low, high, low, high]
-        out_specs += [low, low]
-        shapes += [jax.ShapeDtypeStruct((rows,) + keep.shape[1:], BF)] * 2
-    size = sum(int(np.prod(k.shape)) for k in keeps)
+    operands, in_specs, out_specs, shapes, widths = [], [], [], [], []
+    for group in groups:
+        for keep, got in group:
+            shape = (block,) + keep.shape[1:]
+            low = pl.BlockSpec(shape, lambda i: (i, 0, 0))
+            high = pl.BlockSpec(shape, lambda i: (i + grid, 0, 0))
+            operands += [keep, keep, got, got]
+            in_specs += [low, high, low, high]
+        widths.append([keep.shape[2] for keep, _ in group])
+        shape = (block, group[0][0].shape[1], sum(widths[-1]))
+        out_specs += [pl.BlockSpec(shape, lambda i: (i, 0, 0))] * 2
+        shapes += [jax.ShapeDtypeStruct((rows,) + shape[1:], BF)] * 2
     outs = pl.pallas_call(
-        add_kernel,
+        functools.partial(add_kernel, widths),
         grid=(grid,),
         in_specs=in_specs,
         out_specs=out_specs,
         out_shape=shapes,
-        compiler_params=pltpu.CompilerParams(vmem_limit_bytes=VMEM_LIMIT),
-        cost_estimate=pl.CostEstimate(flops=size, bytes_accessed=6 * size, transcendentals=0),
+        compiler_params=pltpu.CompilerParams(vmem_limit_bytes=24 * MIB),
+        cost_estimate=SHORT,
         name="add_halves",
     )(*operands)
     return outs[0::2], outs[1::2]
+
+
+def last_add_kernel(core_ref, *refs):
+    first = core_ref[0] == 0
+    *ins, mine, theirs, mine_down, theirs_down = refs
+    start = 0
+    for index in range(0, len(ins), 2):
+        value = ins[index][0].astype(F32) + ins[index + 1][0].astype(F32)
+        height, width = value.shape
+        low, high = value[: height // 2], value[height // 2 :]
+        own, other = jnp.where(first, low, high), jnp.where(first, high, low)
+        if height == 24:
+            mine[:, start : start + width] = own
+            theirs[:, start : start + width] = other.astype(BF)
+            start += width
+        else:
+            mine_down[...] = own
+            theirs_down[...] = other.astype(BF)
+
+
+def last_add(core, pairs):
+    flat = [value for pair in pairs for value in pair]
+    width = sum(keep.shape[2] for keep, _ in pairs if keep.shape[1] == 24)
+    down = next(keep for keep, _ in pairs if keep.shape[1] != 24)
+    shapes = [(12, width), (12, width)] + [(down.shape[1] // 2, down.shape[2])] * 2
+    return pl.pallas_call(
+        last_add_kernel,
+        grid_spec=pltpu.PrefetchScalarGridSpec(
+            num_scalar_prefetch=1,
+            grid=(1,),
+            in_specs=[pl.BlockSpec(v.shape, lambda i, _: (0, 0, 0)) for v in flat],
+            out_specs=[pl.BlockSpec(shape, lambda i, _: (0, 0)) for shape in shapes],
+        ),
+        out_shape=[jax.ShapeDtypeStruct(s, t) for s, t in zip(shapes, (F32, BF, F32, BF))],
+        compiler_params=pltpu.CompilerParams(vmem_limit_bytes=16 * MIB),
+        cost_estimate=SHORT,
+        name="last_add",
+    )(core, *flat)
+
+
+PLACES = (
+    ((2048, 768),),
+    ((2816, 512), (5376, 256)),
+    ((5632, 768),),
+    ((6400, 256), (6656, 512)),
+    ((7168, 768),),
+    ((0, 2048),),
+    ((3328, 2048),),
+)
+
+
+def finish_kernel(core_ref, mine, other, mine_down, other_down, *outs):
+    first = core_ref[0] == 0
+    for pieces, out in zip(PLACES, outs):
+        half = out.shape[1] // 2
+        done = 0
+        for start, width in pieces:
+            a = mine[:, start : start + width]
+            b = other[:, start : start + width].astype(F32)
+            out[:, done : done + width] = jnp.where(first, a, b)
+            out[:, half + done : half + done + width] = jnp.where(first, b, a)
+            done += width
+    a, b = mine_down[...], other_down[...].astype(F32)
+    half = a.shape[1]
+    outs[7][:, :half] = jnp.where(first, a, b)
+    outs[7][:, half:] = jnp.where(first, b, a)
+    outs[8][...] = mine[:, 7936:] + other[:, 7936:].astype(F32)
+
+
+def finish(core, mine, other, mine_down, other_down):
+    rows, down_rows = mine.shape[0], mine_down.shape[0]
+    shapes = [(rows, 2 * sum(w for _, w in pieces)) for pieces in PLACES]
+    shapes += [(down_rows, 2 * mine_down.shape[1]), (rows, 128)]
+    operands = (mine, other, mine_down, other_down)
+    return pl.pallas_call(
+        finish_kernel,
+        grid_spec=pltpu.PrefetchScalarGridSpec(
+            num_scalar_prefetch=1,
+            grid=(1,),
+            in_specs=[pl.BlockSpec(v.shape, lambda i, _: (0, 0)) for v in operands],
+            out_specs=[pl.BlockSpec(shape, lambda i, _: (0, 0)) for shape in shapes],
+        ),
+        out_shape=[jax.ShapeDtypeStruct(shape, F32) for shape in shapes],
+        compiler_params=pltpu.CompilerParams(vmem_limit_bytes=16 * MIB),
+        cost_estimate=SHORT,
+        name="finish",
+    )(core, *operands)
 
 
 def send_step(value, stream, step):
@@ -700,25 +849,51 @@
     return lax.ppermute(value, "fsdp", pairs)
 
 
-def reduce_streams(keeps, sends):
-    for step in range(6):
-        gots = [send_step(send, stream, step) for stream, send in enumerate(sends)]
-        if step == 5:
-            return [(keep + got)[0] for keep, got in zip(keeps, gots)]
-        keeps, sends = add_halves(keeps, gots)
-
-
-def own_rows(block, core):
-    rows = block.shape[0] // 2
-    first = jnp.where(core == 0, block[:rows], block[rows:])
-    second = jnp.where(core == 0, block[rows:], block[:rows])
-    return first, swap(second)
-
-
-def both_halves(mine, other, core):
-    left = jnp.where(core == 0, mine, other)
-    right = jnp.where(core == 0, other, mine)
-    return jnp.concatenate([left, right], axis=1).astype(F32)
+def after(values, earlier):
+    flat, tree = jax.tree.flatten(values)
+    kept = lax.optimization_barrier((*flat, *jax.tree.leaves(earlier)))
+    return jax.tree.unflatten(tree, kept[: len(flat)])
+
+
+def exchange(sends, step, streams=(0, 1, 2)):
+    return [send_step(send, stream, step) for stream, send in zip(streams, sends)]
+
+
+def blocks(turned, height):
+    return turned.reshape(turned.shape[0] // height, height, turned.shape[1])
+
+
+def gather_streams(parts):
+    for step in range(5, -1, -1):
+        gots = [send_step(part, stream, step) for stream, part in enumerate(parts)]
+        parts = [jnp.concatenate(pair, axis=0) for pair in zip(parts, gots)]
+    return parts
+
+
+def in_order_kernel(place_ref, *refs):
+    streams, out = refs[:-1], refs[-1]
+    width = streams[0].shape[2]
+    for index, stream in enumerate(streams):
+        for place in range(stream.shape[0]):
+            out[place_ref[index, place], :, index * width : (index + 1) * width] = stream[place]
+
+
+def in_order(places, streams):
+    chips, height, width = streams[0].shape
+    shape = (chips, height, width * len(streams))
+    return pl.pallas_call(
+        in_order_kernel,
+        grid_spec=pltpu.PrefetchScalarGridSpec(
+            num_scalar_prefetch=1,
+            grid=(1,),
+            in_specs=[pl.BlockSpec(s.shape, lambda i, _: (0, 0, 0)) for s in streams],
+            out_specs=pl.BlockSpec(shape, lambda i, _: (0, 0, 0)),
+        ),
+        out_shape=jax.ShapeDtypeStruct(shape, BF),
+        compiler_params=pltpu.CompilerParams(vmem_limit_bytes=40 * MIB),
+        cost_estimate=SHORT,
+        name="in_order",
+    )(places, *streams)
 
 
 def body(
@@ -775,131 +950,90 @@
     )
     by_core = [[*range(0, devices, 2), *range(1, devices, 2)]]
     attn = lax.all_gather(slab, "fsdp", axis=0, tiled=True, axis_index_groups=by_core)
-    down = lax.all_gather(slab_down, "fsdp", axis=0, tiled=True, axis_index_groups=by_core)
+    third = half // 3
+    streams = gather_streams([slab_down[None, :, third * i : third * (i + 1)] for i in range(3)])
+    down_own = in_order(places, streams).reshape(hidden_units, half)
+    downs = (down_own, swap(down_own))
 
     flat = tokens.reshape(count, width)
     valid = lax.broadcasted_iota(jnp.int32, (count, 1), 0) < lengths[0]
     cot = jnp.where(valid, cotangent.reshape(count, width), jnp.zeros((), BF))
     cot_other = swap(cot)
 
-    normed, q, k, v, h, att, probs, carried, inverse, beta = attention_forward(flat, lengths, attn)
-    normed_other, att_other = swap(normed), swap(att)
-    second, acts, mixed, hidden_grad, branch, ffn_gain = feedforward(
-        flat, lengths, att, cot, attn, down
-    )
-    second_other, acts_other, branch_other = swap(second), swap(acts), swap(branch)
-
-    unit = hidden_units // 2 // 512
-    pairs = [
-        weight_gradient(
-            places[0],
-            core_at,
-            second,
-            second_other,
-            acts,
-            acts_other,
-            24,
-            512,
-            lambda i, _, c: (1, 0, unit * c[0] + i),
-            unit,
-        ),
-        weight_gradient(
-            places[1],
-            core_at,
-            second,
-            second_other,
-            acts,
-            acts_other,
-            24,
-            512,
-            lambda i, _, c: (2, 0, unit * c[0] + i),
-            unit,
-        ),
-        weight_gradient(
-            places[2],
-            core_at,
-            acts,
-            acts_other,
-            cot[None],
-            cot_other[None],
-            64,
-            256,
-            lambda i, _, c: (0, 0, 3 * c[0] + i),
-            3,
-        ),
+    normed_t, q, k, v, h, att, att_t, probs, carried, inverse, beta = attention_forward(
+        flat, lengths, attn
+    )
+    normed_x, att_x = (
+        (blocks(value, 24), blocks(swap(value), 24)) for value in (normed_t, att_t)
+    )
+    cots = (
+        cot,
+        jnp.where(core == 0, cot[:, :half], cot[:, half:]),
+        jnp.where(core == 0, cot[:, half:], cot[:, :half]),
+    )
+    second_t, product_t, acts, mixed, hidden_grad, branch, ffn_gain = feedforward(
+        flat, lengths, core_at, att, cots, attn, downs
+    )
+    second_x = (blocks(second_t, 24), blocks(swap(second_t), 24))
+    product_x = (blocks(product_t, 64), blocks(swap(product_t), 64))
+    acts_y = (acts, swap(acts))
+    cot_y = (cot[None], cot_other[None])
+    branch_y = (branch[None], swap(branch)[None])
+
+    part = hidden_units // 2
+    jobs = [
+        ([second_x], [acts_y], [(0, 0, 0, 0, part)]),
+        ([second_x], [acts_y], [(0, 0, 1, 0, part)]),
+        ([product_x], [cot_y], [(0, 0, 0, 0, half)]),
     ]
-    gate_sum, up_sum, down_sum = reduce_streams([p[0] for p in pairs], [p[1] for p in pairs])
+    sends = [weight_gradient(places[s], core_at, *job)[0] for s, job in enumerate(jobs)]
+    gots = exchange(sends, 0)
+    branch = after(branch, sends)
 
     grads, grad_tokens, misc_grad = attention_backward(
-        flat, normed, branch, hidden_grad, ffn_gain, (q, k, v, h, probs, carried, inverse, beta), attn
-    )
-    grads_other = swap(grads)
-    tile_index = lambda first: lambda i, _, c: ((first + i) // 3, 0, 3 * c[0] + (first + i) % 3)
-    qkvh = lambda stream, first, tiles: weight_gradient(
-        places[stream],
-        core_at,
-        normed,
-        normed_other,
-        grads,
-        grads_other,
-        24,
-        256,
-        tile_index(first),
-        tiles,
-    )
-    out_pair = weight_gradient(
-        places[2],
-        core_at,
-        att,
-        att_other,
-        branch[None],
-        branch_other[None],
-        24,
-        256,
-        lambda i, _, c: (0, 0, 3 * c[0] + i),
-        3,
-    )
-    misc_blocks = misc_grad.reshape(-1, 24, 128)[places[2]]
-    last_pair = qkvh(2, 10, 2)
-    cut = misc_blocks.shape[0] // 2
-    pairs = [
-        qkvh(0, 0, 5),
-        qkvh(1, 5, 5),
-        [
-            jnp.concatenate([last_pair[0], out_pair[0], misc_blocks[:cut]], axis=2),
-            jnp.concatenate([last_pair[1], out_pair[1], misc_blocks[cut:]], axis=2),
-        ],
+        flat, normed_t, branch, hidden_grad, ffn_gain, (q, k, v, h, probs, carried, inverse, beta), attn
+    )
+    grads_y = (grads, swap(grads))
+    misc_x = misc_grad.reshape(-1, 24, 128)
+    attn_jobs = [
+        ([normed_x], [grads_y], [(0, 0, 0, 0, 768), (0, 0, 1, 0, 512)]),
+        ([normed_x], [grads_y], [(0, 0, 1, 512, 256), (0, 0, 2, 0, 768), (0, 0, 3, 0, 256)]),
+        ([normed_x, att_x], [grads_y, branch_y], [(0, 0, 3, 256, 512), (1, 1, 0, 0, 768)], misc_x),
     ]
-    sums = reduce_streams([p[0] for p in pairs], [p[1] for p in pairs])
-
-    gate_up = jnp.concatenate([gate_sum, up_sum], axis=1)
-    mine, other = own_rows(gate_up, core)
-    part = hidden_units // 2
-    grad_gate = both_halves(mine[:, :part], other[:, :part], core)
-    grad_up = both_halves(mine[:, part:], other[:, part:], core)
-    mine, other = own_rows(down_sum, core)
-    grad_down = both_halves(mine, other, core)
-    joined = jnp.concatenate(sums, axis=1)
-    mine, other = own_rows(joined, core)
-    small = [
-        both_halves(mine[:, half * i : half * (i + 1)], other[:, half * i : half * (i + 1)], core)
-        for i in range(5)
+    attn_sends = [
+        weight_gradient(after(places[s], gots[s]), core_at, *job)[0]
+        for s, job in enumerate(attn_jobs)
     ]
-    misc_sum = mine[:, 5 * half :].astype(F32) + other[:, 5 * half :].astype(F32)
+    attn_gots = exchange(attn_sends, 0)
+
+    def kept(jobs, gots):
+        pairs = [
+            weight_gradient(places[s], core_at, *job, got=gots[s]) for s, job in enumerate(jobs)
+        ]
+        return [p[0] for p in pairs], [p[1] for p in pairs]
+
+    keeps, sends = kept(jobs, gots)
+    gots = exchange(sends, 1)
+    attn_keeps, attn_sends = kept(attn_jobs, [after(got, keeps) for got in attn_gots])
+    attn_gots = exchange(attn_sends, 1)
+    first, second = list(zip(keeps, gots)), list(zip(attn_keeps, attn_gots))
+    groups = [[first[0], second[0]], [first[1], second[1]], [first[2]], [second[2]]]
+    for step in range(2, 6):
+        keeps, sends = add_halves(groups)
+        gots = exchange(sends, step, (0, 1, 2, 2))
+        groups = [[pair] for pair in zip(keeps, gots)]
+    mine, theirs, mine_down, theirs_down = last_add(core_at, [group[0] for group in groups])
+    *large, misc_sum = finish(core_at, mine, swap(theirs), mine_down, swap(theirs_down))
+
     return (
         mixed.reshape(seqs, count, width),
         grad_tokens.reshape(seqs, count, width),
         misc_sum[:, heads],
-        small[0],
-        small[1],
-        small[2],
-        small[3],
+        *large[:4],
         misc_sum[:, :heads],
-        small[4],
+        large[4],
         misc_sum[:, heads + 1],
-        grad_gate,
-        grad_up,
-        grad_down,
+        *large[5:],
     )
 
 

time: 580 us -> 402 us (0.69)
  waiting for transfers between devices: 309 us -> 177 us
  Pallas kernels: 161 us -> 111 us
  starting transfers between devices: 56.4 us -> 72.4 us
  other arithmetic: 15.6 us -> 1.98 us
    all_gather x1, waiting for transfers between devices: 133 us -> 60.1 us  [body(): lax.all_gather(slab, 'fsdp', axis=0, tiled=True, axis_index_groups=by_core)]
    all_gather x1 -> x0, waiting for transfers between devices: 54.7 us -> none  [body(): lax.all_gather(slab_down, 'fsdp', axis=0, tiled=True, axis_index_groups=b...]
    pallas_call x17 -> x19, Pallas kernels: 91 us -> 43.8 us  [the longest x12 36.2 us: weight_gradient(): pl.pallas_call(functools.partial(weight_gradient_kernel, segments, len(xs...]
    ppermute x36 -> x46, starting transfers between devices: 29.7 us -> 48.1 us  [send_step(): return lax.ppermute(value, 'fsdp', pairs)]
    ppermute x36 -> x46, waiting for transfers between devices: 117 us -> 104 us  [send_step(): return lax.ppermute(value, 'fsdp', pairs)]
    ppermute x12 -> x13, waiting for transfers between devices: 3.75 us -> 13.1 us  [swap(): return lax.ppermute(value, 'fsdp', [(d, d ^ 1) for d in range(count)])]
    concatenate x0 -> x6, local copies, waits for them, and re-layouts: none -> 7.08 us  [gather_streams(): parts = [jnp.concatenate(pair, axis=0) for pair in zip(parts, gots)]]
    ppermute x12 -> x13, starting transfers between devices: 26.6 us -> 24.3 us  [swap(): return lax.ppermute(value, 'fsdp', [(d, d ^ 1) for d in range(count)])]
  transfers between devices with their start and end apart: 50 -> 60, of which waited for: 29 -> 30; matrix products, arithmetic and copies ran while one was open for 3% -> 4% of each run, Pallas kernels for 17% -> 20%
where the time goes in v2:
time: 402 us; the launch traced here: 401 us
  waiting for transfers between devices  177 us (44%)
  Pallas kernels  111 us (28%)
  starting transfers between devices  72.4 us (18%)
  local copies, waits for them, and re-layouts  23.9 us (6%)
  between operations  15.2 us (4%)
    ppermute x46, waiting for transfers between devices, send_step(): return lax.ppermute(value, 'fsdp', pairs)  104 us
    all_gather x1, waiting for transfers between devices, body(): lax.all_gather(slab, 'fsdp', axis=0, tiled=True, axis_index_groups=by_core)  60.1 us
    ppermute x46, starting transfers between devices, send_step(): return lax.ppermute(value, 'fsdp', pairs)  48.1 us
    pallas_call x12, Pallas kernels, weight_gradient(): pl.pallas_call(functools.partial(weight_gradient_kernel, segments, len(xs...  36.2 us
    pallas_call x1, Pallas kernels, feedforward(): pl.pallas_call(feedforward_kernel, grid_spec=pltpu.PrefetchScalarGridSpec...  26.1 us
    ppermute x13, starting transfers between devices, swap(): return lax.ppermute(value, 'fsdp', [(d, d ^ 1) for d in range(count)])  24.3 us
    pallas_call x1, Pallas kernels, attention_forward(): pl.pallas_call(attention_forward_kernel, grid_spec=pltpu.PrefetchScalarGr...  21.4 us
    pallas_call x1, Pallas kernels, attention_backward(): pl.pallas_call(attention_backward_kernel, grid=(steps,), in_specs=[rows,...  19.4 us
  transfers between devices with their start and end apart: 60, of which 30 were waited for; matrix products, arithmetic and copies ran while one was open for 4% of the time, Pallas kernels for 20%

profile of v2, /device:TPU:1, one launch (start us, length us, event | category | flops | bytes accessed | tf_op | source)
XLA Modules:
  0.0 401.2 jit_solution(7638103488502965830)
XLA Ops:
  25.5 3.3 collective-permute-start.15
  40.0 3.9 collective-permute-done.5
  47.9 7.6 %collective-permute-done.6 = bf16[16,64,256]{2,1,0:T(8,128)(2,1)S(1)} collective-permute-done((bf16[16,64,256]{2,1,0:T(8,128)(2,1)S(1)}, bf16[16,64,256]{2,1,0:T(8,128)(2,1)S(1)}, u32[]{:S(2)}, u32[]{:S(2)}) %collective-permute-start.6) | collective-permute-done | bytes 524320 | tf_op jit(solution)/shard_map/ppermute | solution.py:849
  56.4 4.9 %collective-permute-start.7 = (bf16[32,64,256]{2,1,0:T(8,128)(2,1)}, bf16[32,64,256]{2,1,0:T(8,128)(2,1)S(1)}, u32[]{:S(2)}, u32[]{:S(2)}) collective-permute-start(bf16[32,64,256]{2,1,0:T(8,128)(2,1)} %get-tuple-element.189), channel_id=1, source_target_pairs={{0,32},{1,97},{2,34},{3,99},{4,36},{5,101},{6,38},{7,103},{8,40},{... | collective-permute-start | bytes 3145736 | tf_op jit(solution)/shard_map/ppermute | solution.py:849
  64.7 21.7 %collective-permute-done.7 = bf16[32,64,256]{2,1,0:T(8,128)(2,1)S(1)} collective-permute-done((bf16[32,64,256]{2,1,0:T(8,128)(2,1)}, bf16[32,64,256]{2,1,0:T(8,128)(2,1)S(1)}, u32[]{:S(2)}, u32[]{:S(2)}) %collective-permute-start.7) | collective-permute-done | bytes 1048608 | tf_op jit(solution)/shard_map/ppermute | solution.py:849
  90.9 4.7 %in_order.1 = bf16[64,64,768]{2,1,0:T(8,128)(2,1)} custom-call(s32[3,64]{1,0:T(4,128)S(1)} %get-tuple-element.248.place_ref, bf16[64,64,256]{2,1,0:T(8,128)(2,1)S(1)} %copy-done.11, bf16[64,64,256]{2,1,0:T(8,128)(2,1)S(1)} %constant_dynamic-update-slice_fusion.29.refs_1_, bf16[64,64,256]{2,1,0:T(8,128)(2,1)S(1)} %constant_dynamic-update-slice_fusion.47.refs_2_), custom_call_target="tpu_custom_call" | custom-call | flops 1 | bytes 1 | tf_op jit(solution)/shard_map/in_order/pallas_call | solution.py:884
  95.6 7.7 %collective-permute-start.20 = (bf16[4096,768]{1,0:T(8,128)(2,1)}, bf16[4096,768]{1,0:T(8,128)(2,1)}, u32[]{:S(2)}, u32[]{:S(2)}) collective-permute-start(bf16[4096,768]{1,0:T(8,128)(2,1)} %bitcast.10.down_own_ref), channel_id=1, source_target_pairs={{0,1},{1,0},{2,3},{3,2},{4,5},{5,4},{6,7},{7,6},{8,9},{9,8},{10,11... | collective-permute-start | bytes 18874376 | tf_op jit(solution)/shard_map/ppermute | solution.py:71
  104.1 60.1 %all-gather.2.cloned.1.call-done.wq_ref.wk_ref.wv_ref.wh_ref.misc_ref.out_lo_ref.out_hi_ref.wg_ref.wu_ref.wo_lo_ref.wo_hi_ref = bf16[3072,8192]{1,0:T(8,128)(2,1)} async-done(((bf16[24,8192]{1,0:T(8,128)(2,1)}), bf16[3072,8192]{1,0:T(8,128)(2,1)}) %all-gather.2.cloned.1.call-update) | async-done | bytes 50331664 | tf_op jit(solution)/shard_map/all_gather | solution.py:952
  164.2 21.4 %attention_forward.1 = (bf16[1536,128]{1,0:T(8,128)(2,1)S(1)}, bf16[128,1536]{1,0:T(8,128)(2,1)S(1)}, bf16[128,1536]{1,0:T(8,128)(2,1)S(1)}, bf16[128,1536]{1,0:...) custom-call(s32[1]{0:T(128)} %copy.81.length_ref, ...), custom_call_target="tpu_custom_call" | custom-call | flops 5435817984 | bytes 23592960 | tf_op jit(solution)/shard_map/attention_forward/pallas_call | solution.py:206
  185.7 26.1 %feedforward.1 = (bf16[1536,128]{1,0:T(8,128)(2,1)S(1)}, bf16[4096,128]{1,0:T(8,128)(2,1)S(1)}, bf16[2,128,4096]{2,1,0:T(8,128)(2,1)}, bf16[128,1536]{1,0:T(8,12...) custom-call(s32[1]{0:T(128)} %copy.81.length_ref, ...), custom_call_target="tpu_custom_call" | custom-call | flops 9663676416 | bytes 37748736 | tf_op jit(solution)/shard_map/feedforward/pallas_call | solution.py:351
  212.6 2.9 collective-permute-done.24
  215.5 3.5 weight_gradient.8
  224.2 3.6 weight_gradient.6
  230.3 3.6 weight_gradient.7
  234.4 19.4 %attention_backward.1 = (bf16[4,128,1536]{2,1,0:T(8,128)(2,1)S(1)}, f32[128,1536]{1,0:T(8,128)}, bf16[1536,128]{1,0:T(8,128)(2,1)S(1)}) custom-call(bf16[128,1536]{1,0:T(8,128)(2,1)S(1)} %bitcast.84, bf16[1536,128]{1,0:T(8,128)(2,1)S(1)} %get-tuple-element.100.normed_t_ref, bf16[128,1536]{1,0:T(8,128)(2,1)S(1)} %get-tuple-element.105.branch_ref, ...), custom_call_target="tpu_custom_call" | custom-call | flops 1 | bytes 1 | tf_op jit(solution)/shard_map/attention_backward/pallas_call | solution.py:564
  254.3 3.5 collective-permute-done.27
  265.4 3.2 weight_gradient.9
  273.9 3.3 weight_gradient_add.8
  278.4 3.3 weight_gradient_add.6
  284.0 12.7 %collective-permute-done.39.refs_11_.refs_12_ = bf16[32,24,1408]{2,1,0:T(8,128)(2,1)S(1)} collective-permute-done((bf16[32,24,1408]{2,1,0:T(8,128)(2,1)S(1)}, bf16[32,24,1408]{2,1,0:T(8,128)(2,1)S(1)}, u32[]{:S(2)}, u32[]{:S(2)}) %collective-permute-start.39) | collective-permute-done | bytes 2162720 | tf_op jit(solution)/shard_map/ppermute | solution.py:849
  301.3 3.8 weight_gradient_add.9
  305.2 3.7 weight_gradient_add.10
  310.0 6.3 %collective-permute-done.33.refs_10_.refs_11_ = bf16[16,24,2048]{2,1,0:T(8,128)(2,1)S(1)} collective-permute-done((bf16[16,24,2048]{2,1,0:T(8,128)(2,1)S(1)}, bf16[16,24,2048]{2,1,0:T(8,128)(2,1)S(1)}, u32[]{:S(2)}, u32[]{:S(2)}) %collective-permute-start.33) | collective-permute-done | bytes 1572896 | tf_op jit(solution)/shard_map/ppermute | solution.py:849
  317.1 3.5 collective-permute-done.32.refs_6_.refs_7_
  320.5 6.3 %collective-permute-done.35.refs_14_.refs_15_ = bf16[16,24,1280]{2,1,0:T(8,128)(2,1)S(1)} collective-permute-done((bf16[16,24,1280]{2,1,0:T(8,128)(2,1)S(1)}, bf16[16,24,1280]{2,1,0:T(8,128)(2,1)S(1)}, u32[]{:S(2)}, u32[]{:S(2)}) %collective-permute-start.35) | collective-permute-done | bytes 983072 | tf_op jit(solution)/shard_map/ppermute | solution.py:849
  327.7 3.0 collective-permute-start.41
  334.9 15.2 %collective-permute-done.44.refs_14_.refs_15_ = bf16[8,24,1408]{2,1,0:T(8,128)(2,1)S(1)} collective-permute-done((bf16[8,24,1408]{2,1,0:T(8,128)(2,1)S(1)}, bf16[8,24,1408]{2,1,0:T(8,128)(2,1)S(1)}, u32[]{:S(2)}, u32[]{:S(2)}) %collective-permute-start.44) | collective-permute-done | bytes 540704 | tf_op jit(solution)/shard_map/ppermute | solution.py:849
  352.3 8.4 %collective-permute-done.48.refs_14_.refs_15_ = bf16[4,24,1408]{2,1,0:T(8,128)(2,1)S(1)} collective-permute-done((bf16[4,24,1408]{2,1,0:T(8,128)(2,1)S(1)}, bf16[4,24,1408]{2,1,0:T(8,128)(2,1)S(1)}, u32[]{:S(2)}, u32[]{:S(2)}) %collective-permute-start.48) | collective-permute-done | bytes 270368 | tf_op jit(solution)/shard_map/ppermute | solution.py:849
  362.2 2.6 collective-permute-start.51
  364.8 5.0 %collective-permute-done.52.refs_14_.refs_15_ = bf16[2,24,1408]{2,1,0:T(8,128)(2,1)S(1)} collective-permute-done((bf16[2,24,1408]{2,1,0:T(8,128)(2,1)S(1)}, bf16[2,24,1408]{2,1,0:T(8,128)(2,1)S(1)}, u32[]{:S(2)}, u32[]{:S(2)}) %collective-permute-start.52) | collective-permute-done | bytes 135200 | tf_op jit(solution)/shard_map/ppermute | solution.py:849
  372.9 4.4 %collective-permute-done.56.refs_7_ = bf16[1,24,1408]{2,1,0:T(8,128)(2,1)S(1)} collective-permute-done((bf16[1,24,1408]{2,1,0:T(8,128)(2,1)S(1)}, bf16[1,24,1408]{2,1,0:T(8,128)(2,1)S(1)}, u32[]{:S(2)}, u32[]{:S(2)}) %collective-permute-start.56) | collective-permute-done | bytes 67616 | tf_op jit(solution)/shard_map/ppermute | solution.py:849
  377.9 12.7 %collective-permute-start.57 = (bf16[12,8064]{1,0:T(8,128)(2,1)S(1)}, bf16[12,8064]{1,0:T(8,128)(2,1)S(1)}, u32[]{:S(2)}, u32[]{:S(2)}) collective-permute-start(bf16[12,8064]{1,0:T(8,128)(2,1)S(1)} %get-tuple-element.171), channel_id=1, source_target_pairs={{0,1},{1,0},{2,3},{3,2},{4,5},{5,4},{6,7},{7,6},{8,9},{9,8},{10,11... | collective-permute-start | bytes 580616 | tf_op jit(solution)/shard_map/ppermute | solution.py:71
  (197 shorter events, 90.7 us)
Async XLA Ops:
  7.2 157.0 %all-gather.2.cloned.1.call-start = ((), (), s32[]{:S(2)}) async-start(), calls=%async_computation | async-start | bytes 50724864 | tf_op jit(solution)/shard_map/all_gather | solution.py:952
  34.6 9.3 %collective-permute-start.5 = (bf16[8,64,256]{2,1,0:T(8,128)(2,1)S(1)}, bf16[8,64,256]{2,1,0:T(8,128)(2,1)S(1)}, u32[]{:S(2)}, u32[]{:S(2)}) collective-permute-start(bf16[8,64,256]{2,1,0:T(8,128)(2,1)S(1)} %pad_maximum_fusion), channel_id=1, source_target_pairs={{0,8},{1,25},{2,10},{3,27},{4,12},{5,29},{6,14},{7,31},{8,0},{9,17... | collective-permute-start | bytes 786440 | tf_op jit(solution)/shard_map/ppermute | solution.py:849
  37.1 9.9 %collective-permute-start.17 = (bf16[8,64,256]{2,1,0:T(8,128)(2,1)S(1)}, bf16[8,64,256]{2,1,0:T(8,128)(2,1)S(1)}, u32[]{:S(2)}, u32[]{:S(2)}) collective-permute-start(bf16[8,64,256]{2,1,0:T(8,128)(2,1)S(1)} %pad_maximum_fusion.2), channel_id=1, source_target_pairs={{0,32},{1,97},{2,34},{3,99},{4,36},{5,101},{6,38},{7,103},{8,40},{... | collective-permute-start | bytes 786440 | tf_op jit(solution)/shard_map/ppermute | solution.py:849
  44.7 10.8 %collective-permute-start.6 = (bf16[16,64,256]{2,1,0:T(8,128)(2,1)S(1)}, bf16[16,64,256]{2,1,0:T(8,128)(2,1)S(1)}, u32[]{:S(2)}, u32[]{:S(2)}) collective-permute-start(bf16[16,64,256]{2,1,0:T(8,128)(2,1)S(1)} %get-tuple-element.203), channel_id=1, source_target_pairs={{0,96},{1,33},{2,98},{3,35},{4,100},{5,37},{6,102},{7,39},{8,104},... | collective-permute-start | bytes 1572872 | tf_op jit(solution)/shard_map/ppermute | solution.py:849
  46.1 15.2 %collective-permute-start.12 = (bf16[16,64,256]{2,1,0:T(8,128)(2,1)S(1)}, bf16[16,64,256]{2,1,0:T(8,128)(2,1)S(1)}, u32[]{:S(2)}, u32[]{:S(2)}) collective-permute-start(bf16[16,64,256]{2,1,0:T(8,128)(2,1)S(1)} %get-tuple-element.200), channel_id=1, source_target_pairs={{0,24},{1,9},{2,26},{3,11},{4,28},{5,13},{6,30},{7,15},{8,16},{9,1... | collective-permute-start | bytes 1572872 | tf_op jit(solution)/shard_map/ppermute | solution.py:849
  47.7 14.9 %collective-permute-start.18 = (bf16[16,64,256]{2,1,0:T(8,128)(2,1)S(1)}, bf16[16,64,256]{2,1,0:T(8,128)(2,1)S(1)}, u32[]{:S(2)}, u32[]{:S(2)}) collective-permute-start(bf16[16,64,256]{2,1,0:T(8,128)(2,1)S(1)} %get-tuple-element.197), channel_id=1, source_target_pairs={{0,6},{1,3},{2,4},{3,1},{4,2},{5,7},{6,0},{7,5},{8,14},{9,11},{10,... | collective-permute-start | bytes 1572872 | tf_op jit(solution)/shard_map/ppermute | solution.py:849
  56.4 30.0 %collective-permute-start.7 = (bf16[32,64,256]{2,1,0:T(8,128)(2,1)}, bf16[32,64,256]{2,1,0:T(8,128)(2,1)S(1)}, u32[]{:S(2)}, u32[]{:S(2)}) collective-permute-start(bf16[32,64,256]{2,1,0:T(8,128)(2,1)} %get-tuple-element.189), channel_id=1, source_target_pairs={{0,32},{1,97},{2,34},{3,99},{4,36},{5,101},{6,38},{7,103},{8,40},{... | collective-permute-start | bytes 3145736 | tf_op jit(solution)/shard_map/ppermute | solution.py:849
  62.2 25.5 %collective-permute-start.13 = (bf16[32,64,256]{2,1,0:T(8,128)(2,1)}, bf16[32,64,256]{2,1,0:T(8,128)(2,1)}, u32[]{:S(2)}, u32[]{:S(2)}) collective-permute-start(bf16[32,64,256]{2,1,0:T(8,128)(2,1)} %get-tuple-element.187), channel_id=1, source_target_pairs={{0,8},{1,25},{2,10},{3,27},{4,12},{5,29},{6,14},{7,31},{8,0},{9,17... | collective-permute-start | bytes 3145736 | tf_op jit(solution)/shard_map/ppermute | solution.py:849
  63.7 25.5 %collective-permute-start.19 = (bf16[32,64,256]{2,1,0:T(8,128)(2,1)}, bf16[32,64,256]{2,1,0:T(8,128)(2,1)}, u32[]{:S(2)}, u32[]{:S(2)}) collective-permute-start(bf16[32,64,256]{2,1,0:T(8,128)(2,1)} %get-tuple-element.185), channel_id=1, source_target_pairs={{0,2},{1,7},{2,0},{3,5},{4,6},{5,3},{6,4},{7,1},{8,10},{9,15},{10,... | collective-permute-start | bytes 3145736 | tf_op jit(solution)/shard_map/ppermute | solution.py:849
  95.6 90.1 %collective-permute-start.20 = (bf16[4096,768]{1,0:T(8,128)(2,1)}, bf16[4096,768]{1,0:T(8,128)(2,1)}, u32[]{:S(2)}, u32[]{:S(2)}) collective-permute-start(bf16[4096,768]{1,0:T(8,128)(2,1)} %bitcast.10.down_own_ref), channel_id=1, source_target_pairs={{0,1},{1,0},{2,3},{3,2},{4,5},{5,4},{6,7},{7,6},{8,9},{9,8},{10,11... | collective-permute-start | bytes 18874376 | tf_op jit(solution)/shard_map/ppermute | solution.py:71
  212.0 12.2 %collective-permute-start.22 = (bf16[2,128,4096]{2,1,0:T(8,128)(2,1)}, bf16[2,128,4096]{2,1,0:T(8,128)(2,1)S(1)}, u32[]{:S(2)}, u32[]{:S(2)}) collective-permute-start(bf16[2,128,4096]{2,1,0:T(8,128)(2,1)} %get-tuple-element.103.refs_4_), channel_id=1, source_target_pairs={{0,1},{1,0},{2,3},{3,2},{4,5},{5,4},{6,7},{7,6},{8,9},{9,8},{10,11... | collective-permute-start | bytes 6291464 | tf_op jit(solution)/shard_map/ppermute | solution.py:71
  220.1 37.9 %collective-permute-start.31 = (bf16[32,64,768]{2,1,0:T(8,128)(2,1)}, bf16[32,64,768]{2,1,0:T(8,128)(2,1)S(1)}, u32[]{:S(2)}, u32[]{:S(2)}) collective-permute-start(bf16[32,64,768]{2,1,0:T(8,128)(2,1)} %weight_gradient.8), channel_id=1, source_target_pairs={{0,2},{1,7},{2,0},{3,5},{4,6},{5,3},{6,4},{7,1},{8,10},{9,15},{10,... | collective-permute-start | bytes 9437192 | tf_op jit(solution)/shard_map/ppermute | solution.py:849
  227.9 37.5 %collective-permute-start.25 = (bf16[32,24,2048]{2,1,0:T(8,128)(2,1)}, bf16[32,24,2048]{2,1,0:T(8,128)(2,1)S(1)}, u32[]{:S(2)}, u32[]{:S(2)}) collective-permute-start(bf16[32,24,2048]{2,1,0:T(8,128)(2,1)} %weight_gradient.6), channel_id=1, source_target_pairs={{0,32},{1,97},{2,34},{3,99},{4,36},{5,101},{6,38},{7,103},{8,40},{... | collective-permute-start | bytes 9437192 | tf_op jit(solution)/shard_map/ppermute | solution.py:849
  233.9 37.5 %collective-permute-start.30 = (bf16[32,24,2048]{2,1,0:T(8,128)(2,1)}, bf16[32,24,2048]{2,1,0:T(8,128)(2,1)S(1)}, u32[]{:S(2)}, u32[]{:S(2)}) collective-permute-start(bf16[32,24,2048]{2,1,0:T(8,128)(2,1)} %weight_gradient.7), channel_id=1, source_target_pairs={{0,8},{1,25},{2,10},{3,27},{4,12},{5,29},{6,14},{7,31},{8,0},{9,17... | collective-permute-start | bytes 9437192 | tf_op jit(solution)/shard_map/ppermute | solution.py:849
  262.1 34.7 %collective-permute-start.39 = (bf16[32,24,1408]{2,1,0:T(8,128)(2,1)S(1)}, bf16[32,24,1408]{2,1,0:T(8,128)(2,1)S(1)}, u32[]{:S(2)}, u32[]{:S(2)}) collective-permute-start(bf16[32,24,1408]{2,1,0:T(8,128)(2,1)S(1)} %weight_gradient.11), channel_id=1, source_target_pairs={{0,2},{1,7},{2,0},{3,5},{4,6},{5,3},{6,4},{7,1},{8,10},{9,15},{10,... | collective-permute-start | bytes 6488072 | tf_op jit(solution)/shard_map/ppermute | solution.py:849
  268.6 32.7 %collective-permute-start.29 = (bf16[32,24,1280]{2,1,0:T(8,128)(2,1)}, bf16[32,24,1280]{2,1,0:T(8,128)(2,1)}, u32[]{:S(2)}, u32[]{:S(2)}) collective-permute-start(bf16[32,24,1280]{2,1,0:T(8,128)(2,1)} %weight_gradient.9), channel_id=1, source_target_pairs={{0,32},{1,97},{2,34},{3,99},{4,36},{5,101},{6,38},{7,103},{8,40},{... | collective-permute-start | bytes 5898248 | tf_op jit(solution)/shard_map/ppermute | solution.py:849
  273.3 31.7 %collective-permute-start.34 = (bf16[32,24,1280]{2,1,0:T(8,128)(2,1)S(1)}, bf16[32,24,1280]{2,1,0:T(8,128)(2,1)}, u32[]{:S(2)}, u32[]{:S(2)}) collective-permute-start(bf16[32,24,1280]{2,1,0:T(8,128)(2,1)S(1)} %weight_gradient.10), channel_id=1, source_target_pairs={{0,8},{1,25},{2,10},{3,27},{4,12},{5,29},{6,14},{7,31},{8,0},{9,17... | collective-permute-start | bytes 5898248 | tf_op jit(solution)/shard_map/ppermute | solution.py:849
  278.4 30.5 %collective-permute-start.36 = (bf16[16,64,768]{2,1,0:T(8,128)(2,1)}, bf16[16,64,768]{2,1,0:T(8,128)(2,1)S(1)}, u32[]{:S(2)}, u32[]{:S(2)}) collective-permute-start(bf16[16,64,768]{2,1,0:T(8,128)(2,1)} %get-tuple-element.131), channel_id=1, source_target_pairs={{0,6},{1,3},{2,4},{3,1},{4,2},{5,7},{6,0},{7,5},{8,14},{9,11},{10,... | collective-permute-start | bytes 4718600 | tf_op jit(solution)/shard_map/ppermute | solution.py:849
  281.7 28.3 %collective-permute-start.26 = (bf16[16,24,2048]{2,1,0:T(8,128)(2,1)}, bf16[16,24,2048]{2,1,0:T(8,128)(2,1)S(1)}, u32[]{:S(2)}, u32[]{:S(2)}) collective-permute-start(bf16[16,24,2048]{2,1,0:T(8,128)(2,1)} %get-tuple-element.118), channel_id=1, source_target_pairs={{0,96},{1,33},{2,98},{3,35},{4,100},{5,37},{6,102},{7,39},{8,104},... | collective-permute-start | bytes 4718600 | tf_op jit(solution)/shard_map/ppermute | solution.py:849
  296.7 19.6 %collective-permute-start.33 = (bf16[16,24,2048]{2,1,0:T(8,128)(2,1)S(1)}, bf16[16,24,2048]{2,1,0:T(8,128)(2,1)S(1)}, u32[]{:S(2)}, u32[]{:S(2)}) collective-permute-start(bf16[16,24,2048]{2,1,0:T(8,128)(2,1)S(1)} %get-tuple-element.126), channel_id=1, source_target_pairs={{0,24},{1,9},{2,26},{3,11},{4,28},{5,13},{6,30},{7,15},{8,16},{9,1... | collective-permute-start | bytes 4718600 | tf_op jit(solution)/shard_map/ppermute | solution.py:849
  301.3 15.8 %collective-permute-start.40 = (bf16[16,24,1408]{2,1,0:T(8,128)(2,1)S(1)}, bf16[16,24,1408]{2,1,0:T(8,128)(2,1)S(1)}, u32[]{:S(2)}, u32[]{:S(2)}) collective-permute-start(bf16[16,24,1408]{2,1,0:T(8,128)(2,1)S(1)} %get-tuple-element.137), channel_id=1, source_target_pairs={{0,6},{1,3},{2,4},{3,1},{4,2},{5,7},{6,0},{7,5},{8,14},{9,11},{10,... | collective-permute-start | bytes 3244040 | tf_op jit(solution)/shard_map/ppermute | solution.py:849
  305.1 15.4 %collective-permute-start.32 = (bf16[16,24,1280]{2,1,0:T(8,128)(2,1)S(1)}, bf16[16,24,1280]{2,1,0:T(8,128)(2,1)S(1)}, u32[]{:S(2)}, u32[]{:S(2)}) collective-permute-start(bf16[16,24,1280]{2,1,0:T(8,128)(2,1)S(1)} %get-tuple-element.125), channel_id=1, source_target_pairs={{0,96},{1,33},{2,98},{3,35},{4,100},{5,37},{6,102},{7,39},{8,104},... | collective-permute-start | bytes 2949128 | tf_op jit(solution)/shard_map/ppermute | solution.py:849
  308.9 17.9 %collective-permute-start.35 = (bf16[16,24,1280]{2,1,0:T(8,128)(2,1)S(1)}, bf16[16,24,1280]{2,1,0:T(8,128)(2,1)S(1)}, u32[]{:S(2)}, u32[]{:S(2)}) collective-permute-start(bf16[16,24,1280]{2,1,0:T(8,128)(2,1)S(1)} %get-tuple-element.130), channel_id=1, source_target_pairs={{0,24},{1,9},{2,26},{3,11},{4,28},{5,13},{6,30},{7,15},{8,16},{9,1... | collective-permute-start | bytes 2949128 | tf_op jit(solution)/shard_map/ppermute | solution.py:849
  327.7 22.4 %collective-permute-start.41 = (bf16[8,24,3328]{2,1,0:T(8,128)(2,1)S(1)}, bf16[8,24,3328]{2,1,0:T(8,128)(2,1)S(1)}, u32[]{:S(2)}, u32[]{:S(2)}) collective-permute-start(bf16[8,24,3328]{2,1,0:T(8,128)(2,1)S(1)} %get-tuple-element.139), channel_id=1, source_target_pairs={{0,8},{1,25},{2,10},{3,27},{4,12},{5,29},{6,14},{7,31},{8,0},{9,17... | collective-permute-start | bytes 3833864 | tf_op jit(solution)/shard_map/ppermute | solution.py:849
  330.7 19.4 %collective-permute-start.42 = (bf16[8,24,3328]{2,1,0:T(8,128)(2,1)S(1)}, bf16[8,24,3328]{2,1,0:T(8,128)(2,1)S(1)}, u32[]{:S(2)}, u32[]{:S(2)}) collective-permute-start(bf16[8,24,3328]{2,1,0:T(8,128)(2,1)S(1)} %get-tuple-element.141), channel_id=1, source_target_pairs={{0,2},{1,7},{2,0},{3,5},{4,6},{5,3},{6,4},{7,1},{8,10},{9,15},{10,... | collective-permute-start | bytes 3833864 | tf_op jit(solution)/shard_map/ppermute | solution.py:849
  332.2 17.8 %collective-permute-start.43 = (bf16[8,64,768]{2,1,0:T(8,128)(2,1)S(1)}, bf16[8,64,768]{2,1,0:T(8,128)(2,1)S(1)}, u32[]{:S(2)}, u32[]{:S(2)}) collective-permute-start(bf16[8,64,768]{2,1,0:T(8,128)(2,1)S(1)} %get-tuple-element.143), channel_id=1, source_target_pairs={{0,32},{1,97},{2,34},{3,99},{4,36},{5,101},{6,38},{7,103},{8,40},{... | collective-permute-start | bytes 2359304 | tf_op jit(solution)/shard_map/ppermute | solution.py:849
  333.3 16.7 %collective-permute-start.44 = (bf16[8,24,1408]{2,1,0:T(8,128)(2,1)S(1)}, bf16[8,24,1408]{2,1,0:T(8,128)(2,1)S(1)}, u32[]{:S(2)}, u32[]{:S(2)}) collective-permute-start(bf16[8,24,1408]{2,1,0:T(8,128)(2,1)S(1)} %get-tuple-element.145), channel_id=1, source_target_pairs={{0,32},{1,97},{2,34},{3,99},{4,36},{5,101},{6,38},{7,103},{8,40},{... | collective-permute-start | bytes 1622024 | tf_op jit(solution)/shard_map/ppermute | solution.py:849
  350.5 10.1 %collective-permute-start.45 = (bf16[4,24,3328]{2,1,0:T(8,128)(2,1)S(1)}, bf16[4,24,3328]{2,1,0:T(8,128)(2,1)S(1)}, u32[]{:S(2)}, u32[]{:S(2)}) collective-permute-start(bf16[4,24,3328]{2,1,0:T(8,128)(2,1)S(1)} %get-tuple-element.147), channel_id=1, source_target_pairs={{0,24},{1,9},{2,26},{3,11},{4,28},{5,13},{6,30},{7,15},{8,16},{9,1... | collective-permute-start | bytes 1916936 | tf_op jit(solution)/shard_map/ppermute | solution.py:849
  350.6 10.0 %collective-permute-start.46 = (bf16[4,24,3328]{2,1,0:T(8,128)(2,1)S(1)}, bf16[4,24,3328]{2,1,0:T(8,128)(2,1)S(1)}, u32[]{:S(2)}, u32[]{:S(2)}) collective-permute-start(bf16[4,24,3328]{2,1,0:T(8,128)(2,1)S(1)} %get-tuple-element.149), channel_id=1, source_target_pairs={{0,6},{1,3},{2,4},{3,1},{4,2},{5,7},{6,0},{7,5},{8,14},{9,11},{10,... | collective-permute-start | bytes 1916936 | tf_op jit(solution)/shard_map/ppermute | solution.py:849
  350.7 9.9 %collective-permute-start.47 = (bf16[4,64,768]{2,1,0:T(8,128)(2,1)S(1)}, bf16[4,64,768]{2,1,0:T(8,128)(2,1)S(1)}, u32[]{:S(2)}, u32[]{:S(2)}) collective-permute-start(bf16[4,64,768]{2,1,0:T(8,128)(2,1)S(1)} %get-tuple-element.151), channel_id=1, source_target_pairs={{0,96},{1,33},{2,98},{3,35},{4,100},{5,37},{6,102},{7,39},{8,104},... | collective-permute-start | bytes 1179656 | tf_op jit(solution)/shard_map/ppermute | solution.py:849
  350.8 9.8 %collective-permute-start.48 = (bf16[4,24,1408]{2,1,0:T(8,128)(2,1)S(1)}, bf16[4,24,1408]{2,1,0:T(8,128)(2,1)S(1)}, u32[]{:S(2)}, u32[]{:S(2)}) collective-permute-start(bf16[4,24,1408]{2,1,0:T(8,128)(2,1)S(1)} %get-tuple-element.153), channel_id=1, source_target_pairs={{0,96},{1,33},{2,98},{3,35},{4,100},{5,37},{6,102},{7,39},{8,104},... | collective-permute-start | bytes 811016 | tf_op jit(solution)/shard_map/ppermute | solution.py:849
  377.9 14.0 %collective-permute-start.57 = (bf16[12,8064]{1,0:T(8,128)(2,1)S(1)}, bf16[12,8064]{1,0:T(8,128)(2,1)S(1)}, u32[]{:S(2)}, u32[]{:S(2)}) collective-permute-start(bf16[12,8064]{1,0:T(8,128)(2,1)S(1)} %get-tuple-element.171), channel_id=1, source_target_pairs={{0,1},{1,0},{2,3},{3,2},{4,5},{5,4},{6,7},{7,6},{8,9},{9,8},{10,11... | collective-permute-start | bytes 580616 | tf_op jit(solution)/shard_map/ppermute | solution.py:71
  (48 other events, 414.9 us)
Sparse Core Ops, SparseCore 0:
  15.3 148.8 all-gather.1

commit v3 on v2

--- a/solution.py
+++ b/solution.py
@@ -104,7 +104,9 @@
     return inverses
 
 
-PER_STEP = 2
+PER_STEP = 4
+SPAN = 128 * PER_STEP
+GATE_AT, UP_AT, FIRST_AT, SECOND_AT = 1024, 3072, 5120, 6656
 
 
 def attention_forward_kernel(
@@ -114,18 +116,22 @@
     wk_ref,
     wv_ref,
     wh_ref,
+    out_lo_ref,
+    out_hi_ref,
     misc_ref,
     normed_t_ref,
     q_ref,
     k_ref,
     v_ref,
     h_ref,
-    att_ref,
+    hidden_ref,
+    second_ref,
     att_t_ref,
     probs_ref,
     carried_ref,
     inverse_ref,
     beta_ref,
+    gain_ref,
     normed_ref,
 ):
     at = pl.program_id(0)
@@ -138,6 +144,7 @@
         normed_ref[...] = value.astype(BF)
         normed_t_ref[...] = value.T.astype(BF)
         beta_ref[...] = dot(normed_ref[...], misc_ref[...])
+        hidden_ref[...] = tokens
 
     normed = normed_ref[...]
     q_all = dot(normed, wq_ref[...]).astype(BF)
@@ -175,6 +182,7 @@
     through = [
         dot_fine(jnp.where(upto, big[i][count:, :count], 0.0), carried[i]) for i in heads
     ]
+    attended = []
     for i in heads:
         logits = (big[i][count:, count:] - through[i]) * 128 ** (-0.5)
         logits = jnp.where(allowed, logits, -1e30)
@@ -185,24 +193,36 @@
         carried_ref[i] = carried[i].astype(BF)
         inverse_ref[i] = inverses[i].astype(BF)
         att = dot(probs.astype(BF), v[i])
-        att_ref[:, 128 * i : 128 * (i + 1)] = att.astype(BF)
+        attended.append(att.astype(BF))
         att_t_ref[128 * i : 128 * (i + 1), :] = att.T.astype(BF)
+    att = jnp.concatenate(attended, axis=1)
+    half = out_lo_ref.shape[1]
+    hidden_ref[:, :half] += dot(att, out_lo_ref[...])
+    hidden_ref[:, half:] += dot(att, out_hi_ref[...])
+
+    @pl.when(at == pl.num_programs(0) - 1)
+    def _():
+        value = hidden_ref[...]
+        scale = lax.rsqrt(jnp.mean(value * value, axis=1, keepdims=True) + EPSILON)
+        gain = gain_row(misc_ref, 13)
+        gain_ref[...] = gain
+        second_ref[...] = (value * scale * gain).astype(BF)
 
 
 def attention_forward(tokens, length, attn):
     count, width = tokens.shape
-    steps = width // 256
+    steps = width // SPAN
     cell = (PER_STEP, count, count)
     whole = lambda i, *_: (0, 0)
     column = lambda i, *_: (0, i)
     weight = lambda half, first: pl.BlockSpec(
-        (width, 256), lambda i, *_: (half, first + i)
-    )
-    row_block = pl.BlockSpec((count, 256), column)
+        (width, SPAN), lambda i, *_: (half, first // SPAN + i)
+    )
+    row_block = pl.BlockSpec((count, SPAN), column)
     cell_block = pl.BlockSpec(cell, lambda i, *_: (i, 0, 0))
     rows = jax.ShapeDtypeStruct((count, width), BF)
     turned = jax.ShapeDtypeStruct((width, count), BF)
-    cells = (2 * steps, count, count)
+    cells = (width // 128, count, count)
     return pl.pallas_call(
         attention_forward_kernel,
         grid_spec=pltpu.PrefetchScalarGridSpec(
@@ -210,10 +230,12 @@
             grid=(steps,),
             in_specs=[
                 pl.BlockSpec((count, width), whole),
-                weight(0, 20),
-                weight(0, 26),
-                weight(1, 20),
-                weight(1, 26),
+                weight(0, FIRST_AT),
+                weight(0, SECOND_AT),
+                weight(1, FIRST_AT),
+                weight(1, SECOND_AT),
+                pl.BlockSpec((SPAN, width // 2), lambda i, *_: (i, 0)),
+                pl.BlockSpec((SPAN, width // 2), lambda i, *_: (steps + i, 0)),
                 pl.BlockSpec((width, 128), lambda i, *_: (0, 6)),
             ],
             out_specs=[
@@ -222,12 +244,14 @@
                 row_block,
                 row_block,
                 row_block,
-                row_block,
-                pl.BlockSpec((256, count), lambda i, *_: (i, 0)),
+                pl.BlockSpec((count, width), whole),
+                pl.BlockSpec((count, width), whole),
+                pl.BlockSpec((SPAN, count), lambda i, *_: (i, 0)),
                 cell_block,
                 cell_block,
                 cell_block,
                 pl.BlockSpec((count, 128), whole),
+                pl.BlockSpec((1, width), whole),
             ],
             scratch_shapes=[pltpu.VMEM((count, width), BF)],
         ),
@@ -237,177 +261,137 @@
             rows,
             rows,
             rows,
+            jax.ShapeDtypeStruct((count, width), F32),
             rows,
             turned,
             jax.ShapeDtypeStruct(cells, F32),
             jax.ShapeDtypeStruct(cells, BF),
             jax.ShapeDtypeStruct(cells, BF),
             jax.ShapeDtypeStruct((count, 128), F32),
+            jax.ShapeDtypeStruct((1, width), F32),
         ],
-        compiler_params=pltpu.CompilerParams(vmem_limit_bytes=32 * MIB),
+        compiler_params=pltpu.CompilerParams(vmem_limit_bytes=58 * MIB),
         cost_estimate=pl.CostEstimate(
             flops=8 * count * width * width + 12 * 60 * 2 * 128**3,
             bytes_accessed=10 * width * width,
             transcendentals=0,
         ),
         name="attention_forward",
-    )(length, tokens, attn, attn, attn, attn, attn)
+    )(length, tokens, attn, attn, attn, attn, attn, attn, attn)
 
 
 FF_BLOCK = 512
 
 
 def feedforward_kernel(
-    length_ref,
     core_ref,
-    tokens_ref,
-    att_ref,
-    out_lo_ref,
-    out_hi_ref,
-    misc_ref,
-    cot_ref,
+    second_own_ref,
+    second_other_ref,
     cot_own_ref,
     cot_other_ref,
     wg_ref,
     wu_ref,
-    down_own_ref,
-    down_other_ref,
+    wd_ref,
     second_t_ref,
     product_t_ref,
-    acts_ref,
-    mixed_ref,
-    hidden_grad_ref,
-    branch_ref,
-    gain_grad_ref,
-    hidden,
-    feed,
-    second_grad,
-    second_ref,
+    gate_low_ref,
+    up_low_ref,
+    feed_own_ref,
+    feed_other_ref,
+    grad_own_ref,
+    grad_other_ref,
+    second,
+    cot,
 ):
-    at = pl.program_id(0)
-    half = out_lo_ref.shape[1]
-
-    @pl.when(at == 0)
+    count = second_own_ref.shape[0]
+
+    @pl.when(pl.program_id(0) == 0)
     def _():
-        att = att_ref[...]
-        hidden[:, :half] = tokens_ref[:, :half].astype(F32) + dot(att, out_lo_ref[...])
-        hidden[:, half:] = tokens_ref[:, half:].astype(F32) + dot(att, out_hi_ref[...])
-        value = hidden[...]
-        scale = lax.rsqrt(jnp.mean(value * value, axis=1, keepdims=True) + EPSILON)
-        value = value * scale * gain_row(misc_ref, 13)
-        second_ref[...] = value.astype(BF)
-        second_t_ref[...] = value.T.astype(BF)
-        feed[...] = jnp.zeros_like(feed)
-        second_grad[...] = jnp.zeros_like(second_grad)
-
-    second = second_ref[...]
-    gate = dot(second, wg_ref[...])
-    upward = dot(second, wu_ref[...])
+        second[:count] = second_own_ref[...]
+        second[count:] = second_other_ref[...]
+        cot[:count] = cot_own_ref[...]
+        cot[count:] = cot_other_ref[...]
+        second_t_ref[:, :count] = second_own_ref[...].astype(F32).T.astype(BF)
+        second_t_ref[:, count:] = second_other_ref[...].astype(F32).T.astype(BF)
+        feed_own_ref[...] = jnp.zeros_like(feed_own_ref)
+        feed_other_ref[...] = jnp.zeros_like(feed_other_ref)
+        grad_own_ref[...] = jnp.zeros_like(grad_own_ref)
+        grad_other_ref[...] = jnp.zeros_like(grad_other_ref)
+
+    gate = dot(second[...], wg_ref[...])
+    upward = dot(second[...], wu_ref[...])
     sigma = jax.nn.sigmoid(gate)
     silu = gate * sigma
     product = silu * upward
     product_t_ref[...] = product.T.astype(BF)
-    product = product.astype(BF)
-    product_grad = dot_nt(cot_own_ref[...], down_own_ref[...]) + dot_nt(
-        cot_other_ref[...], down_other_ref[...]
-    )
+    product_grad = dot_nt(cot[...], wd_ref[...])
     gate_low = (product_grad * upward * (sigma * (1.0 + gate * (1.0 - sigma)))).astype(BF)
     up_low = (product_grad * silu).astype(BF)
-    acts_ref[0] = gate_low
-    acts_ref[1] = up_low
-    feed[0] += dot(product, down_own_ref[...])
-    feed[1] += dot(product, down_other_ref[...])
-    second_grad[...] += dot_nt(gate_low, wg_ref[...]) + dot_nt(up_low, wu_ref[...])
-
-    @pl.when(at == pl.num_programs(0) - 1)
-    def _():
-        value = hidden[...]
-        valid = lax.broadcasted_iota(jnp.int32, value.shape, 0) < length_ref[0]
-        fed = jnp.concatenate([feed[core_ref[0]], feed[1 - core_ref[0]]], axis=1)
-        mixed_ref[...] = jnp.where(valid, value + fed, 0.0).astype(BF)
-        scale = lax.rsqrt(jnp.mean(value * value, axis=1, keepdims=True) + EPSILON)
-        grad = second_grad[...]
-        scaled = grad * gain_row(misc_ref, 13)
-        along = jnp.mean(scaled * value, axis=1, keepdims=True)
-        hidden_grad = (
-            cot_ref[...].astype(F32) + scale * scaled - value * (scale * scale * scale * along)
-        )
-        hidden_grad_ref[...] = hidden_grad
-        branch_ref[...] = hidden_grad.astype(BF)
-        gain_grad_ref[...] = jnp.sum(grad * value * scale, axis=0, keepdims=True)
-
-
-def feedforward(tokens, length, core, att, cots, attn, downs):
-    count, width = tokens.shape
-    hidden_units = downs[0].shape[0]
-    steps = hidden_units // FF_BLOCK
-    half = width // 2
-    whole = lambda i, *_: (0, 0)
+    gate_low_ref[...] = gate_low
+    up_low_ref[...] = up_low
+    feed = dot(product.astype(BF), wd_ref[...])
+    feed_own_ref[...] += feed[:count]
+    feed_other_ref[...] += feed[count:]
+    grad = dot_nt(gate_low, wg_ref[...]) + dot_nt(up_low, wu_ref[...])
+    grad_own_ref[...] += grad[:count]
+    grad_other_ref[...] += grad[count:]
+
+
+def feedforward(core, seconds, cots, attn, w_down):
+    count, width = seconds[0].shape
+    units = w_down.shape[0]
+    whole = lambda i, _: (0, 0)
     rows = pl.BlockSpec((count, width), whole)
-    weight = lambda side: pl.BlockSpec(
-        (width, FF_BLOCK), lambda i, *_: (side, 1024 // FF_BLOCK + i)
-    )
-    down_block = pl.BlockSpec((FF_BLOCK, half), lambda i, *_: (i, 0))
+    columns = pl.BlockSpec((2 * count, FF_BLOCK), lambda i, _: (0, i))
+    turned = pl.BlockSpec((FF_BLOCK, 2 * count), lambda i, _: (i, 0))
+    weight = lambda first: pl.BlockSpec(
+        (width, FF_BLOCK), lambda i, c: (c[0], first // FF_BLOCK + i)
+    )
+    sums = jax.ShapeDtypeStruct((count, width), F32)
+    acts = jax.ShapeDtypeStruct((2 * count, units), BF)
     return pl.pallas_call(
         feedforward_kernel,
         grid_spec=pltpu.PrefetchScalarGridSpec(
-            num_scalar_prefetch=2,
-            grid=(steps,),
-            in_specs=[
-                rows,
-                rows,
-                pl.BlockSpec((width, half), whole),
-                pl.BlockSpec((width, half), lambda i, *_: (1, 0)),
-                pl.BlockSpec((width, 128), lambda i, *_: (0, 6)),
-                rows,
-                pl.BlockSpec((count, half), whole),
-                pl.BlockSpec((count, half), whole),
-                weight(0),
-                weight(1),
-                down_block,
-                down_block,
+            num_scalar_prefetch=1,
+            grid=(units // FF_BLOCK,),
+            in_specs=[rows] * 4
+            + [
+                weight(GATE_AT),
+                weight(UP_AT),
+                pl.BlockSpec((FF_BLOCK, width), lambda i, _: (i, 0)),
             ],
-            out_specs=[
-                pl.BlockSpec((width, count), whole),
-                pl.BlockSpec((FF_BLOCK, count), lambda i, *_: (i, 0)),
-                pl.BlockSpec((2, count, FF_BLOCK), lambda i, *_: (0, 0, i)),
-                rows,
-                rows,
-                rows,
-                pl.BlockSpec((1, width), whole),
-            ],
-            scratch_shapes=[
-                pltpu.VMEM((count, width), F32),
-                pltpu.VMEM((2, count, half), F32),
-                pltpu.VMEM((count, width), F32),
-                pltpu.VMEM((count, width), BF),
-            ],
+            out_specs=[pl.BlockSpec((width, 2 * count), whole), turned, columns, columns]
+            + [rows] * 4,
+            scratch_shapes=[pltpu.VMEM((2 * count, width), BF)] * 2,
         ),
         out_shape=[
-            jax.ShapeDtypeStruct((width, count), BF),
-            jax.ShapeDtypeStruct((hidden_units, count), BF),
-            jax.ShapeDtypeStruct((2, count, hidden_units), BF),
-            jax.ShapeDtypeStruct((count, width), BF),
-            jax.ShapeDtypeStruct((count, width), F32),
-            jax.ShapeDtypeStruct((count, width), BF),
-            jax.ShapeDtypeStruct((1, width), F32),
+            jax.ShapeDtypeStruct((width, 2 * count), BF),
+            jax.ShapeDtypeStruct((units, 2 * count), BF),
+            acts,
+            acts,
+            sums,
+            sums,
+            sums,
+            sums,
         ],
-        compiler_params=pltpu.CompilerParams(vmem_limit_bytes=48 * MIB),
+        compiler_params=pltpu.CompilerParams(vmem_limit_bytes=58 * MIB),
         cost_estimate=pl.CostEstimate(
-            flops=12 * count * width * hidden_units,
-            bytes_accessed=6 * width * hidden_units,
+            flops=24 * count * width * units,
+            bytes_accessed=6 * width * units,
             transcendentals=0,
         ),
         name="feedforward",
-    )(length, core, tokens, att, attn, attn, attn, *cots, attn, attn, *downs)
+    )(core, *seconds, *cots, attn, attn, w_down)
 
 
 def attention_backward_kernel(
     tokens_ref,
     normed_t_ref,
-    branch_ref,
-    hidden_grad_ref,
-    ffn_gain_ref,
+    gain_ref,
+    hidden_ref,
+    cot_ref,
+    grad_own_ref,
+    grad_got_ref,
     beta_ref,
     q_ref,
     k_ref,
@@ -424,10 +408,13 @@
     wh_ref,
     misc_ref,
     grads_ref,
+    branch_ref,
     grad_tokens_ref,
     misc_grad_ref,
     normed_grad,
     beta_grad,
+    hidden_grad_ref,
+    ffn_gain_ref,
 ):
     at = pl.program_id(0)
     half = wo_lo_ref.shape[1]
@@ -436,6 +423,17 @@
     def _():
         normed_grad[...] = jnp.zeros_like(normed_grad)
         beta_grad[...] = jnp.zeros_like(beta_grad)
+        value = hidden_ref[...]
+        scale = lax.rsqrt(jnp.mean(value * value, axis=1, keepdims=True) + EPSILON)
+        grad = grad_own_ref[...] + grad_got_ref[...]
+        scaled = grad * gain_ref[...]
+        along = jnp.mean(scaled * value, axis=1, keepdims=True)
+        hidden_grad = (
+            cot_ref[...].astype(F32) + scale * scaled - value * (scale * scale * scale * along)
+        )
+        hidden_grad_ref[...] = hidden_grad
+        branch_ref[...] = hidden_grad.astype(BF)
+        ffn_gain_ref[...] = jnp.sum(grad * value * scale, axis=0, keepdims=True)
 
     att_grad_all = (
         dot_nt(branch_ref[:, :half], wo_lo_ref[...]) + dot_nt(branch_ref[:, half:], wo_hi_ref[...])
@@ -550,26 +548,28 @@
         misc_grad_ref[...] = misc_grad.astype(BF)
 
 
-def attention_backward(tokens, normed_t, branch, hidden_grad, ffn_gain, saved, attn):
+def attention_backward(tokens, normed_t, norm, saved, attn):
     q, k, v, h, probs, carried, inverse, beta = saved
     count, width = tokens.shape
-    steps = width // 256
+    steps = width // SPAN
     half = width // 2
     whole = lambda i: (0, 0)
     rows = pl.BlockSpec((count, width), whole)
-    row_block = pl.BlockSpec((count, 256), lambda i: (0, i))
+    row_block = pl.BlockSpec((count, SPAN), lambda i: (0, i))
     cell_block = pl.BlockSpec((PER_STEP, count, count), lambda i: (i, 0, 0))
-    weight = lambda side, first: pl.BlockSpec((width, 256), lambda i: (side, first + i))
-    out_rows = lambda side: pl.BlockSpec((256, half), lambda i: (side * steps + i, 0))
+    weight = lambda side, first: pl.BlockSpec((width, SPAN), lambda i: (side, first // SPAN + i))
+    out_rows = lambda side: pl.BlockSpec((SPAN, half), lambda i: (side * steps + i, 0))
     return pl.pallas_call(
         attention_backward_kernel,
         grid=(steps,),
         in_specs=[
             rows,
             pl.BlockSpec((width, count), whole),
+            pl.BlockSpec((1, width), whole),
             rows,
             rows,
-            pl.BlockSpec((1, width), whole),
+            rows,
+            rows,
             pl.BlockSpec((count, 128), whole),
             row_block,
             row_block,
@@ -580,32 +580,37 @@
             cell_block,
             out_rows(0),
             out_rows(1),
-            weight(0, 20),
-            weight(0, 26),
-            weight(1, 20),
-            weight(1, 26),
+            weight(0, FIRST_AT),
+            weight(0, SECOND_AT),
+            weight(1, FIRST_AT),
+            weight(1, SECOND_AT),
             pl.BlockSpec((width, 128), lambda i: (0, 6)),
         ],
         out_specs=[
-            pl.BlockSpec((4, count, 256), lambda i: (0, 0, i)),
+            pl.BlockSpec((4, count, SPAN), lambda i: (0, 0, i)),
+            rows,
             rows,
             pl.BlockSpec((width, 128), whole),
         ],
         out_shape=[
             jax.ShapeDtypeStruct((4, count, width), BF),
+            jax.ShapeDtypeStruct((count, width), BF),
             jax.ShapeDtypeStruct((count, width), F32),
             jax.ShapeDtypeStruct((width, 128), BF),
         ],
-        scratch_shapes=[pltpu.VMEM((count, width), F32), pltpu.VMEM((count, 128), F32)],
-        compiler_params=pltpu.CompilerParams(vmem_limit_bytes=40 * MIB),
+        scratch_shapes=[
+            pltpu.VMEM((count, width), F32),
+            pltpu.VMEM((count, 128), F32),
+            pltpu.VMEM((count, width), F32),
+            pltpu.VMEM((1, width), F32),
+        ],
+        compiler_params=pltpu.CompilerParams(vmem_limit_bytes=58 * MIB),
         cost_estimate=SHORT,
         name="attention_backward",
     )(
         tokens,
         normed_t,
-        branch,
-        hidden_grad,
-        ffn_gain,
+        *norm,
         beta,
         q,
         k,
@@ -624,15 +629,11 @@
     )
 
 
-def weight_gradient_kernel(segments, n_x, n_y, has_misc, second_half, *refs):
-    place_ref, refs = refs[0], refs[2:]
-    xs = [(refs[2 * i], refs[2 * i + 1]) for i in range(n_x)]
-    refs = refs[2 * n_x :]
-    ys = [(refs[2 * i], refs[2 * i + 1]) for i in range(n_y)]
-    refs = refs[2 * n_y :]
-    misc_ref = None
-    if has_misc:
-        misc_ref, refs = refs[0], refs[1:]
+def weight_gradient_kernel(segments, x_counts, y_counts, has_misc, second_half, *refs):
+    place_ref, refs = refs[0], list(refs[2:])
+    xs = [[refs.pop(0) for _ in range(n)] for n in x_counts]
+    ys = [[refs.pop(0) for _ in range(n)] for n in y_counts]
+    misc_ref = refs.pop(0) if has_misc else None
     at = pl.program_id(0)
     chips, height = xs[0][0].shape[0], xs[0][0].shape[1]
     if second_half:
@@ -643,19 +644,18 @@
         spots += [(send, got_hi, i, chips // 4 + 4 * at + i) for i in range(4)]
     owners = [place_ref[spot[3]] for spot in spots]
     lefts = []
-    for mine, other in xs:
+    for pieces in xs:
         rows = [
-            jnp.concatenate([mine[owner].astype(F32), other[owner].astype(F32)], axis=1)
+            jnp.concatenate([piece[owner].astype(F32) for piece in pieces], axis=1)
             for owner in owners
         ]
         lefts.append(jnp.concatenate(rows, axis=0).astype(BF))
     done = 0
     for x_at, y_at, matrix, start, size in segments:
-        mine, other = ys[y_at]
         columns = slice(start, start + size)
         part = dot(
             lefts[x_at],
-            jnp.concatenate([mine[matrix, :, columns], other[matrix, :, columns]], axis=0),
+            jnp.concatenate([piece[matrix, :, columns] for piece in ys[y_at]], axis=0),
         )
         for index, (out, got, i, _) in enumerate(spots):
             value = part[index * height : (index + 1) * height]
@@ -672,16 +672,20 @@
 
 
 def weight_gradient(places, core, xs, ys, segments, misc=None, got=None):
-    chips, height, count = xs[0][0].shape
+    chips, height = xs[0][0].shape[:2]
     columns = sum(segment[4] for segment in segments) + (128 if misc is not None else 0)
     operands, in_specs = [], []
-    for mine, other in xs:
-        operands += [mine, other]
-        in_specs += [pl.BlockSpec(mine.shape, lambda i, *_: (0, 0, 0))] * 2
-    for mine, other in ys:
-        operands += [mine, other]
-        half = (mine.shape[0], mine.shape[1], mine.shape[2] // 2)
-        in_specs += [pl.BlockSpec(half, lambda i, _, c: (0, 0, c[0]))] * 2
+    for pieces in xs:
+        operands += pieces
+        in_specs += [pl.BlockSpec(p.shape, lambda i, *_: (0, 0, 0)) for p in pieces]
+    for pieces in ys:
+        operands += pieces
+        shape = pieces[0].shape
+        if len(pieces) == 2:
+            half = (shape[0], shape[1], shape[2] // 2)
+            in_specs += [pl.BlockSpec(half, lambda i, _, c: (0, 0, c[0]))] * 2
+        else:
+            in_specs.append(pl.BlockSpec(shape, lambda i, *_: (0, 0, 0)))
     if misc is not None:
         operands.append(misc)
         in_specs.append(pl.BlockSpec(misc.shape, lambda i, *_: (0, 0, 0)))
@@ -698,9 +702,10 @@
         ]
         out_specs = [pl.BlockSpec(block, lambda i, *_: (i, 0, 0))] * 2
         out_shape = [jax.ShapeDtypeStruct((chips // 4, height, columns), BF)] * 2
+    x_counts, y_counts = [len(p) for p in xs], [len(p) for p in ys]
     return pl.pallas_call(
         functools.partial(
-            weight_gradient_kernel, segments, len(xs), len(ys), misc is not None, got is None
+            weight_gradient_kernel, segments, x_counts, y_counts, misc is not None, got is None
         ),
         grid_spec=pltpu.PrefetchScalarGridSpec(
             num_scalar_prefetch=2, grid=(steps,), in_specs=in_specs, out_specs=out_specs
@@ -712,6 +717,19 @@
     )(places, core, *operands)
 
 
+def fold(value):
+    part = value.shape[2] // 4
+    last = value[:, :, 3 * part :]
+    below = jnp.concatenate([last[:, 8 * i : 8 * (i + 1)] for i in range(3)], axis=2)
+    return jnp.concatenate([value[:, :, : 3 * part], below], axis=1)
+
+
+def unfold(value):
+    part = value.shape[1] // 3
+    last = [value[24:, part * i : part * (i + 1)] for i in range(3)]
+    return jnp.concatenate([value[:24], jnp.concatenate(last, axis=0)], axis=1)
+
+
 def add_kernel(widths, *refs):
     total = sum(len(group) for group in widths)
     ins, outs = refs[: 4 * total], refs[4 * total :]
@@ -720,9 +738,15 @@
         start = 0
         for width in group:
             keep_lo, keep_hi, got_lo, got_hi = ins[4 * at : 4 * at + 4]
+            low = keep_lo[...].astype(F32) + got_lo[...].astype(F32)
+            high = keep_hi[...].astype(F32) + got_hi[...].astype(F32)
+            if low.shape[1] != outs[2 * index].shape[1]:
+                pad = jnp.zeros((*low.shape[:2], 4 * width // 3 - low.shape[2]), F32)
+                low = fold(jnp.concatenate([low, pad], axis=2))
+                high = fold(jnp.concatenate([high, pad], axis=2))
             columns = slice(start, start + width)
-            outs[2 * index][:, :, columns] = keep_lo[...] + got_lo[...]
-            outs[2 * index + 1][:, :, columns] = keep_hi[...] + got_hi[...]
+            outs[2 * index][:, :, columns] = low.astype(BF)
+            outs[2 * index + 1][:, :, columns] = high.astype(BF)
             start += width
             at += 1
 
@@ -739,8 +763,14 @@
             high = pl.BlockSpec(shape, lambda i: (i + grid, 0, 0))
             operands += [keep, keep, got, got]
             in_specs += [low, high, low, high]
-        widths.append([keep.shape[2] for keep, _ in group])
-        shape = (block, group[0][0].shape[1], sum(widths[-1]))
+        height = group[0][0].shape[1]
+        widths.append(
+            [
+                keep.shape[2] if keep.shape[1] == height else -(-keep.shape[2] // 512) * 384
+                for keep, _ in group
+            ]
+        )
+        shape = (block, height, sum(widths[-1]))
         out_specs += [pl.BlockSpec(shape, lambda i: (i, 0, 0))] * 2
         shapes += [jax.ShapeDtypeStruct((rows,) + shape[1:], BF)] * 2
     outs = pl.pallas_call(
@@ -758,27 +788,28 @@
 
 def last_add_kernel(core_ref, *refs):
     first = core_ref[0] == 0
-    *ins, mine, theirs, mine_down, theirs_down = refs
+    *ins, mine, theirs, down = refs
+    values = [
+        ins[index][0].astype(F32) + ins[index + 1][0].astype(F32)
+        for index in range(0, len(ins), 2)
+    ]
+    width = down.shape[1]
+    down[...] = values[2][:, :width]
+    values[2] = unfold(values[2][:, width:])
     start = 0
-    for index in range(0, len(ins), 2):
-        value = ins[index][0].astype(F32) + ins[index + 1][0].astype(F32)
-        height, width = value.shape
-        low, high = value[: height // 2], value[height // 2 :]
-        own, other = jnp.where(first, low, high), jnp.where(first, high, low)
-        if height == 24:
-            mine[:, start : start + width] = own
-            theirs[:, start : start + width] = other.astype(BF)
-            start += width
-        else:
-            mine_down[...] = own
-            theirs_down[...] = other.astype(BF)
-
-
-def last_add(core, pairs):
+    for value in values:
+        low, high = value[:12], value[12:]
+        columns = slice(start, start + value.shape[1])
+        mine[:, columns] = jnp.where(first, low, high)
+        theirs[:, columns] = jnp.where(first, high, low).astype(BF)
+        start += value.shape[1]
+
+
+def last_add(core, pairs, down_shape):
     flat = [value for pair in pairs for value in pair]
-    width = sum(keep.shape[2] for keep, _ in pairs if keep.shape[1] == 24)
-    down = next(keep for keep, _ in pairs if keep.shape[1] != 24)
-    shapes = [(12, width), (12, width)] + [(down.shape[1] // 2, down.shape[2])] * 2
+    folded = pairs[2][0].shape[2] - down_shape[1]
+    width = pairs[0][0].shape[2] + pairs[1][0].shape[2] + folded // 3 * 4
+    shapes = [(12, width), (12, width), down_shape]
     return pl.pallas_call(
         last_add_kernel,
         grid_spec=pltpu.PrefetchScalarGridSpec(
@@ -787,7 +818,7 @@
             in_specs=[pl.BlockSpec(v.shape, lambda i, _: (0, 0, 0)) for v in flat],
             out_specs=[pl.BlockSpec(shape, lambda i, _: (0, 0)) for shape in shapes],
         ),
-        out_shape=[jax.ShapeDtypeStruct(s, t) for s, t in zip(shapes, (F32, BF, F32, BF))],
+        out_shape=[jax.ShapeDtypeStruct(s, t) for s, t in zip(shapes, (F32, BF, F32))],
         compiler_params=pltpu.CompilerParams(vmem_limit_bytes=16 * MIB),
         cost_estimate=SHORT,
         name="last_add",
@@ -800,12 +831,18 @@
     ((5632, 768),),
     ((6400, 256), (6656, 512)),
     ((7168, 768),),
-    ((0, 2048),),
-    ((3328, 2048),),
 )
-
-
-def finish_kernel(core_ref, mine, other, mine_down, other_down, *outs):
+HIDDEN_PLACES = (0, 3328)
+TILE = 256
+
+
+def deal(parity):
+    row = lax.broadcasted_iota(jnp.int32, (TILE // 2, TILE), 0)
+    col = lax.broadcasted_iota(jnp.int32, (TILE // 2, TILE), 1)
+    return (col == 64 * (row // 32) + 32 * parity + row % 32).astype(F32).astype(BF)
+
+
+def finish_kernel(core_ref, mine, other, *outs):
     first = core_ref[0] == 0
     for pieces, out in zip(PLACES, outs):
         half = out.shape[1] // 2
@@ -816,18 +853,41 @@
             out[:, done : done + width] = jnp.where(first, a, b)
             out[:, half + done : half + done + width] = jnp.where(first, b, a)
             done += width
-    a, b = mine_down[...], other_down[...].astype(F32)
-    half = a.shape[1]
-    outs[7][:, :half] = jnp.where(first, a, b)
-    outs[7][:, half:] = jnp.where(first, b, a)
-    outs[8][...] = mine[:, 7936:] + other[:, 7936:].astype(F32)
-
-
-def finish(core, mine, other, mine_down, other_down):
-    rows, down_rows = mine.shape[0], mine_down.shape[0]
+    own, their = deal(core_ref[0]), deal(1 - core_ref[0])
+    rows = mine.shape[0]
+    pad = jnp.zeros((16 - rows, TILE // 2), F32)
+    for start, out in zip(HIDDEN_PLACES, outs[5:7]):
+        tiles = out.shape[1] // TILE
+        stack = lambda ref: jnp.concatenate(
+            [
+                jnp.concatenate(
+                    [ref[:, start + 128 * t : start + 128 * (t + 1)].astype(F32), pad], axis=0
+                )
+                for t in range(tiles)
+            ],
+            axis=0,
+        )
+        high, low = two_parts(stack(mine))
+        value = dot(high, own) + dot(low, own) + dot(stack(other).astype(BF), their)
+        for t in range(tiles):
+            out[:, TILE * t : TILE * (t + 1)] = value[16 * t : 16 * t + rows]
+    misc = mine[:, 7936:8064] + other[:, 7936:8064].astype(F32)
+    heads = outs[7].shape[1]
+    outs[7][...] = misc[:, :heads]
+    row = lax.broadcasted_iota(jnp.int32, (rows, 128), 0)
+    col = lax.broadcasted_iota(jnp.int32, (rows, 128), 1)
+    eye = (row == col).astype(F32).astype(BF)
+    high, low = two_parts(misc)
+    turned = dot_tn(high, eye) + dot_tn(low, eye)
+    outs[8][...] = turned[heads : heads + 1, :rows]
+    outs[9][...] = turned[heads + 1 : heads + 2, :rows]
+
+
+def finish(core, mine, other, hidden_units, heads):
+    rows = mine.shape[0]
     shapes = [(rows, 2 * sum(w for _, w in pieces)) for pieces in PLACES]
-    shapes += [(down_rows, 2 * mine_down.shape[1]), (rows, 128)]
-    operands = (mine, other, mine_down, other_down)
+    shapes += [(rows, hidden_units), (rows, hidden_units), (rows, heads), (1, rows), (1, rows)]
+    operands = (mine, other)
     return pl.pallas_call(
         finish_kernel,
         grid_spec=pltpu.PrefetchScalarGridSpec(
@@ -843,6 +903,73 @@
     )(core, *operands)
 
 
+def pack_kernel(core_ref, gain_attn, gain_ffn, *refs):
+    w_out, w_query, w_key, w_value, w_house, w_beta, w_gate, w_up = refs[:8]
+    mine, theirs = refs[8:]
+    first = core_ref[0] == 0
+    rows, width = w_out.shape
+    half, units = width // 2, w_gate.shape[1]
+    gains = jnp.concatenate(
+        [gain_attn[...].astype(F32), gain_ffn[...].astype(F32), jnp.zeros((6, rows), F32)], axis=0
+    )
+    place = lax.broadcasted_iota(jnp.int32, (8, 256), 0)
+    lane = lax.broadcasted_iota(jnp.int32, (8, 256), 1)
+    pick = ((place < 2) & (lane == 12 + place)).astype(F32)
+    misc = dot_tn(gains.astype(BF), pick.astype(BF))
+    beta = w_beta[...].astype(F32)
+    misc += jnp.concatenate([beta, jnp.zeros((rows, 256 - beta.shape[1]), F32)], axis=1)
+    split = lambda a, b: (jnp.where(first, a, b), jnp.where(first, b, a))
+    pieces = [
+        split(w_out[:, :half], w_out[:, half:]),
+        (misc.astype(BF), misc.astype(BF)),
+        split(w_query[...], w_value[...]),
+        split(w_key[...], w_house[...]),
+    ]
+    for start, (own, other) in zip((0, half, FIRST_AT, SECOND_AT), pieces):
+        size = own.shape[1]
+        mine[:, start : start + size] = own
+        theirs[:, start : start + size] = other
+    pad = jnp.zeros((16 - rows, TILE), F32)
+    row = lax.broadcasted_iota(jnp.int32, (TILE, TILE), 0)
+    col = lax.broadcasted_iota(jnp.int32, (TILE, TILE), 1)
+    parity = jnp.where(col < 128, core_ref[0], 1 - core_ref[0])
+    at = col % 128
+    pick = (row == 64 * (at // 32) + 32 * parity + at % 32).astype(F32).astype(BF)
+    tiles = units // TILE
+    for start, ref in ((GATE_AT, w_gate), (UP_AT, w_up)):
+        stack = jnp.concatenate(
+            [
+                jnp.concatenate([ref[:, TILE * t : TILE * (t + 1)].astype(F32), pad], axis=0)
+                for t in range(tiles)
+            ],
+            axis=0,
+        ).astype(BF)
+        value = dot(stack, pick)
+        for t in range(tiles):
+            part = value[16 * t : 16 * t + rows].astype(BF)
+            mine[:, start + 128 * t : start + 128 * (t + 1)] = part[:, :128]
+            theirs[:, start + 128 * t : start + 128 * (t + 1)] = part[:, 128:]
+
+
+def pack(core, gains, weights):
+    rows, width = weights[0].shape
+    shapes = [(rows, SECOND_AT + width)] * 2
+    operands = [gain[None, :] for gain in gains] + list(weights)
+    return pl.pallas_call(
+        pack_kernel,
+        grid_spec=pltpu.PrefetchScalarGridSpec(
+            num_scalar_prefetch=1,
+            grid=(1,),
+            in_specs=[pl.BlockSpec(v.shape, lambda i, _: (0, 0)) for v in operands],
+            out_specs=[pl.BlockSpec(shape, lambda i, _: (0, 0)) for shape in shapes],
+        ),
+        out_shape=[jax.ShapeDtypeStruct(shape, BF) for shape in shapes],
+        compiler_params=pltpu.CompilerParams(vmem_limit_bytes=58 * MIB),
+        cost_estimate=SHORT,
+        name="pack",
+    )(core, *operands)
+
+
 def send_step(value, stream, step):
     count = lax.axis_size("fsdp")
     pairs = [(d, d ^ (2 * MASKS[stream][d & 1][step])) for d in range(count)]
@@ -855,8 +982,8 @@
     return jax.tree.unflatten(tree, kept[: len(flat)])
 
 
-def exchange(sends, step, streams=(0, 1, 2)):
-    return [send_step(send, stream, step) for stream, send in zip(streams, sends)]
+def exchange(sends, step):
+    return [send_step(send, stream, step) for stream, send in enumerate(sends)]
 
 
 def blocks(turned, height):
@@ -864,36 +991,39 @@
 
 
 def gather_streams(parts):
-    for step in range(5, -1, -1):
-        gots = [send_step(part, stream, step) for stream, part in enumerate(parts)]
+    for step in range(5, 0, -1):
+        gots = exchange(parts, step)
         parts = [jnp.concatenate(pair, axis=0) for pair in zip(parts, gots)]
-    return parts
+    return parts, exchange(parts, 0)
 
 
 def in_order_kernel(place_ref, *refs):
-    streams, out = refs[:-1], refs[-1]
-    width = streams[0].shape[2]
-    for index, stream in enumerate(streams):
-        for place in range(stream.shape[0]):
-            out[place_ref[index, place], :, index * width : (index + 1) * width] = stream[place]
-
-
-def in_order(places, streams):
-    chips, height, width = streams[0].shape
-    shape = (chips, height, width * len(streams))
-    return pl.pallas_call(
+    lows, highs, out = refs[:3], refs[3:6], refs[6]
+    half, _, width = lows[0].shape
+    for stream, (low, high) in enumerate(zip(lows, highs)):
+        columns = slice(width * stream, width * (stream + 1))
+        for place in range(half):
+            out[place_ref[stream, place], :, columns] = low[place]
+            out[place_ref[stream, half + place], :, columns] = high[place]
+
+
+def in_order(places, lows, highs):
+    half, height, width = lows[0].shape
+    shape = (2 * half, height, 3 * width)
+    out = pl.pallas_call(
         in_order_kernel,
         grid_spec=pltpu.PrefetchScalarGridSpec(
             num_scalar_prefetch=1,
             grid=(1,),
-            in_specs=[pl.BlockSpec(s.shape, lambda i, _: (0, 0, 0)) for s in streams],
+            in_specs=[pl.BlockSpec(lows[0].shape, lambda i, _: (0, 0, 0))] * 6,
             out_specs=pl.BlockSpec(shape, lambda i, _: (0, 0, 0)),
         ),
         out_shape=jax.ShapeDtypeStruct(shape, BF),
-        compiler_params=pltpu.CompilerParams(vmem_limit_bytes=40 * MIB),
+        compiler_params=pltpu.CompilerParams(vmem_limit_bytes=58 * MIB),
         cost_estimate=SHORT,
         name="in_order",
-    )(places, *streams)
+    )(places, *lows, *highs)
+    return out.reshape(2 * half * height, 3 * width)
 
 
 def body(
@@ -923,77 +1053,59 @@
     places = jnp.where(core == 0, offsets[0], offsets[1]) ^ chip
     core_at = core.astype(jnp.int32)[None]
 
-    misc = jnp.concatenate(
-        [
-            w_beta,
-            gain_attn[:, None],
-            gain_ffn[:, None],
-            jnp.zeros((w_beta.shape[0], 256 - heads - 2), BF),
-        ],
-        axis=1,
-    )
-    pack_a = jnp.concatenate([w_out[:, :half], misc, w_gate, w_query, w_key], axis=1)
-    pack_b = jnp.concatenate([w_out[:, half:], misc, w_up, w_value, w_house], axis=1)
-    mine = jnp.where(core == 0, pack_a, pack_b)
-    theirs = swap(jnp.where(core == 0, pack_b, pack_a))
-    slab = jnp.where(
+    mine, theirs = pack(
+        core_at,
+        (gain_attn, gain_ffn),
+        (w_out, w_query, w_key, w_value, w_house, w_beta, w_gate, w_up),
+    )
+    stack = lambda own, other: jnp.where(
         core == 0,
-        jnp.concatenate([mine, theirs], axis=0),
-        jnp.concatenate([theirs, mine], axis=0),
-    )
-    mine = jnp.where(core == 0, w_down[:, :half], w_down[:, half:])
-    theirs = swap(jnp.where(core == 0, w_down[:, half:], w_down[:, :half]))
-    slab_down = jnp.where(
-        core == 0,
-        jnp.concatenate([mine, theirs], axis=0),
-        jnp.concatenate([theirs, mine], axis=0),
-    )
+        jnp.concatenate([own, other], axis=0),
+        jnp.concatenate([other, own], axis=0),
+    )
+    slab = stack(mine, swap(theirs))
     by_core = [[*range(0, devices, 2), *range(1, devices, 2)]]
     attn = lax.all_gather(slab, "fsdp", axis=0, tiled=True, axis_index_groups=by_core)
-    third = half // 3
-    streams = gather_streams([slab_down[None, :, third * i : third * (i + 1)] for i in range(3)])
-    down_own = in_order(places, streams).reshape(hidden_units, half)
-    downs = (down_own, swap(down_own))
+    part, third = hidden_units // 2, width // 3
+    lows, highs = gather_streams([w_down[None, :, third * s : third * (s + 1)] for s in range(3)])
+    full_down = in_order(places, lows, highs)
 
     flat = tokens.reshape(count, width)
     valid = lax.broadcasted_iota(jnp.int32, (count, 1), 0) < lengths[0]
     cot = jnp.where(valid, cotangent.reshape(count, width), jnp.zeros((), BF))
-    cot_other = swap(cot)
-
-    normed_t, q, k, v, h, att, att_t, probs, carried, inverse, beta = attention_forward(
-        flat, lengths, attn
+    cots = (cot, swap(cot))
+
+    normed_t, q, k, v, h, hidden, second, att_t, *cells, beta, gain = attention_forward(
+        after(flat, full_down), lengths, attn
     )
     normed_x, att_x = (
         (blocks(value, 24), blocks(swap(value), 24)) for value in (normed_t, att_t)
     )
-    cots = (
-        cot,
-        jnp.where(core == 0, cot[:, :half], cot[:, half:]),
-        jnp.where(core == 0, cot[:, half:], cot[:, :half]),
-    )
-    second_t, product_t, acts, mixed, hidden_grad, branch, ffn_gain = feedforward(
-        flat, lengths, core_at, att, cots, attn, downs
-    )
-    second_x = (blocks(second_t, 24), blocks(swap(second_t), 24))
-    product_x = (blocks(product_t, 64), blocks(swap(product_t), 64))
-    acts_y = (acts, swap(acts))
-    cot_y = (cot[None], cot_other[None])
+    second_t, product_t, gate_low, up_low, feed, feed_other, second_grad, grad_other = feedforward(
+        core_at, (second, swap(second)), cots, attn, full_down
+    )
+    grad_got = swap(grad_other)
+    mixed = jnp.where(valid, hidden + feed + swap(feed_other), 0.0).astype(BF)
+    second_x, product_x = (blocks(second_t, 24),), (blocks(product_t, 32),)
+
+    jobs = [
+        ([second_x], [(gate_low[None],)], [(0, 0, 0, 0, part)]),
+        ([second_x], [(up_low[None],)], [(0, 0, 0, 0, part)]),
+        ([product_x], [(jnp.concatenate(cots, axis=0)[None],)], [(0, 0, 0, 0, width)]),
+    ]
+    early = [places[0], after(places[1], (grad_got, normed_x, att_x)), places[2]]
+    sends = [weight_gradient(early[s], core_at, *job)[0] for s, job in enumerate(jobs)]
+    gots = exchange(sends, 0)
+
+    grads, branch, grad_tokens, misc_grad = attention_backward(
+        flat,
+        normed_t,
+        (gain, after(hidden, sends), cot, second_grad, grad_got),
+        (q, k, v, h, *cells, beta),
+        attn,
+    )
+    grads_y = (grads, swap(grads))
     branch_y = (branch[None], swap(branch)[None])
-
-    part = hidden_units // 2
-    jobs = [
-        ([second_x], [acts_y], [(0, 0, 0, 0, part)]),
-        ([second_x], [acts_y], [(0, 0, 1, 0, part)]),
-        ([product_x], [cot_y], [(0, 0, 0, 0, half)]),
-    ]
-    sends = [weight_gradient(places[s], core_at, *job)[0] for s, job in enumerate(jobs)]
-    gots = exchange(sends, 0)
-    branch = after(branch, sends)
-
-    grads, grad_tokens, misc_grad = attention_backward(
-        flat, normed_t, branch, hidden_grad, ffn_gain, (q, k, v, h, probs, carried, inverse, beta), attn
-    )
-    grads_y = (grads, swap(grads))
     misc_x = misc_grad.reshape(-1, 24, 128)
     attn_jobs = [
         ([normed_x], [grads_y], [(0, 0, 0, 0, 768), (0, 0, 1, 0, 512)]),
@@ -1013,27 +1125,31 @@
         return [p[0] for p in pairs], [p[1] for p in pairs]
 
     keeps, sends = kept(jobs, gots)
-    gots = exchange(sends, 1)
+    gots = exchange([after(send, got) for send, got in zip(sends, attn_gots)], 1)
     attn_keeps, attn_sends = kept(attn_jobs, [after(got, keeps) for got in attn_gots])
     attn_gots = exchange(attn_sends, 1)
     first, second = list(zip(keeps, gots)), list(zip(attn_keeps, attn_gots))
-    groups = [[first[0], second[0]], [first[1], second[1]], [first[2]], [second[2]]]
+    groups = [list(pair) for pair in zip(first, second)]
     for step in range(2, 6):
         keeps, sends = add_halves(groups)
-        gots = exchange(sends, step, (0, 1, 2, 2))
+        gots = exchange(sends, step)
         groups = [[pair] for pair in zip(keeps, gots)]
-    mine, theirs, mine_down, theirs_down = last_add(core_at, [group[0] for group in groups])
-    *large, misc_sum = finish(core_at, mine, swap(theirs), mine_down, swap(theirs_down))
+    mine, theirs, grad_down = last_add(core_at, [group[0] for group in groups], w_down.shape)
+    *large, grad_gate, grad_up, grad_beta, attn_gain, ffn_gain = finish(
+        core_at, mine, swap(theirs), hidden_units, heads
+    )
 
     return (
         mixed.reshape(seqs, count, width),
         grad_tokens.reshape(seqs, count, width),
-        misc_sum[:, heads],
+        attn_gain.reshape(-1),
         *large[:4],
-        misc_sum[:, :heads],
+        grad_beta,
         large[4],
-        misc_sum[:, heads + 1],
-        *large[5:],
+        ffn_gain.reshape(-1),
+        grad_gate,
+        grad_up,
+        grad_down,
     )
 
 

time: 402 us -> 385 us (0.958)
  local copies, waits for them, and re-layouts: 23.9 us -> 13.4 us
  Pallas kernels: 111 us -> 103 us
  waiting for transfers between devices: 177 us -> 170 us
  starting transfers between devices: 72.4 us -> 79.2 us
    ppermute x13 -> x10, starting transfers between devices: 24.3 us -> 41.2 us  [swap(): return lax.ppermute(value, 'fsdp', [(d, d ^ 1) for d in range(count)])]
    all_gather x1, waiting for transfers between devices: 60.1 us -> 70.5 us  [body(): lax.all_gather(slab, 'fsdp', axis=0, tiled=True, axis_index_groups=by_core)]
    ppermute x46 -> x42, starting transfers between devices: 48.1 us -> 38 us  [send_step(): return lax.ppermute(value, 'fsdp', pairs)]
    ppermute x13 -> x10, waiting for transfers between devices: 13.1 us -> 3.33 us  [swap(): return lax.ppermute(value, 'fsdp', [(d, d ^ 1) for d in range(count)])]
    pallas_call x1, Pallas kernels: 26.1 us -> 16.7 us  [feedforward(): pl.pallas_call(feedforward_kernel, grid_spec=pltpu.PrefetchScalarGridSpec...]
    ppermute x46 -> x42, waiting for transfers between devices: 104 us -> 96.3 us  [send_step(): return lax.ppermute(value, 'fsdp', pairs)]
    unnamed x53 -> x80, local copies, waits for them, and re-layouts: 11.1 us -> 10.2 us
    pallas_call x12 -> x13, Pallas kernels: 36.2 us -> 35.7 us  [the longest x12 33.5 us: weight_gradient(): pl.pallas_call(functools.partial(weight_gradient_kernel, segments, x_coun...]
  transfers between devices with their start and end apart: 60 -> 53, of which waited for: 30 -> 26; matrix products, arithmetic and copies ran while one was open for 4% -> 2% of each run, Pallas kernels for 20% -> 21%
where the time goes in v3:
time: 385 us
  waiting for transfers between devices  170 us (44%)
  Pallas kernels  103 us (27%)
  starting transfers between devices  79.2 us (21%)
  between operations  15.3 us (4%)
  local copies, waits for them, and re-layouts  13.4 us (3%)
    ppermute x42, waiting for transfers between devices, send_step(): return lax.ppermute(value, 'fsdp', pairs)  96.3 us
    all_gather x1, waiting for transfers between devices, body(): lax.all_gather(slab, 'fsdp', axis=0, tiled=True, axis_index_groups=by_core)  70.5 us
    ppermute x10, starting transfers between devices, swap(): return lax.ppermute(value, 'fsdp', [(d, d ^ 1) for d in range(count)])  41.2 us
    ppermute x42, starting transfers between devices, send_step(): return lax.ppermute(value, 'fsdp', pairs)  38 us
    pallas_call x12, Pallas kernels, weight_gradient(): pl.pallas_call(functools.partial(weight_gradient_kernel, segments, x_coun...  33.5 us
    pallas_call x1, Pallas kernels, attention_backward(): pl.pallas_call(attention_backward_kernel, grid=(steps,), in_specs=[rows,...  18.7 us
    pallas_call x1, Pallas kernels, attention_forward(): pl.pallas_call(attention_forward_kernel, grid_spec=pltpu.PrefetchScalarGr...  18.3 us
    pallas_call x1, Pallas kernels, feedforward(): pl.pallas_call(feedforward_kernel, grid_spec=pltpu.PrefetchScalarGridSpec...  16.7 us
  transfers between devices with their start and end apart: 53, of which 26 were waited for; matrix products, arithmetic and copies ran while one was open for 2% of the time, Pallas kernels for 21%

profile of v3, /device:TPU:1, one launch (start us, length us, event | category | flops | bytes accessed | tf_op | source)
XLA Modules:
  0.0 384.8 jit_solution(8976156250884156913)
XLA Ops:
  23.9 2.6 collective-permute-start.6
  29.7 3.8 collective-permute-done.12
  36.6 4.4 %collective-permute-done.13 = bf16[8,32,512]{2,1,0:T(8,128)(2,1)S(1)} collective-permute-done((bf16[8,32,512]{2,1,0:T(8,128)(2,1)S(1)}, bf16[8,32,512]{2,1,0:T(8,128)(2,1)S(1)}, u32[]{:S(2)}, u32[]{:S(2)}) %collective-permute-start.13) | collective-permute-done | bytes 262176 | tf_op jit(solution)/shard_map/ppermute | solution.py:976
  44.9 10.6 %collective-permute-done.14 = bf16[16,32,512]{2,1,0:T(8,128)(2,1)S(1)} collective-permute-done((bf16[16,32,512]{2,1,0:T(8,128)(2,1)S(1)}, bf16[16,32,512]{2,1,0:T(8,128)(2,1)S(1)}, u32[]{:S(2)}, u32[]{:S(2)}) %collective-permute-start.14) | collective-permute-done | bytes 524320 | tf_op jit(solution)/shard_map/ppermute | solution.py:976
  58.7 22.6 %collective-permute-start.20 = (bf16[128,1536]{1,0:T(8,128)(2,1)S(1)}, bf16[128,1536]{1,0:T(8,128)(2,1)S(1)}, u32[]{:S(2)}, u32[]{:S(2)}) collective-permute-start(bf16[128,1536]{1,0:T(8,128)(2,1)S(1)} %bitcast_select_fusion.cot_own_ref.cot_ref), channel_id=1, source_target_pairs={{0,1},{1,0},{2,3},{3,2},{4,5},{5,4},{6,7},{7,6},{8,9},{9,8},{10,11... | collective-permute-start | bytes 1179656 | tf_op jit(solution)/shard_map/ppermute | solution.py:71
  82.1 5.0 %collective-permute-done.16.refs_4_ = bf16[32,32,512]{2,1,0:T(8,128)(2,1)} collective-permute-done((bf16[32,32,512]{2,1,0:T(8,128)(2,1)}, bf16[32,32,512]{2,1,0:T(8,128)(2,1)}, u32[]{:S(2)}, u32[]{:S(2)}) %collective-permute-start.16) | collective-permute-done | bytes 1048608 | tf_op jit(solution)/shard_map/ppermute | solution.py:976
  87.1 8.1 %in_order.1 = bf16[64,32,1536]{2,1,0:T(8,128)(2,1)} custom-call(s32[3,64]{1,0:T(4,128)} %get-tuple-element.223.place_ref, bf16[32,32,512]{2,1,0:T(8,128)(2,1)} %copy-done.24, bf16[32,32,512]{2,1,0:T(8,128)(2,1)} %constant_dynamic-update-slice_fusion.16.refs_1_, bf16[32,32,512]{2,1,0:T(8,128)(2,1)} %constant_dynamic-update-slice_fusion.27.refs_2_, ...), custom_call_target="tpu_custom_call" | custom-call | flops 1 | bytes 1 | tf_op jit(solution)/shard_map/in_order/pallas_call | solution.py:1013
  95.2 70.5 %all-gather.2.cloned.1.call-done.wq_ref.wk_ref.wv_ref.wh_ref.out_lo_ref.out_hi_ref.misc_ref.wg_ref.wu_ref.wo_lo_ref.wo_hi_ref = bf16[3072,8192]{1,0:T(8,128)(2,1)} async-done(((bf16[24,8192]{1,0:T(8,128)(2,1)}), bf16[3072,8192]{1,0:T(8,128)(2,1)}) %all-gather.2.cloned.1.call-update) | async-done | bytes 50331664 | tf_op jit(solution)/shard_map/all_gather | solution.py:1068
  165.7 18.3 %attention_forward.1 = (bf16[1536,128]{1,0:T(8,128)(2,1)}, bf16[128,1536]{1,0:T(8,128)(2,1)}, bf16[128,1536]{1,0:T(8,128)(2,1)}, bf16[128,1536]{1,0:T(8,128)(2,1...) custom-call(s32[1]{0:T(128)} %copy.55.length_ref, ...), custom_call_target="tpu_custom_call" | custom-call | flops 5435817984 | bytes 23592960 | tf_op jit(solution)/shard_map/attention_forward/pallas_call | solution.py:226
  187.0 16.7 %feedforward.1 = (bf16[1536,256]{1,0:T(8,128)(2,1)}, bf16[2048,256]{1,0:T(8,128)(2,1)}, bf16[256,2048]{1,0:T(8,128)(2,1)}, bf16[256,2048]{1,0:T(8,128)(2,1)}, f3...) custom-call(s32[1]{0:T(128)} %bitcast.7.core_ref.refs_1_, ...), custom_call_target="tpu_custom_call" | custom-call | flops 9663676416 | bytes 18874368 | tf_op jit(solution)/shard_map/feedforward/pallas_call | solution.py:352
  206.9 3.5 weight_gradient.6
  210.5 2.4 collective-permute-start.25
  213.0 3.5 weight_gradient.8
  216.4 2.5 collective-permute-start.30
  218.9 3.5 weight_gradient.7
  223.0 18.7 %attention_backward.1 = (bf16[4,128,1536]{2,1,0:T(8,128)(2,1)}, bf16[128,1536]{1,0:T(8,128)(2,1)}, f32[128,1536]{1,0:T(8,128)}, bf16[1536,128]{1,0:T(8,128)(2,1)}) custom-call(bf16[128,1536]{1,0:T(8,128)(2,1)} %bitcast.87, bf16[1536,128]{1,0:T(8,128)(2,1)} %get-tuple-element.108.normed_t_ref, f32[1,1536]{1,0:T(1,128)} %get-tuple-element.109.gain_ref, ...), custom_call_target="tpu_custom_call" | custom-call | flops 1 | bytes 1 | tf_op jit(solution)/shard_map/attention_backward/pallas_call | solution.py:562
  242.3 5.7 %collective-permute-done.25.refs_4_.refs_5_ = bf16[32,24,2048]{2,1,0:T(8,128)(2,1)S(1)} collective-permute-done((bf16[32,24,2048]{2,1,0:T(8,128)(2,1)}, bf16[32,24,2048]{2,1,0:T(8,128)(2,1)S(1)}, u32[]{:S(2)}, u32[]{:S(2)}) %collective-permute-start.25) | collective-permute-done | bytes 3145760 | tf_op jit(solution)/shard_map/ppermute | solution.py:976
  249.4 3.2 weight_gradient.9
  252.6 2.4 collective-permute-start.27
  257.1 2.6 collective-permute-start.36
  262.8 4.0 %weight_gradient_add.8 = (bf16[16,32,1536]{2,1,0:T(8,128)(2,1)S(1)}, bf16[16,32,1536]{2,1,0:T(8,128)(2,1)S(1)}) custom-call(s32[64]{0:T(128)S(1)} %get-tuple-element.145.refs_0_, s32[1]{0:T(128)} %bitcast.7.core_ref.refs_1_, bf16[64,32,256]{2,1,0:T(8,128)(2,1)S(1)} %bitcast.74, bf16[1,256,1536]{2,1,0:T(8,128)(2,1)S(1)} %maximum_bitcast_fusion.refs_3_, ...), custom_call_target="tpu_custom_call" | custom-call | flops 1 | bytes 1 | tf_op jit(solution)/shard_map/weight_gradient_add/pallas_call | solution.py:706
  270.1 4.1 %weight_gradient_add.7 = (bf16[16,24,2048]{2,1,0:T(8,128)(2,1)S(1)}, bf16[16,24,2048]{2,1,0:T(8,128)(2,1)S(1)}) custom-call(s32[64]{0:T(128)S(1)} %get-tuple-element.139.refs_0_, s32[1]{0:T(128)} %bitcast.7.core_ref.refs_1_, bf16[64,24,256]{2,1,0:T(8,128)(2,1)S(1)} %bitcast.68, bf16[1,256,2048]{2,1,0:T(8,128)(2,1)S(1)} %bitcast.70, ...), custom_call_target="tpu_custom_call" | custom-call | flops 1 | bytes 1 | tf_op jit(solution)/shard_map/weight_gradient_add/pallas_call | solution.py:706
  274.2 3.3 collective-permute-done.27.refs_6_.refs_7_
  281.0 3.2 collective-permute-done.36.refs_11_.refs_12_
  284.2 3.0 collective-permute-done.32.refs_6_.refs_7_
  293.1 22.3 %collective-permute-done.38.refs_22_.refs_23_ = bf16[16,24,1408]{2,1,0:T(8,128)(2,1)S(1)} collective-permute-done((bf16[16,24,1408]{2,1,0:T(8,128)(2,1)S(1)}, bf16[16,24,1408]{2,1,0:T(8,128)(2,1)S(1)}, u32[]{:S(2)}, u32[]{:S(2)}) %collective-permute-start.38) | collective-permute-done | bytes 1081376 | tf_op jit(solution)/shard_map/ppermute | solution.py:976
  321.7 16.0 %collective-permute-done.39.refs_2_.refs_3_ = bf16[8,24,3328]{2,1,0:T(8,128)(2,1)S(1)} collective-permute-done((bf16[8,24,3328]{2,1,0:T(8,128)(2,1)S(1)}, bf16[8,24,3328]{2,1,0:T(8,128)(2,1)S(1)}, u32[]{:S(2)}, u32[]{:S(2)}) %collective-permute-start.39) | collective-permute-done | bytes 1277984 | tf_op jit(solution)/shard_map/ppermute | solution.py:976
  339.8 4.5 %collective-permute-start.21 = (f32[128,1536]{1,0:T(8,128)S(1)}, f32[128,1536]{1,0:T(8,128)S(1)}, u32[]{:S(2)}, u32[]{:S(2)}) collective-permute-start(f32[128,1536]{1,0:T(8,128)S(1)} %copy-done.34), channel_id=1, source_target_pairs={{0,1},{1,0},{2,3},{3,2},{4,5},{5,4},{6,7},{7,6},{8,9},{9,8},{10,11... | collective-permute-start | bytes 2359304 | tf_op jit(solution)/shard_map/ppermute | solution.py:71
  344.3 5.0 %collective-permute-done.42.refs_2_.refs_3_ = bf16[4,24,3328]{2,1,0:T(8,128)(2,1)S(1)} collective-permute-done((bf16[4,24,3328]{2,1,0:T(8,128)(2,1)S(1)}, bf16[4,24,3328]{2,1,0:T(8,128)(2,1)S(1)}, u32[]{:S(2)}, u32[]{:S(2)}) %collective-permute-start.42) | collective-permute-done | bytes 639008 | tf_op jit(solution)/shard_map/ppermute | solution.py:976
  354.1 5.0 %collective-permute-done.45.refs_2_.refs_3_ = bf16[2,24,3328]{2,1,0:T(8,128)(2,1)S(1)} collective-permute-done((bf16[2,24,3328]{2,1,0:T(8,128)(2,1)S(1)}, bf16[2,24,3328]{2,1,0:T(8,128)(2,1)S(1)}, u32[]{:S(2)}, u32[]{:S(2)}) %collective-permute-start.45) | collective-permute-done | bytes 319520 | tf_op jit(solution)/shard_map/ppermute | solution.py:976
  361.2 2.7 collective-permute-done.48.refs_1_
  364.7 10.8 %collective-permute-start.51 = (bf16[12,8192]{1,0:T(8,128)(2,1)S(1)}, bf16[12,8192]{1,0:T(8,128)(2,1)S(1)}, u32[]{:S(2)}, u32[]{:S(2)}) collective-permute-start(bf16[12,8192]{1,0:T(8,128)(2,1)S(1)} %get-tuple-element.177), channel_id=1, source_target_pairs={{0,1},{1,0},{2,3},{3,2},{4,5},{5,4},{6,7},{7,6},{8,9},{9,8},{10,11... | collective-permute-start | bytes 589832 | tf_op jit(solution)/shard_map/ppermute | solution.py:71
  (201 shorter events, 75.2 us)
Async XLA Ops:
  7.2 158.5 %all-gather.2.cloned.1.call-start = ((), (), s32[]{:S(2)}) async-start(), calls=%async_computation | async-start | bytes 50724864 | tf_op jit(solution)/shard_map/all_gather | solution.py:1068
  33.7 11.1 %collective-permute-start.3 = (bf16[8,32,512]{2,1,0:T(8,128)(2,1)S(1)}, bf16[8,32,512]{2,1,0:T(8,128)(2,1)S(1)}, u32[]{:S(2)}, u32[]{:S(2)}) collective-permute-start(bf16[8,32,512]{2,1,0:T(8,128)(2,1)S(1)} %pad_maximum_fusion), channel_id=1, source_target_pairs={{0,8},{1,25},{2,10},{3,27},{4,12},{5,29},{6,14},{7,31},{8,0},{9,17... | collective-permute-start | bytes 786440 | tf_op jit(solution)/shard_map/ppermute | solution.py:976
  33.8 10.0 %collective-permute-start.8 = (bf16[8,32,512]{2,1,0:T(8,128)(2,1)S(1)}, bf16[8,32,512]{2,1,0:T(8,128)(2,1)S(1)}, u32[]{:S(2)}, u32[]{:S(2)}) collective-permute-start(bf16[8,32,512]{2,1,0:T(8,128)(2,1)S(1)} %pad_maximum_fusion.1), channel_id=1, source_target_pairs={{0,2},{1,7},{2,0},{3,5},{4,6},{5,3},{6,4},{7,1},{8,10},{9,15},{10,... | collective-permute-start | bytes 786440 | tf_op jit(solution)/shard_map/ppermute | solution.py:976
  41.8 13.7 %collective-permute-start.14 = (bf16[16,32,512]{2,1,0:T(8,128)(2,1)S(1)}, bf16[16,32,512]{2,1,0:T(8,128)(2,1)S(1)}, u32[]{:S(2)}, u32[]{:S(2)}) collective-permute-start(bf16[16,32,512]{2,1,0:T(8,128)(2,1)S(1)} %get-tuple-element.189), channel_id=1, source_target_pairs={{0,6},{1,3},{2,4},{3,1},{4,2},{5,7},{6,0},{7,5},{8,14},{9,11},{10,... | collective-permute-start | bytes 1572872 | tf_op jit(solution)/shard_map/ppermute | solution.py:976
  44.6 11.8 %collective-permute-start.9 = (bf16[16,32,512]{2,1,0:T(8,128)(2,1)S(1)}, bf16[16,32,512]{2,1,0:T(8,128)(2,1)S(1)}, u32[]{:S(2)}, u32[]{:S(2)}) collective-permute-start(bf16[16,32,512]{2,1,0:T(8,128)(2,1)S(1)} %get-tuple-element.191), channel_id=1, source_target_pairs={{0,24},{1,9},{2,26},{3,11},{4,28},{5,13},{6,30},{7,15},{8,16},{9,1... | collective-permute-start | bytes 1572872 | tf_op jit(solution)/shard_map/ppermute | solution.py:976
  44.8 12.3 %collective-permute-start.4 = (bf16[16,32,512]{2,1,0:T(8,128)(2,1)S(1)}, bf16[16,32,512]{2,1,0:T(8,128)(2,1)S(1)}, u32[]{:S(2)}, u32[]{:S(2)}) collective-permute-start(bf16[16,32,512]{2,1,0:T(8,128)(2,1)S(1)} %get-tuple-element.193), channel_id=1, source_target_pairs={{0,96},{1,33},{2,98},{3,35},{4,100},{5,37},{6,102},{7,39},{8,104},... | collective-permute-start | bytes 1572872 | tf_op jit(solution)/shard_map/ppermute | solution.py:976
  56.3 25.8 %collective-permute-start.17 = (bf16[32,32,512]{2,1,0:T(8,128)(2,1)}, bf16[32,32,512]{2,1,0:T(8,128)(2,1)}, u32[]{:S(2)}, u32[]{:S(2)}) collective-permute-start(bf16[32,32,512]{2,1,0:T(8,128)(2,1)} %constant_dynamic-update-slice_fusion.27.refs_2_), channel_id=1, source_target_pairs={{0,2},{1,7},{2,0},{3,5},{4,6},{5,3},{6,4},{7,1},{8,10},{9,15},{10,... | collective-permute-start | bytes 3145736 | tf_op jit(solution)/shard_map/ppermute | solution.py:976
  57.2 30.0 %collective-permute-start.16 = (bf16[32,32,512]{2,1,0:T(8,128)(2,1)}, bf16[32,32,512]{2,1,0:T(8,128)(2,1)}, u32[]{:S(2)}, u32[]{:S(2)}) collective-permute-start(bf16[32,32,512]{2,1,0:T(8,128)(2,1)} %constant_dynamic-update-slice_fusion.16.refs_1_), channel_id=1, source_target_pairs={{0,8},{1,25},{2,10},{3,27},{4,12},{5,29},{6,14},{7,31},{8,0},{9,17... | collective-permute-start | bytes 3145736 | tf_op jit(solution)/shard_map/ppermute | solution.py:976
  57.2 29.9 %collective-permute-start.15 = (bf16[32,32,512]{2,1,0:T(8,128)(2,1)S(1)}, bf16[32,32,512]{2,1,0:T(8,128)(2,1)}, u32[]{:S(2)}, u32[]{:S(2)}) collective-permute-start(bf16[32,32,512]{2,1,0:T(8,128)(2,1)S(1)} %constant_dynamic-update-slice_fusion.5.refs_0_), channel_id=1, source_target_pairs={{0,32},{1,97},{2,34},{3,99},{4,36},{5,101},{6,38},{7,103},{8,40},{... | collective-permute-start | bytes 3145736 | tf_op jit(solution)/shard_map/ppermute | solution.py:976
  58.7 126.0 %collective-permute-start.20 = (bf16[128,1536]{1,0:T(8,128)(2,1)S(1)}, bf16[128,1536]{1,0:T(8,128)(2,1)S(1)}, u32[]{:S(2)}, u32[]{:S(2)}) collective-permute-start(bf16[128,1536]{1,0:T(8,128)(2,1)S(1)} %bitcast_select_fusion.cot_own_ref.cot_ref), channel_id=1, source_target_pairs={{0,1},{1,0},{2,3},{3,2},{4,5},{5,4},{6,7},{7,6},{8,9},{9,8},{10,11... | collective-permute-start | bytes 1179656 | tf_op jit(solution)/shard_map/ppermute | solution.py:71
  203.7 15.2 %collective-permute-start.22 = (f32[128,1536]{1,0:T(8,128)}, f32[128,1536]{1,0:T(8,128)S(1)}, u32[]{:S(2)}, u32[]{:S(2)}) collective-permute-start(f32[128,1536]{1,0:T(8,128)} %get-tuple-element.112), channel_id=1, source_target_pairs={{0,1},{1,0},{2,3},{3,2},{4,5},{5,4},{6,7},{7,6},{8,9},{9,8},{10,11... | collective-permute-start | bytes 2359304 | tf_op jit(solution)/shard_map/ppermute | solution.py:71
  204.1 14.8 %collective-permute-start.24 = (bf16[1536,128]{1,0:T(8,128)(2,1)S(1)}, bf16[1536,128]{1,0:T(8,128)(2,1)S(1)}, u32[]{:S(2)}, u32[]{:S(2)}) collective-permute-start(bf16[1536,128]{1,0:T(8,128)(2,1)S(1)} %copy-done.12), channel_id=1, source_target_pairs={{0,1},{1,0},{2,3},{3,2},{4,5},{5,4},{6,7},{7,6},{8,9},{9,8},{10,11... | collective-permute-start | bytes 1179656 | tf_op jit(solution)/shard_map/ppermute | solution.py:71
  204.3 14.6 %collective-permute-start.23 = (bf16[1536,128]{1,0:T(8,128)(2,1)S(1)}, bf16[1536,128]{1,0:T(8,128)(2,1)S(1)}, u32[]{:S(2)}, u32[]{:S(2)}) collective-permute-start(bf16[1536,128]{1,0:T(8,128)(2,1)S(1)} %copy-done.2), channel_id=1, source_target_pairs={{0,1},{1,0},{2,3},{3,2},{4,5},{5,4},{6,7},{7,6},{8,9},{9,8},{10,11... | collective-permute-start | bytes 1179656 | tf_op jit(solution)/shard_map/ppermute | solution.py:71
  210.5 37.5 %collective-permute-start.25 = (bf16[32,24,2048]{2,1,0:T(8,128)(2,1)}, bf16[32,24,2048]{2,1,0:T(8,128)(2,1)S(1)}, u32[]{:S(2)}, u32[]{:S(2)}) collective-permute-start(bf16[32,24,2048]{2,1,0:T(8,128)(2,1)} %weight_gradient.6), channel_id=1, source_target_pairs={{0,32},{1,97},{2,34},{3,99},{4,36},{5,101},{6,38},{7,103},{8,40},{... | collective-permute-start | bytes 9437192 | tf_op jit(solution)/shard_map/ppermute | solution.py:976
  216.4 38.6 %collective-permute-start.30 = (bf16[32,32,1536]{2,1,0:T(8,128)(2,1)}, bf16[32,32,1536]{2,1,0:T(8,128)(2,1)}, u32[]{:S(2)}, u32[]{:S(2)}) collective-permute-start(bf16[32,32,1536]{2,1,0:T(8,128)(2,1)} %weight_gradient.8), channel_id=1, source_target_pairs={{0,2},{1,7},{2,0},{3,5},{4,6},{5,3},{6,4},{7,1},{8,10},{9,15},{10,... | collective-permute-start | bytes 9437192 | tf_op jit(solution)/shard_map/ppermute | solution.py:976
  222.5 37.6 %collective-permute-start.29 = (bf16[32,24,2048]{2,1,0:T(8,128)(2,1)}, bf16[32,24,2048]{2,1,0:T(8,128)(2,1)}, u32[]{:S(2)}, u32[]{:S(2)}) collective-permute-start(bf16[32,24,2048]{2,1,0:T(8,128)(2,1)} %weight_gradient.7), channel_id=1, source_target_pairs={{0,8},{1,25},{2,10},{3,27},{4,12},{5,29},{6,14},{7,31},{8,0},{9,17... | collective-permute-start | bytes 9437192 | tf_op jit(solution)/shard_map/ppermute | solution.py:976
  241.8 13.2 %collective-permute-start.35 = (bf16[128,1536]{1,0:T(8,128)(2,1)}, bf16[128,1536]{1,0:T(8,128)(2,1)S(1)}, u32[]{:S(2)}, u32[]{:S(2)}) collective-permute-start(bf16[128,1536]{1,0:T(8,128)(2,1)} %get-tuple-element.146), channel_id=1, source_target_pairs={{0,1},{1,0},{2,3},{3,2},{4,5},{5,4},{6,7},{7,6},{8,9},{9,8},{10,11... | collective-permute-start | bytes 1179656 | tf_op jit(solution)/shard_map/ppermute | solution.py:71
  252.6 24.9 %collective-permute-start.27 = (bf16[32,24,1280]{2,1,0:T(8,128)(2,1)}, bf16[32,24,1280]{2,1,0:T(8,128)(2,1)S(1)}, u32[]{:S(2)}, u32[]{:S(2)}) collective-permute-start(bf16[32,24,1280]{2,1,0:T(8,128)(2,1)} %weight_gradient.9), channel_id=1, source_target_pairs={{0,32},{1,97},{2,34},{3,99},{4,36},{5,101},{6,38},{7,103},{8,40},{... | collective-permute-start | bytes 5898248 | tf_op jit(solution)/shard_map/ppermute | solution.py:976
  257.1 27.2 %collective-permute-start.36 = (bf16[32,24,1408]{2,1,0:T(8,128)(2,1)S(1)}, bf16[32,24,1408]{2,1,0:T(8,128)(2,1)S(1)}, u32[]{:S(2)}, u32[]{:S(2)}) collective-permute-start(bf16[32,24,1408]{2,1,0:T(8,128)(2,1)S(1)} %weight_gradient.11), channel_id=1, source_target_pairs={{0,2},{1,7},{2,0},{3,5},{4,6},{5,3},{6,4},{7,1},{8,10},{9,15},{10,... | collective-permute-start | bytes 6488072 | tf_op jit(solution)/shard_map/ppermute | solution.py:976
  262.0 25.3 %collective-permute-start.32 = (bf16[32,24,1280]{2,1,0:T(8,128)(2,1)S(1)}, bf16[32,24,1280]{2,1,0:T(8,128)(2,1)S(1)}, u32[]{:S(2)}, u32[]{:S(2)}) collective-permute-start(bf16[32,24,1280]{2,1,0:T(8,128)(2,1)S(1)} %weight_gradient.10), channel_id=1, source_target_pairs={{0,8},{1,25},{2,10},{3,27},{4,12},{5,29},{6,14},{7,31},{8,0},{9,17... | collective-permute-start | bytes 5898248 | tf_op jit(solution)/shard_map/ppermute | solution.py:976
  279.4 13.3 %collective-permute-start.31 = (bf16[16,24,1280]{2,1,0:T(8,128)(2,1)S(1)}, bf16[16,24,1280]{2,1,0:T(8,128)(2,1)S(1)}, u32[]{:S(2)}, u32[]{:S(2)}) collective-permute-start(bf16[16,24,1280]{2,1,0:T(8,128)(2,1)S(1)} %get-tuple-element.137), channel_id=1, source_target_pairs={{0,96},{1,33},{2,98},{3,35},{4,100},{5,37},{6,102},{7,39},{8,104},... | collective-permute-start | bytes 2949128 | tf_op jit(solution)/shard_map/ppermute | solution.py:976
  279.5 35.8 %collective-permute-start.28 = (bf16[16,24,2048]{2,1,0:T(8,128)(2,1)S(1)}, bf16[16,24,2048]{2,1,0:T(8,128)(2,1)S(1)}, u32[]{:S(2)}, u32[]{:S(2)}) collective-permute-start(bf16[16,24,2048]{2,1,0:T(8,128)(2,1)S(1)} %copy-done.18), channel_id=1, source_target_pairs={{0,96},{1,33},{2,98},{3,35},{4,100},{5,37},{6,102},{7,39},{8,104},... | collective-permute-start | bytes 4718600 | tf_op jit(solution)/shard_map/ppermute | solution.py:976
  284.2 31.2 %collective-permute-start.37 = (bf16[16,32,1536]{2,1,0:T(8,128)(2,1)S(1)}, bf16[16,32,1536]{2,1,0:T(8,128)(2,1)S(1)}, u32[]{:S(2)}, u32[]{:S(2)}) collective-permute-start(bf16[16,32,1536]{2,1,0:T(8,128)(2,1)S(1)} %get-tuple-element.148), channel_id=1, source_target_pairs={{0,6},{1,3},{2,4},{3,1},{4,2},{5,7},{6,0},{7,5},{8,14},{9,11},{10,... | collective-permute-start | bytes 4718600 | tf_op jit(solution)/shard_map/ppermute | solution.py:976
  287.3 30.1 %collective-permute-start.33 = (bf16[16,24,2048]{2,1,0:T(8,128)(2,1)S(1)}, bf16[16,24,2048]{2,1,0:T(8,128)(2,1)S(1)}, u32[]{:S(2)}, u32[]{:S(2)}) collective-permute-start(bf16[16,24,2048]{2,1,0:T(8,128)(2,1)S(1)} %get-tuple-element.140), channel_id=1, source_target_pairs={{0,24},{1,9},{2,26},{3,11},{4,28},{5,13},{6,30},{7,15},{8,16},{9,1... | collective-permute-start | bytes 4718600 | tf_op jit(solution)/shard_map/ppermute | solution.py:976
  289.3 26.1 %collective-permute-start.38 = (bf16[16,24,1408]{2,1,0:T(8,128)(2,1)S(1)}, bf16[16,24,1408]{2,1,0:T(8,128)(2,1)S(1)}, u32[]{:S(2)}, u32[]{:S(2)}) collective-permute-start(bf16[16,24,1408]{2,1,0:T(8,128)(2,1)S(1)} %get-tuple-element.151), channel_id=1, source_target_pairs={{0,6},{1,3},{2,4},{3,1},{4,2},{5,7},{6,0},{7,5},{8,14},{9,11},{10,... | collective-permute-start | bytes 3244040 | tf_op jit(solution)/shard_map/ppermute | solution.py:976
  292.8 24.6 %collective-permute-start.34 = (bf16[16,24,1280]{2,1,0:T(8,128)(2,1)S(1)}, bf16[16,24,1280]{2,1,0:T(8,128)(2,1)S(1)}, u32[]{:S(2)}, u32[]{:S(2)}) collective-permute-start(bf16[16,24,1280]{2,1,0:T(8,128)(2,1)S(1)} %get-tuple-element.143), channel_id=1, source_target_pairs={{0,24},{1,9},{2,26},{3,11},{4,28},{5,13},{6,30},{7,15},{8,16},{9,1... | collective-permute-start | bytes 2949128 | tf_op jit(solution)/shard_map/ppermute | solution.py:976
  319.2 19.4 %collective-permute-start.41 = (bf16[8,32,2688]{2,1,0:T(8,128)(2,1)S(1)}, bf16[8,32,2688]{2,1,0:T(8,128)(2,1)S(1)}, u32[]{:S(2)}, u32[]{:S(2)}) collective-permute-start(bf16[8,32,2688]{2,1,0:T(8,128)(2,1)S(1)} %get-tuple-element.157), channel_id=1, source_target_pairs={{0,32},{1,97},{2,34},{3,99},{4,36},{5,101},{6,38},{7,103},{8,40},{... | collective-permute-start | bytes 4128776 | tf_op jit(solution)/shard_map/ppermute | solution.py:976
  320.4 17.3 %collective-permute-start.39 = (bf16[8,24,3328]{2,1,0:T(8,128)(2,1)S(1)}, bf16[8,24,3328]{2,1,0:T(8,128)(2,1)S(1)}, u32[]{:S(2)}, u32[]{:S(2)}) collective-permute-start(bf16[8,24,3328]{2,1,0:T(8,128)(2,1)S(1)} %get-tuple-element.153), channel_id=1, source_target_pairs={{0,8},{1,25},{2,10},{3,27},{4,12},{5,29},{6,14},{7,31},{8,0},{9,17... | collective-permute-start | bytes 3833864 | tf_op jit(solution)/shard_map/ppermute | solution.py:976
  321.3 17.3 %collective-permute-start.40 = (bf16[8,24,3328]{2,1,0:T(8,128)(2,1)S(1)}, bf16[8,24,3328]{2,1,0:T(8,128)(2,1)S(1)}, u32[]{:S(2)}, u32[]{:S(2)}) collective-permute-start(bf16[8,24,3328]{2,1,0:T(8,128)(2,1)S(1)} %get-tuple-element.155), channel_id=1, source_target_pairs={{0,2},{1,7},{2,0},{3,5},{4,6},{5,3},{6,4},{7,1},{8,10},{9,15},{10,... | collective-permute-start | bytes 3833864 | tf_op jit(solution)/shard_map/ppermute | solution.py:976
  339.6 10.2 %collective-permute-start.44 = (bf16[4,32,2688]{2,1,0:T(8,128)(2,1)S(1)}, bf16[4,32,2688]{2,1,0:T(8,128)(2,1)S(1)}, u32[]{:S(2)}, u32[]{:S(2)}) collective-permute-start(bf16[4,32,2688]{2,1,0:T(8,128)(2,1)S(1)} %get-tuple-element.163), channel_id=1, source_target_pairs={{0,96},{1,33},{2,98},{3,35},{4,100},{5,37},{6,102},{7,39},{8,104},... | collective-permute-start | bytes 2064392 | tf_op jit(solution)/shard_map/ppermute | solution.py:976
  339.8 35.7 %collective-permute-start.21 = (f32[128,1536]{1,0:T(8,128)S(1)}, f32[128,1536]{1,0:T(8,128)S(1)}, u32[]{:S(2)}, u32[]{:S(2)}) collective-permute-start(f32[128,1536]{1,0:T(8,128)S(1)} %copy-done.34), channel_id=1, source_target_pairs={{0,1},{1,0},{2,3},{3,2},{4,5},{5,4},{6,7},{7,6},{8,9},{9,8},{10,11... | collective-permute-start | bytes 2359304 | tf_op jit(solution)/shard_map/ppermute | solution.py:71
  364.7 11.9 %collective-permute-start.51 = (bf16[12,8192]{1,0:T(8,128)(2,1)S(1)}, bf16[12,8192]{1,0:T(8,128)(2,1)S(1)}, u32[]{:S(2)}, u32[]{:S(2)}) collective-permute-start(bf16[12,8192]{1,0:T(8,128)(2,1)S(1)} %get-tuple-element.177), channel_id=1, source_target_pairs={{0,1},{1,0},{2,3},{3,2},{4,5},{5,4},{6,7},{7,6},{8,9},{9,8},{10,11... | collective-permute-start | bytes 589832 | tf_op jit(solution)/shard_map/ppermute | solution.py:71
  (56 other events, 485.0 us)
Sparse Core Ops, SparseCore 0:
  14.4 151.2 all-gather.1

commit v4 on v3

--- a/solution.py
+++ b/solution.py
@@ -104,9 +104,9 @@
     return inverses
 
 
-PER_STEP = 4
+PER_STEP = 6
 SPAN = 128 * PER_STEP
-GATE_AT, UP_AT, FIRST_AT, SECOND_AT = 1024, 3072, 5120, 6656
+FIRST_AT, SECOND_AT, MISC_AT, GATE_AT, UP_AT = 768, 2304, 3840, 4096, 6144
 
 
 def attention_forward_kernel(
@@ -236,7 +236,7 @@
                 weight(1, SECOND_AT),
                 pl.BlockSpec((SPAN, width // 2), lambda i, *_: (i, 0)),
                 pl.BlockSpec((SPAN, width // 2), lambda i, *_: (steps + i, 0)),
-                pl.BlockSpec((width, 128), lambda i, *_: (0, 6)),
+                pl.BlockSpec((width, 128), lambda i, *_: (0, MISC_AT // 128)),
             ],
             out_specs=[
                 pl.BlockSpec((width, count), whole),
@@ -584,7 +584,7 @@
             weight(0, SECOND_AT),
             weight(1, FIRST_AT),
             weight(1, SECOND_AT),
-            pl.BlockSpec((width, 128), lambda i: (0, 6)),
+            pl.BlockSpec((width, 128), lambda i: (0, MISC_AT // 128)),
         ],
         out_specs=[
             pl.BlockSpec((4, count, SPAN), lambda i: (0, 0, i)),
@@ -629,6 +629,10 @@
     )
 
 
+OWNERS = 16
+AHEAD = ((), (1,), (0, 2))
+
+
 def weight_gradient_kernel(segments, x_counts, y_counts, has_misc, second_half, *refs):
     place_ref, refs = refs[0], list(refs[2:])
     xs = [[refs.pop(0) for _ in range(n)] for n in x_counts]
@@ -637,11 +641,12 @@
     at = pl.program_id(0)
     chips, height = xs[0][0].shape[0], xs[0][0].shape[1]
     if second_half:
-        spots = [(refs[0], None, i, chips // 2 + 8 * at + i) for i in range(8)]
+        spots = [(refs[0], None, i, chips // 2 + OWNERS * at + i) for i in range(OWNERS)]
     else:
         got_lo, got_hi, keep, send = refs
-        spots = [(keep, got_lo, i, 4 * at + i) for i in range(4)]
-        spots += [(send, got_hi, i, chips // 4 + 4 * at + i) for i in range(4)]
+        half = OWNERS // 2
+        spots = [(keep, got_lo, i, half * at + i) for i in range(half)]
+        spots += [(send, got_hi, i, chips // 4 + half * at + i) for i in range(half)]
     owners = [place_ref[spot[3]] for spot in spots]
     lefts = []
     for pieces in xs:
@@ -689,12 +694,12 @@
     if misc is not None:
         operands.append(misc)
         in_specs.append(pl.BlockSpec(misc.shape, lambda i, *_: (0, 0, 0)))
-    steps = chips // 16
+    steps = chips // 2 // OWNERS
     if got is None:
-        out_specs = [pl.BlockSpec((8, height, columns), lambda i, *_: (i, 0, 0))]
+        out_specs = [pl.BlockSpec((OWNERS, height, columns), lambda i, *_: (i, 0, 0))]
         out_shape = [jax.ShapeDtypeStruct((chips // 2, height, columns), BF)]
     else:
-        block = (4, height, columns)
+        block = (OWNERS // 2, height, columns)
         operands += [got, got]
         in_specs += [
             pl.BlockSpec(block, lambda i, *_: (i, 0, 0)),
@@ -925,7 +930,7 @@
         split(w_query[...], w_value[...]),
         split(w_key[...], w_house[...]),
     ]
-    for start, (own, other) in zip((0, half, FIRST_AT, SECOND_AT), pieces):
+    for start, (own, other) in zip((0, MISC_AT, FIRST_AT, SECOND_AT), pieces):
         size = own.shape[1]
         mine[:, start : start + size] = own
         theirs[:, start : start + size] = other
@@ -953,7 +958,7 @@
 
 def pack(core, gains, weights):
     rows, width = weights[0].shape
-    shapes = [(rows, SECOND_AT + width)] * 2
+    shapes = [(rows, UP_AT + weights[6].shape[1] // 2)] * 2
     operands = [gain[None, :] for gain in gains] + list(weights)
     return pl.pallas_call(
         pack_kernel,
@@ -1093,7 +1098,8 @@
         ([second_x], [(up_low[None],)], [(0, 0, 0, 0, part)]),
         ([product_x], [(jnp.concatenate(cots, axis=0)[None],)], [(0, 0, 0, 0, width)]),
     ]
-    early = [places[0], after(places[1], (grad_got, normed_x, att_x)), places[2]]
+    late = after(places, (grad_got, normed_x, att_x))
+    early = [places[0], late[1], late[2]]
     sends = [weight_gradient(early[s], core_at, *job)[0] for s, job in enumerate(jobs)]
     gots = exchange(sends, 0)
 
@@ -1113,7 +1119,7 @@
         ([normed_x, att_x], [grads_y, branch_y], [(0, 0, 3, 256, 512), (1, 1, 0, 0, 768)], misc_x),
     ]
     attn_sends = [
-        weight_gradient(after(places[s], gots[s]), core_at, *job)[0]
+        weight_gradient(after(places[s], [gots[t] for t in AHEAD[s]]), core_at, *job)[0]
         for s, job in enumerate(attn_jobs)
     ]
     attn_gots = exchange(attn_sends, 0)
@@ -1125,7 +1131,7 @@
         return [p[0] for p in pairs], [p[1] for p in pairs]
 
     keeps, sends = kept(jobs, gots)
-    gots = exchange([after(send, got) for send, got in zip(sends, attn_gots)], 1)
+    gots = exchange([after(sends[0], attn_gots[0]), *sends[1:]], 1)
     attn_keeps, attn_sends = kept(attn_jobs, [after(got, keeps) for got in attn_gots])
     attn_gots = exchange(attn_sends, 1)
     first, second = list(zip(keeps, gots)), list(zip(attn_keeps, attn_gots))

time: 385 us -> 382 us (level); the launches traced: 385 us -> 377 us
  Pallas kernels: 103 us -> 94.6 us
  local copies, waits for them, and re-layouts: 13.4 us -> 6.66 us
  waiting for transfers between devices: 170 us -> 176 us
    pallas_call x12, Pallas kernels: 33.5 us -> 26.9 us  [weight_gradient(): pl.pallas_call(functools.partial(weight_gradient_kernel, segments, x_coun...]
    unnamed x80 -> x78, local copies, waits for them, and re-layouts: 10.2 us -> 6.43 us
  transfers between devices with their start and end apart: 53 -> 53, of which waited for: 26 -> 28; matrix products, arithmetic and copies ran while one was open for 2% -> 1% of each run, Pallas kernels for 21% -> 19%
where the time goes in v4:
time: 382 us; the launch traced here: 377 us
  waiting for transfers between devices  176 us (46%)
  Pallas kernels  94.6 us (25%)
  starting transfers between devices  78.2 us (20%)
  between operations  15.8 us (4%)
  local copies, waits for them, and re-layouts  6.66 us (2%)
  other arithmetic  5.63 us (1%)
    ppermute x42, waiting for transfers between devices, send_step(): return lax.ppermute(value, 'fsdp', pairs)  98.3 us
    all_gather x1, waiting for transfers between devices, body(): lax.all_gather(slab, 'fsdp', axis=0, tiled=True, axis_index_groups=by_core)  71.2 us
    ppermute x42, starting transfers between devices, send_step(): return lax.ppermute(value, 'fsdp', pairs)  40.6 us
    ppermute x10, starting transfers between devices, swap(): return lax.ppermute(value, 'fsdp', [(d, d ^ 1) for d in range(count)])  37.5 us
    pallas_call x12, Pallas kernels, weight_gradient(): pl.pallas_call(functools.partial(weight_gradient_kernel, segments, x_coun...  26.9 us
    pallas_call x1, Pallas kernels, attention_backward(): pl.pallas_call(attention_backward_kernel, grid=(steps,), in_specs=[rows,...  19.4 us
    pallas_call x1, Pallas kernels, feedforward(): pl.pallas_call(feedforward_kernel, grid_spec=pltpu.PrefetchScalarGridSpec...  16.7 us
    pallas_call x1, Pallas kernels, attention_forward(): pl.pallas_call(attention_forward_kernel, grid_spec=pltpu.PrefetchScalarGr...  16 us
  transfers between devices with their start and end apart: 53, of which 28 were waited for; matrix products, arithmetic and copies ran while one was open for 1% of the time, Pallas kernels for 19%

profile of v4, /device:TPU:1, one launch (start us, length us, event | category | flops | bytes accessed | tf_op | source)
XLA Modules:
  0.0 377.0 jit_solution(13229426671097623747)
XLA Ops:
  21.1 2.8 collective-permute-start.1
  23.9 2.6 collective-permute-start.6
  28.5 4.4 %collective-permute-done.12 = bf16[4,32,512]{2,1,0:T(8,128)(2,1)S(1)} collective-permute-done((bf16[4,32,512]{2,1,0:T(8,128)(2,1)S(1)}, bf16[4,32,512]{2,1,0:T(8,128)(2,1)S(1)}, u32[]{:S(2)}, u32[]{:S(2)}) %collective-permute-start.12) | collective-permute-done | bytes 131104 | tf_op jit(solution)/shard_map/ppermute | solution.py:981
  35.4 5.5 %collective-permute-done.13 = bf16[8,32,512]{2,1,0:T(8,128)(2,1)S(1)} collective-permute-done((bf16[8,32,512]{2,1,0:T(8,128)(2,1)S(1)}, bf16[8,32,512]{2,1,0:T(8,128)(2,1)S(1)}, u32[]{:S(2)}, u32[]{:S(2)}) %collective-permute-start.13) | collective-permute-done | bytes 262176 | tf_op jit(solution)/shard_map/ppermute | solution.py:981
  41.1 2.6 collective-permute-done.8
  44.4 7.8 %collective-permute-done.14 = bf16[16,32,512]{2,1,0:T(8,128)(2,1)S(1)} collective-permute-done((bf16[16,32,512]{2,1,0:T(8,128)(2,1)S(1)}, bf16[16,32,512]{2,1,0:T(8,128)(2,1)S(1)}, u32[]{:S(2)}, u32[]{:S(2)}) %collective-permute-start.14) | collective-permute-done | bytes 524320 | tf_op jit(solution)/shard_map/ppermute | solution.py:981
  57.4 22.9 %collective-permute-start.20 = (bf16[128,1536]{1,0:T(8,128)(2,1)}, bf16[128,1536]{1,0:T(8,128)(2,1)S(1)}, u32[]{:S(2)}, u32[]{:S(2)}) collective-permute-start(bf16[128,1536]{1,0:T(8,128)(2,1)} %bitcast_select_fusion.cot_own_ref.cot_ref), channel_id=1, source_target_pairs={{0,1},{1,0},{2,3},{3,2},{4,5},{5,4},{6,7},{7,6},{8,9},{9,8},{10,11... | collective-permute-start | bytes 1179656 | tf_op jit(solution)/shard_map/ppermute | solution.py:71
  81.6 5.5 %collective-permute-done.16.refs_4_ = bf16[32,32,512]{2,1,0:T(8,128)(2,1)} collective-permute-done((bf16[32,32,512]{2,1,0:T(8,128)(2,1)S(1)}, bf16[32,32,512]{2,1,0:T(8,128)(2,1)}, u32[]{:S(2)}, u32[]{:S(2)}) %collective-permute-start.16) | collective-permute-done | bytes 1048608 | tf_op jit(solution)/shard_map/ppermute | solution.py:981
  87.2 8.1 %in_order.1 = bf16[64,32,1536]{2,1,0:T(8,128)(2,1)} custom-call(s32[3,64]{1,0:T(4,128)} %get-tuple-element.111.place_ref, bf16[32,32,512]{2,1,0:T(8,128)(2,1)} %copy-done.20, bf16[32,32,512]{2,1,0:T(8,128)(2,1)} %copy-done.21, bf16[32,32,512]{2,1,0:T(8,128)(2,1)} %copy-done.22, bf16[32,32,512]{2,1,0:T(8,128)(2,1)} %collective-permute-done.15.refs_3_, ...), custom_call_target="tpu_custom_call" | custom-call | flops 1 | bytes 1 | tf_op jit(solution)/shard_map/in_order/pallas_call | solution.py:1018
  95.3 71.2 %all-gather.2.cloned.1.call-done.wq_ref.wk_ref.wv_ref.wh_ref.out_lo_ref.out_hi_ref.misc_ref.wg_ref.wu_ref.wo_lo_ref.wo_hi_ref = bf16[3072,8192]{1,0:T(8,128)(2,1)} async-done(((bf16[24,8192]{1,0:T(8,128)(2,1)}), bf16[3072,8192]{1,0:T(8,128)(2,1)}) %all-gather.2.cloned.1.call-update) | async-done | bytes 50331664 | tf_op jit(solution)/shard_map/all_gather | solution.py:1073
  166.5 16.0 %attention_forward.1 = (bf16[1536,128]{1,0:T(8,128)(2,1)}, bf16[128,1536]{1,0:T(8,128)(2,1)}, bf16[128,1536]{1,0:T(8,128)(2,1)}, bf16[128,1536]{1,0:T(8,128)(2,1...) custom-call(s32[1]{0:T(128)} %copy.55.length_ref, ...), custom_call_target="tpu_custom_call" | custom-call | flops 5435817984 | bytes 23592960 | tf_op jit(solution)/shard_map/attention_forward/pallas_call | solution.py:226
  185.3 16.7 %feedforward.1 = (bf16[1536,256]{1,0:T(8,128)(2,1)}, bf16[2048,256]{1,0:T(8,128)(2,1)}, bf16[256,2048]{1,0:T(8,128)(2,1)}, bf16[256,2048]{1,0:T(8,128)(2,1)}, f3...) custom-call(s32[1]{0:T(128)} %bitcast.7.core_ref.refs_1_, ...), custom_call_target="tpu_custom_call" | custom-call | flops 9663676416 | bytes 18874368 | tf_op jit(solution)/shard_map/feedforward/pallas_call | solution.py:352
  205.2 2.9 weight_gradient.6
  212.2 2.9 weight_gradient.8
  217.6 2.9 weight_gradient.7
  221.2 19.4 %attention_backward.1 = (bf16[4,128,1536]{2,1,0:T(8,128)(2,1)}, bf16[128,1536]{1,0:T(8,128)(2,1)}, f32[128,1536]{1,0:T(8,128)}, bf16[1536,128]{1,0:T(8,128)(2,1)}) custom-call(bf16[128,1536]{1,0:T(8,128)(2,1)} %bitcast.91, bf16[1536,128]{1,0:T(8,128)(2,1)} %get-tuple-element.105.normed_t_ref, f32[1,1536]{1,0:T(1,128)} %get-tuple-element.106.gain_ref, ...), custom_call_target="tpu_custom_call" | custom-call | flops 1 | bytes 1 | tf_op jit(solution)/shard_map/attention_backward/pallas_call | solution.py:562
  241.6 3.2 collective-permute-done.26.refs_5_.refs_7_
  249.6 3.1 collective-permute-done.30.refs_4_.refs_5_
  254.4 2.6 collective-permute-start.37
  263.1 3.2 weight_gradient_add.7
  267.4 3.1 weight_gradient_add.8
  274.6 7.4 %collective-permute-done.37.refs_11_.refs_12_ = bf16[32,24,1408]{2,1,0:T(8,128)(2,1)S(1)} collective-permute-done((bf16[32,24,1408]{2,1,0:T(8,128)(2,1)S(1)}, bf16[32,24,1408]{2,1,0:T(8,128)(2,1)S(1)}, u32[]{:S(2)}, u32[]{:S(2)}) %collective-permute-start.37) | collective-permute-done | bytes 2162720 | tf_op jit(solution)/shard_map/ppermute | solution.py:981
  283.6 7.4 %collective-permute-done.33.refs_6_.refs_7_ = bf16[32,24,1280]{2,1,0:T(8,128)(2,1)S(1)} collective-permute-done((bf16[32,24,1280]{2,1,0:T(8,128)(2,1)}, bf16[32,24,1280]{2,1,0:T(8,128)(2,1)S(1)}, u32[]{:S(2)}, u32[]{:S(2)}) %collective-permute-start.33) | collective-permute-done | bytes 1966112 | tf_op jit(solution)/shard_map/ppermute | solution.py:981
  292.9 7.4 %collective-permute-done.32.refs_10_.refs_11_ = bf16[16,24,2048]{2,1,0:T(8,128)(2,1)S(1)} collective-permute-done((bf16[16,24,2048]{2,1,0:T(8,128)(2,1)S(1)}, bf16[16,24,2048]{2,1,0:T(8,128)(2,1)S(1)}, u32[]{:S(2)}, u32[]{:S(2)}) %collective-permute-start.32) | collective-permute-done | bytes 1572896 | tf_op jit(solution)/shard_map/ppermute | solution.py:981
  300.4 3.8 %collective-permute-done.28.refs_2_.refs_3_ = bf16[16,24,2048]{2,1,0:T(8,128)(2,1)S(1)} collective-permute-done((bf16[16,24,2048]{2,1,0:T(8,128)(2,1)S(1)}, bf16[16,24,2048]{2,1,0:T(8,128)(2,1)S(1)}, u32[]{:S(2)}, u32[]{:S(2)}) %collective-permute-start.28) | collective-permute-done | bytes 1572896 | tf_op jit(solution)/shard_map/ppermute | solution.py:981
  304.2 6.7 %collective-permute-done.34.refs_14_.refs_15_ = bf16[16,24,1280]{2,1,0:T(8,128)(2,1)S(1)} collective-permute-done((bf16[16,24,1280]{2,1,0:T(8,128)(2,1)S(1)}, bf16[16,24,1280]{2,1,0:T(8,128)(2,1)S(1)}, u32[]{:S(2)}, u32[]{:S(2)}) %collective-permute-start.34) | collective-permute-done | bytes 983072 | tf_op jit(solution)/shard_map/ppermute | solution.py:981
  316.9 15.0 %collective-permute-done.39.refs_2_.refs_3_ = bf16[8,24,3328]{2,1,0:T(8,128)(2,1)S(1)} collective-permute-done((bf16[8,24,3328]{2,1,0:T(8,128)(2,1)S(1)}, bf16[8,24,3328]{2,1,0:T(8,128)(2,1)S(1)}, u32[]{:S(2)}, u32[]{:S(2)}) %collective-permute-start.39) | collective-permute-done | bytes 1277984 | tf_op jit(solution)/shard_map/ppermute | solution.py:981
  333.7 4.3 %collective-permute-start.21 = (f32[128,1536]{1,0:T(8,128)S(1)}, f32[128,1536]{1,0:T(8,128)S(1)}, u32[]{:S(2)}, u32[]{:S(2)}) collective-permute-start(f32[128,1536]{1,0:T(8,128)S(1)} %copy-done.33), channel_id=1, source_target_pairs={{0,1},{1,0},{2,3},{3,2},{4,5},{5,4},{6,7},{7,6},{8,9},{9,8},{10,11... | collective-permute-start | bytes 2359304 | tf_op jit(solution)/shard_map/ppermute | solution.py:71
  338.1 5.2 %collective-permute-done.42.refs_2_.refs_3_ = bf16[4,24,3328]{2,1,0:T(8,128)(2,1)S(1)} collective-permute-done((bf16[4,24,3328]{2,1,0:T(8,128)(2,1)S(1)}, bf16[4,24,3328]{2,1,0:T(8,128)(2,1)S(1)}, u32[]{:S(2)}, u32[]{:S(2)}) %collective-permute-start.42) | collective-permute-done | bytes 639008 | tf_op jit(solution)/shard_map/ppermute | solution.py:981
  348.9 4.3 %collective-permute-done.45.refs_2_.refs_3_ = bf16[2,24,3328]{2,1,0:T(8,128)(2,1)S(1)} collective-permute-done((bf16[2,24,3328]{2,1,0:T(8,128)(2,1)S(1)}, bf16[2,24,3328]{2,1,0:T(8,128)(2,1)S(1)}, u32[]{:S(2)}, u32[]{:S(2)}) %collective-permute-start.45) | collective-permute-done | bytes 319520 | tf_op jit(solution)/shard_map/ppermute | solution.py:981
  356.0 3.9 %collective-permute-done.48.refs_1_ = bf16[1,24,3328]{2,1,0:T(8,128)(2,1)S(1)} collective-permute-done((bf16[1,24,3328]{2,1,0:T(8,128)(2,1)S(1)}, bf16[1,24,3328]{2,1,0:T(8,128)(2,1)S(1)}, u32[]{:S(2)}, u32[]{:S(2)}) %collective-permute-start.48) | collective-permute-done | bytes 159776 | tf_op jit(solution)/shard_map/ppermute | solution.py:981
  360.6 6.6 %collective-permute-start.51 = (bf16[12,8192]{1,0:T(8,128)(2,1)S(1)}, bf16[12,8192]{1,0:T(8,128)(2,1)S(1)}, u32[]{:S(2)}, u32[]{:S(2)}) collective-permute-start(bf16[12,8192]{1,0:T(8,128)(2,1)S(1)} %get-tuple-element.171), channel_id=1, source_target_pairs={{0,1},{1,0},{2,3},{3,2},{4,5},{5,4},{6,7},{7,6},{8,9},{9,8},{10,11... | collective-permute-start | bytes 589832 | tf_op jit(solution)/shard_map/ppermute | solution.py:71
  (200 shorter events, 79.7 us)
Async XLA Ops:
  7.2 159.3 %all-gather.2.cloned.1.call-start = ((), (), s32[]{:S(2)}) async-start(), calls=%async_computation | async-start | bytes 50724864 | tf_op jit(solution)/shard_map/all_gather | solution.py:1073
  33.0 10.8 %collective-permute-start.3 = (bf16[8,32,512]{2,1,0:T(8,128)(2,1)S(1)}, bf16[8,32,512]{2,1,0:T(8,128)(2,1)S(1)}, u32[]{:S(2)}, u32[]{:S(2)}) collective-permute-start(bf16[8,32,512]{2,1,0:T(8,128)(2,1)S(1)} %pad_maximum_fusion), channel_id=1, source_target_pairs={{0,8},{1,25},{2,10},{3,27},{4,12},{5,29},{6,14},{7,31},{8,0},{9,17... | collective-permute-start | bytes 786440 | tf_op jit(solution)/shard_map/ppermute | solution.py:981
  33.3 10.4 %collective-permute-start.8 = (bf16[8,32,512]{2,1,0:T(8,128)(2,1)S(1)}, bf16[8,32,512]{2,1,0:T(8,128)(2,1)S(1)}, u32[]{:S(2)}, u32[]{:S(2)}) collective-permute-start(bf16[8,32,512]{2,1,0:T(8,128)(2,1)S(1)} %pad_maximum_fusion.1), channel_id=1, source_target_pairs={{0,2},{1,7},{2,0},{3,5},{4,6},{5,3},{6,4},{7,1},{8,10},{9,15},{10,... | collective-permute-start | bytes 786440 | tf_op jit(solution)/shard_map/ppermute | solution.py:981
  41.0 11.2 %collective-permute-start.14 = (bf16[16,32,512]{2,1,0:T(8,128)(2,1)S(1)}, bf16[16,32,512]{2,1,0:T(8,128)(2,1)S(1)}, u32[]{:S(2)}, u32[]{:S(2)}) collective-permute-start(bf16[16,32,512]{2,1,0:T(8,128)(2,1)S(1)} %get-tuple-element.183), channel_id=1, source_target_pairs={{0,6},{1,3},{2,4},{3,1},{4,2},{5,7},{6,0},{7,5},{8,14},{9,11},{10,... | collective-permute-start | bytes 1572872 | tf_op jit(solution)/shard_map/ppermute | solution.py:981
  43.7 8.8 %collective-permute-start.9 = (bf16[16,32,512]{2,1,0:T(8,128)(2,1)S(1)}, bf16[16,32,512]{2,1,0:T(8,128)(2,1)S(1)}, u32[]{:S(2)}, u32[]{:S(2)}) collective-permute-start(bf16[16,32,512]{2,1,0:T(8,128)(2,1)S(1)} %get-tuple-element.185), channel_id=1, source_target_pairs={{0,24},{1,9},{2,26},{3,11},{4,28},{5,13},{6,30},{7,15},{8,16},{9,1... | collective-permute-start | bytes 1572872 | tf_op jit(solution)/shard_map/ppermute | solution.py:981
  43.9 10.1 %collective-permute-start.4 = (bf16[16,32,512]{2,1,0:T(8,128)(2,1)S(1)}, bf16[16,32,512]{2,1,0:T(8,128)(2,1)S(1)}, u32[]{:S(2)}, u32[]{:S(2)}) collective-permute-start(bf16[16,32,512]{2,1,0:T(8,128)(2,1)S(1)} %get-tuple-element.187), channel_id=1, source_target_pairs={{0,96},{1,33},{2,98},{3,35},{4,100},{5,37},{6,102},{7,39},{8,104},... | collective-permute-start | bytes 1572872 | tf_op jit(solution)/shard_map/ppermute | solution.py:981
  52.3 29.4 %collective-permute-start.17 = (bf16[32,32,512]{2,1,0:T(8,128)(2,1)S(1)}, bf16[32,32,512]{2,1,0:T(8,128)(2,1)}, u32[]{:S(2)}, u32[]{:S(2)}) collective-permute-start(bf16[32,32,512]{2,1,0:T(8,128)(2,1)S(1)} %constant_dynamic-update-slice_fusion.27.refs_2_), channel_id=1, source_target_pairs={{0,2},{1,7},{2,0},{3,5},{4,6},{5,3},{6,4},{7,1},{8,10},{9,15},{10,... | collective-permute-start | bytes 3145736 | tf_op jit(solution)/shard_map/ppermute | solution.py:981
  52.6 34.6 %collective-permute-start.16 = (bf16[32,32,512]{2,1,0:T(8,128)(2,1)S(1)}, bf16[32,32,512]{2,1,0:T(8,128)(2,1)}, u32[]{:S(2)}, u32[]{:S(2)}) collective-permute-start(bf16[32,32,512]{2,1,0:T(8,128)(2,1)S(1)} %constant_dynamic-update-slice_fusion.16.refs_1_), channel_id=1, source_target_pairs={{0,8},{1,25},{2,10},{3,27},{4,12},{5,29},{6,14},{7,31},{8,0},{9,17... | collective-permute-start | bytes 3145736 | tf_op jit(solution)/shard_map/ppermute | solution.py:981
  54.0 33.2 %collective-permute-start.15 = (bf16[32,32,512]{2,1,0:T(8,128)(2,1)S(1)}, bf16[32,32,512]{2,1,0:T(8,128)(2,1)}, u32[]{:S(2)}, u32[]{:S(2)}) collective-permute-start(bf16[32,32,512]{2,1,0:T(8,128)(2,1)S(1)} %constant_dynamic-update-slice_fusion.5.refs_0_), channel_id=1, source_target_pairs={{0,32},{1,97},{2,34},{3,99},{4,36},{5,101},{6,38},{7,103},{8,40},{... | collective-permute-start | bytes 3145736 | tf_op jit(solution)/shard_map/ppermute | solution.py:981
  57.4 125.4 %collective-permute-start.20 = (bf16[128,1536]{1,0:T(8,128)(2,1)}, bf16[128,1536]{1,0:T(8,128)(2,1)S(1)}, u32[]{:S(2)}, u32[]{:S(2)}) collective-permute-start(bf16[128,1536]{1,0:T(8,128)(2,1)} %bitcast_select_fusion.cot_own_ref.cot_ref), channel_id=1, source_target_pairs={{0,1},{1,0},{2,3},{3,2},{4,5},{5,4},{6,7},{7,6},{8,9},{9,8},{10,11... | collective-permute-start | bytes 1179656 | tf_op jit(solution)/shard_map/ppermute | solution.py:71
  202.0 9.4 %collective-permute-start.22 = (f32[128,1536]{1,0:T(8,128)}, f32[128,1536]{1,0:T(8,128)S(1)}, u32[]{:S(2)}, u32[]{:S(2)}) collective-permute-start(f32[128,1536]{1,0:T(8,128)} %get-tuple-element.109), channel_id=1, source_target_pairs={{0,1},{1,0},{2,3},{3,2},{4,5},{5,4},{6,7},{7,6},{8,9},{9,8},{10,11... | collective-permute-start | bytes 2359304 | tf_op jit(solution)/shard_map/ppermute | solution.py:71
  208.1 41.5 %collective-permute-start.25 = (bf16[32,24,2048]{2,1,0:T(8,128)(2,1)}, bf16[32,24,2048]{2,1,0:T(8,128)(2,1)S(1)}, u32[]{:S(2)}, u32[]{:S(2)}) collective-permute-start(bf16[32,24,2048]{2,1,0:T(8,128)(2,1)} %weight_gradient.6), channel_id=1, source_target_pairs={{0,32},{1,97},{2,34},{3,99},{4,36},{5,101},{6,38},{7,103},{8,40},{... | collective-permute-start | bytes 9437192 | tf_op jit(solution)/shard_map/ppermute | solution.py:981
  215.1 37.6 %collective-permute-start.30 = (bf16[32,32,1536]{2,1,0:T(8,128)(2,1)}, bf16[32,32,1536]{2,1,0:T(8,128)(2,1)}, u32[]{:S(2)}, u32[]{:S(2)}) collective-permute-start(bf16[32,32,1536]{2,1,0:T(8,128)(2,1)} %weight_gradient.8), channel_id=1, source_target_pairs={{0,2},{1,7},{2,0},{3,5},{4,6},{5,3},{6,4},{7,1},{8,10},{9,15},{10,... | collective-permute-start | bytes 9437192 | tf_op jit(solution)/shard_map/ppermute | solution.py:981
  220.5 37.8 %collective-permute-start.29 = (bf16[32,24,2048]{2,1,0:T(8,128)(2,1)}, bf16[32,24,2048]{2,1,0:T(8,128)(2,1)}, u32[]{:S(2)}, u32[]{:S(2)}) collective-permute-start(bf16[32,24,2048]{2,1,0:T(8,128)(2,1)} %weight_gradient.7), channel_id=1, source_target_pairs={{0,8},{1,25},{2,10},{3,27},{4,12},{5,29},{6,14},{7,31},{8,0},{9,17... | collective-permute-start | bytes 9437192 | tf_op jit(solution)/shard_map/ppermute | solution.py:981
  241.5 11.2 %collective-permute-start.36 = (bf16[128,1536]{1,0:T(8,128)(2,1)}, bf16[128,1536]{1,0:T(8,128)(2,1)S(1)}, u32[]{:S(2)}, u32[]{:S(2)}) collective-permute-start(bf16[128,1536]{1,0:T(8,128)(2,1)} %get-tuple-element.140), channel_id=1, source_target_pairs={{0,1},{1,0},{2,3},{3,2},{4,5},{5,4},{6,7},{7,6},{8,9},{9,8},{10,11... | collective-permute-start | bytes 1179656 | tf_op jit(solution)/shard_map/ppermute | solution.py:71
  247.8 24.8 %collective-permute-start.27 = (bf16[32,24,1280]{2,1,0:T(8,128)(2,1)S(1)}, bf16[32,24,1280]{2,1,0:T(8,128)(2,1)S(1)}, u32[]{:S(2)}, u32[]{:S(2)}) collective-permute-start(bf16[32,24,1280]{2,1,0:T(8,128)(2,1)S(1)} %weight_gradient.9), channel_id=1, source_target_pairs={{0,32},{1,97},{2,34},{3,99},{4,36},{5,101},{6,38},{7,103},{8,40},{... | collective-permute-start | bytes 5898248 | tf_op jit(solution)/shard_map/ppermute | solution.py:981
  254.4 27.6 %collective-permute-start.37 = (bf16[32,24,1408]{2,1,0:T(8,128)(2,1)S(1)}, bf16[32,24,1408]{2,1,0:T(8,128)(2,1)S(1)}, u32[]{:S(2)}, u32[]{:S(2)}) collective-permute-start(bf16[32,24,1408]{2,1,0:T(8,128)(2,1)S(1)} %weight_gradient.11), channel_id=1, source_target_pairs={{0,2},{1,7},{2,0},{3,5},{4,6},{5,3},{6,4},{7,1},{8,10},{9,15},{10,... | collective-permute-start | bytes 6488072 | tf_op jit(solution)/shard_map/ppermute | solution.py:981
  260.8 30.2 %collective-permute-start.33 = (bf16[32,24,1280]{2,1,0:T(8,128)(2,1)}, bf16[32,24,1280]{2,1,0:T(8,128)(2,1)S(1)}, u32[]{:S(2)}, u32[]{:S(2)}) collective-permute-start(bf16[32,24,1280]{2,1,0:T(8,128)(2,1)} %weight_gradient.10), channel_id=1, source_target_pairs={{0,8},{1,25},{2,10},{3,27},{4,12},{5,29},{6,14},{7,31},{8,0},{9,17... | collective-permute-start | bytes 5898248 | tf_op jit(solution)/shard_map/ppermute | solution.py:981
  274.0 18.8 %collective-permute-start.31 = (bf16[16,24,1280]{2,1,0:T(8,128)(2,1)S(1)}, bf16[16,24,1280]{2,1,0:T(8,128)(2,1)S(1)}, u32[]{:S(2)}, u32[]{:S(2)}) collective-permute-start(bf16[16,24,1280]{2,1,0:T(8,128)(2,1)S(1)} %get-tuple-element.133), channel_id=1, source_target_pairs={{0,96},{1,33},{2,98},{3,35},{4,100},{5,37},{6,102},{7,39},{8,104},... | collective-permute-start | bytes 2949128 | tf_op jit(solution)/shard_map/ppermute | solution.py:981
  274.1 26.2 %collective-permute-start.32 = (bf16[16,24,2048]{2,1,0:T(8,128)(2,1)S(1)}, bf16[16,24,2048]{2,1,0:T(8,128)(2,1)S(1)}, u32[]{:S(2)}, u32[]{:S(2)}) collective-permute-start(bf16[16,24,2048]{2,1,0:T(8,128)(2,1)S(1)} %copy-done.17), channel_id=1, source_target_pairs={{0,24},{1,9},{2,26},{3,11},{4,28},{5,13},{6,30},{7,15},{8,16},{9,1... | collective-permute-start | bytes 4718600 | tf_op jit(solution)/shard_map/ppermute | solution.py:981
  274.2 26.1 %collective-permute-start.35 = (bf16[16,32,1536]{2,1,0:T(8,128)(2,1)S(1)}, bf16[16,32,1536]{2,1,0:T(8,128)(2,1)S(1)}, u32[]{:S(2)}, u32[]{:S(2)}) collective-permute-start(bf16[16,32,1536]{2,1,0:T(8,128)(2,1)S(1)} %get-tuple-element.139), channel_id=1, source_target_pairs={{0,6},{1,3},{2,4},{3,1},{4,2},{5,7},{6,0},{7,5},{8,14},{9,11},{10,... | collective-permute-start | bytes 4718600 | tf_op jit(solution)/shard_map/ppermute | solution.py:981
  282.0 22.2 %collective-permute-start.28 = (bf16[16,24,2048]{2,1,0:T(8,128)(2,1)S(1)}, bf16[16,24,2048]{2,1,0:T(8,128)(2,1)S(1)}, u32[]{:S(2)}, u32[]{:S(2)}) collective-permute-start(bf16[16,24,2048]{2,1,0:T(8,128)(2,1)S(1)} %get-tuple-element.128), channel_id=1, source_target_pairs={{0,96},{1,33},{2,98},{3,35},{4,100},{5,37},{6,102},{7,39},{8,104},... | collective-permute-start | bytes 4718600 | tf_op jit(solution)/shard_map/ppermute | solution.py:981
  291.0 19.9 %collective-permute-start.38 = (bf16[16,24,1408]{2,1,0:T(8,128)(2,1)S(1)}, bf16[16,24,1408]{2,1,0:T(8,128)(2,1)S(1)}, u32[]{:S(2)}, u32[]{:S(2)}) collective-permute-start(bf16[16,24,1408]{2,1,0:T(8,128)(2,1)S(1)} %get-tuple-element.145), channel_id=1, source_target_pairs={{0,6},{1,3},{2,4},{3,1},{4,2},{5,7},{6,0},{7,5},{8,14},{9,11},{10,... | collective-permute-start | bytes 3244040 | tf_op jit(solution)/shard_map/ppermute | solution.py:981
  292.8 18.1 %collective-permute-start.34 = (bf16[16,24,1280]{2,1,0:T(8,128)(2,1)S(1)}, bf16[16,24,1280]{2,1,0:T(8,128)(2,1)S(1)}, u32[]{:S(2)}, u32[]{:S(2)}) collective-permute-start(bf16[16,24,1280]{2,1,0:T(8,128)(2,1)S(1)} %get-tuple-element.138), channel_id=1, source_target_pairs={{0,24},{1,9},{2,26},{3,11},{4,28},{5,13},{6,30},{7,15},{8,16},{9,1... | collective-permute-start | bytes 2949128 | tf_op jit(solution)/shard_map/ppermute | solution.py:981
  312.7 19.7 %collective-permute-start.41 = (bf16[8,32,2688]{2,1,0:T(8,128)(2,1)S(1)}, bf16[8,32,2688]{2,1,0:T(8,128)(2,1)S(1)}, u32[]{:S(2)}, u32[]{:S(2)}) collective-permute-start(bf16[8,32,2688]{2,1,0:T(8,128)(2,1)S(1)} %get-tuple-element.151), channel_id=1, source_target_pairs={{0,32},{1,97},{2,34},{3,99},{4,36},{5,101},{6,38},{7,103},{8,40},{... | collective-permute-start | bytes 4128776 | tf_op jit(solution)/shard_map/ppermute | solution.py:981
  314.6 17.3 %collective-permute-start.39 = (bf16[8,24,3328]{2,1,0:T(8,128)(2,1)S(1)}, bf16[8,24,3328]{2,1,0:T(8,128)(2,1)S(1)}, u32[]{:S(2)}, u32[]{:S(2)}) collective-permute-start(bf16[8,24,3328]{2,1,0:T(8,128)(2,1)S(1)} %get-tuple-element.147), channel_id=1, source_target_pairs={{0,8},{1,25},{2,10},{3,27},{4,12},{5,29},{6,14},{7,31},{8,0},{9,17... | collective-permute-start | bytes 3833864 | tf_op jit(solution)/shard_map/ppermute | solution.py:981
  315.1 17.3 %collective-permute-start.40 = (bf16[8,24,3328]{2,1,0:T(8,128)(2,1)S(1)}, bf16[8,24,3328]{2,1,0:T(8,128)(2,1)S(1)}, u32[]{:S(2)}, u32[]{:S(2)}) collective-permute-start(bf16[8,24,3328]{2,1,0:T(8,128)(2,1)S(1)} %get-tuple-element.149), channel_id=1, source_target_pairs={{0,2},{1,7},{2,0},{3,5},{4,6},{5,3},{6,4},{7,1},{8,10},{9,15},{10,... | collective-permute-start | bytes 3833864 | tf_op jit(solution)/shard_map/ppermute | solution.py:981
  333.3 10.2 %collective-permute-start.44 = (bf16[4,32,2688]{2,1,0:T(8,128)(2,1)S(1)}, bf16[4,32,2688]{2,1,0:T(8,128)(2,1)S(1)}, u32[]{:S(2)}, u32[]{:S(2)}) collective-permute-start(bf16[4,32,2688]{2,1,0:T(8,128)(2,1)S(1)} %get-tuple-element.157), channel_id=1, source_target_pairs={{0,96},{1,33},{2,98},{3,35},{4,100},{5,37},{6,102},{7,39},{8,104},... | collective-permute-start | bytes 2064392 | tf_op jit(solution)/shard_map/ppermute | solution.py:981
  333.7 9.6 %collective-permute-start.42 = (bf16[4,24,3328]{2,1,0:T(8,128)(2,1)S(1)}, bf16[4,24,3328]{2,1,0:T(8,128)(2,1)S(1)}, u32[]{:S(2)}, u32[]{:S(2)}) collective-permute-start(bf16[4,24,3328]{2,1,0:T(8,128)(2,1)S(1)} %get-tuple-element.153), channel_id=1, source_target_pairs={{0,24},{1,9},{2,26},{3,11},{4,28},{5,13},{6,30},{7,15},{8,16},{9,1... | collective-permute-start | bytes 1916936 | tf_op jit(solution)/shard_map/ppermute | solution.py:981
  333.7 9.6 %collective-permute-start.43 = (bf16[4,24,3328]{2,1,0:T(8,128)(2,1)S(1)}, bf16[4,24,3328]{2,1,0:T(8,128)(2,1)S(1)}, u32[]{:S(2)}, u32[]{:S(2)}) collective-permute-start(bf16[4,24,3328]{2,1,0:T(8,128)(2,1)S(1)} %get-tuple-element.155), channel_id=1, source_target_pairs={{0,6},{1,3},{2,4},{3,1},{4,2},{5,7},{6,0},{7,5},{8,14},{9,11},{10,... | collective-permute-start | bytes 1916936 | tf_op jit(solution)/shard_map/ppermute | solution.py:981
  333.7 33.5 %collective-permute-start.21 = (f32[128,1536]{1,0:T(8,128)S(1)}, f32[128,1536]{1,0:T(8,128)S(1)}, u32[]{:S(2)}, u32[]{:S(2)}) collective-permute-start(f32[128,1536]{1,0:T(8,128)S(1)} %copy-done.33), channel_id=1, source_target_pairs={{0,1},{1,0},{2,3},{3,2},{4,5},{5,4},{6,7},{7,6},{8,9},{9,8},{10,11... | collective-permute-start | bytes 2359304 | tf_op jit(solution)/shard_map/ppermute | solution.py:71
  344.0 10.8 %collective-permute-start.47 = (bf16[2,32,2688]{2,1,0:T(8,128)(2,1)S(1)}, bf16[2,32,2688]{2,1,0:T(8,128)(2,1)S(1)}, u32[]{:S(2)}, u32[]{:S(2)}) collective-permute-start(bf16[2,32,2688]{2,1,0:T(8,128)(2,1)S(1)} %get-tuple-element.163), channel_id=1, source_target_pairs={{0,8},{1,25},{2,10},{3,27},{4,12},{5,29},{6,14},{7,31},{8,0},{9,17... | collective-permute-start | bytes 1032200 | tf_op jit(solution)/shard_map/ppermute | solution.py:981
  (55 other events, 482.4 us)
Sparse Core Ops, SparseCore 0:
  14.4 152.0 all-gather.1

commit v5 on v4

--- a/solution.py
+++ b/solution.py
@@ -106,7 +106,9 @@
 
 PER_STEP = 6
 SPAN = 128 * PER_STEP
-FIRST_AT, SECOND_AT, MISC_AT, GATE_AT, UP_AT = 768, 2304, 3840, 4096, 6144
+BACK_STEP = 3
+BACK_SPAN = 128 * BACK_STEP
+FIRST_AT, SECOND_AT, GATE_AT, UP_AT, MISC_AT = 768, 2304, 3840, 5888, 7936
 
 
 def attention_forward_kernel(
@@ -280,7 +282,7 @@
     )(length, tokens, attn, attn, attn, attn, attn, attn, attn)
 
 
-FF_BLOCK = 512
+FF_BLOCK = 256
 
 
 def feedforward_kernel(
@@ -374,7 +376,7 @@
             sums,
             sums,
         ],
-        compiler_params=pltpu.CompilerParams(vmem_limit_bytes=58 * MIB),
+        compiler_params=pltpu.CompilerParams(vmem_limit_bytes=46 * MIB),
         cost_estimate=pl.CostEstimate(
             flops=24 * count * width * units,
             bytes_accessed=6 * width * units,
@@ -444,7 +446,7 @@
     upto = row >= col
     raw = beta_ref[...]
     lane = lax.broadcasted_iota(jnp.int32, raw.shape, 1)
-    heads = range(PER_STEP)
+    heads = range(BACK_STEP)
     part = lambda ref: [ref[:, 128 * i : 128 * (i + 1)] for i in heads]
     q, k, v, h = part(q_ref), part(k_ref), part(v_ref), part(h_ref)
     att_grad = [att_grad_all[:, 128 * i : 128 * (i + 1)] for i in heads]
@@ -478,7 +480,7 @@
     for i in heads:
         house = h[i].astype(F32)
         inverse_square = 1.0 / (jnp.sum(house * house, axis=1, keepdims=True) + EPSILON)
-        sigma = jax.nn.sigmoid(beta_of(raw, at * PER_STEP + i))
+        sigma = jax.nn.sigmoid(beta_of(raw, at * BACK_STEP + i))
         strength = 2.0 * sigma * inverse_square
         key_part = (strength * source_grad[i]).astype(BF)
         self_part = (strength * system_grad[i]).astype(BF)
@@ -503,7 +505,7 @@
         h_grads.append(house_grad.astype(BF))
         v_grads.append(value_grad[i].astype(BF))
         raw_grad = strength_grad * inverse_square * (2.0 * sigma * (1.0 - sigma))
-        total_beta += jnp.where(lane == at * PER_STEP + i, raw_grad, 0.0)
+        total_beta += jnp.where(lane == at * BACK_STEP + i, raw_grad, 0.0)
     beta_grad[...] += total_beta
     update = None
     for index, (pieces, weight_ref) in enumerate(
@@ -551,14 +553,14 @@
 def attention_backward(tokens, normed_t, norm, saved, attn):
     q, k, v, h, probs, carried, inverse, beta = saved
     count, width = tokens.shape
-    steps = width // SPAN
+    steps = width // BACK_SPAN
     half = width // 2
     whole = lambda i: (0, 0)
     rows = pl.BlockSpec((count, width), whole)
-    row_block = pl.BlockSpec((count, SPAN), lambda i: (0, i))
-    cell_block = pl.BlockSpec((PER_STEP, count, count), lambda i: (i, 0, 0))
-    weight = lambda side, first: pl.BlockSpec((width, SPAN), lambda i: (side, first // SPAN + i))
-    out_rows = lambda side: pl.BlockSpec((SPAN, half), lambda i: (side * steps + i, 0))
+    row_block = pl.BlockSpec((count, BACK_SPAN), lambda i: (0, i))
+    cell_block = pl.BlockSpec((BACK_STEP, count, count), lambda i: (i, 0, 0))
+    weight = lambda side, first: pl.BlockSpec((width, BACK_SPAN), lambda i: (side, first // BACK_SPAN + i))
+    out_rows = lambda side: pl.BlockSpec((BACK_SPAN, half), lambda i: (side * steps + i, 0))
     return pl.pallas_call(
         attention_backward_kernel,
         grid=(steps,),
@@ -587,7 +589,7 @@
             pl.BlockSpec((width, 128), lambda i: (0, MISC_AT // 128)),
         ],
         out_specs=[
-            pl.BlockSpec((4, count, SPAN), lambda i: (0, 0, i)),
+            pl.BlockSpec((4, count, BACK_SPAN), lambda i: (0, 0, i)),
             rows,
             rows,
             pl.BlockSpec((width, 128), whole),
@@ -917,12 +919,12 @@
     gains = jnp.concatenate(
         [gain_attn[...].astype(F32), gain_ffn[...].astype(F32), jnp.zeros((6, rows), F32)], axis=0
     )
-    place = lax.broadcasted_iota(jnp.int32, (8, 256), 0)
-    lane = lax.broadcasted_iota(jnp.int32, (8, 256), 1)
+    place = lax.broadcasted_iota(jnp.int32, (8, 128), 0)
+    lane = lax.broadcasted_iota(jnp.int32, (8, 128), 1)
     pick = ((place < 2) & (lane == 12 + place)).astype(F32)
     misc = dot_tn(gains.astype(BF), pick.astype(BF))
     beta = w_beta[...].astype(F32)
-    misc += jnp.concatenate([beta, jnp.zeros((rows, 256 - beta.shape[1]), F32)], axis=1)
+    misc += jnp.concatenate([beta, jnp.zeros((rows, 128 - beta.shape[1]), F32)], axis=1)
     split = lambda a, b: (jnp.where(first, a, b), jnp.where(first, b, a))
     pieces = [
         split(w_out[:, :half], w_out[:, half:]),
@@ -958,7 +960,7 @@
 
 def pack(core, gains, weights):
     rows, width = weights[0].shape
-    shapes = [(rows, UP_AT + weights[6].shape[1] // 2)] * 2
+    shapes = [(rows, MISC_AT + 128)] * 2
     operands = [gain[None, :] for gain in gains] + list(weights)
     return pl.pallas_call(
         pack_kernel,

time: 382 us -> 372 us (0.974); the launches traced: 377 us -> 372 us
  starting transfers between devices: 78.2 us -> 72.3 us
    ppermute x42, starting transfers between devices: 40.6 us -> 36.6 us  [send_step(): return lax.ppermute(value, 'fsdp', pairs)]
    unnamed x78 -> x88, local copies, waits for them, and re-layouts: 6.43 us -> 8.08 us
  transfers between devices with their start and end apart: 53 -> 53, of which waited for: 28 -> 26; matrix products, arithmetic and copies ran while one was open for 1% -> 2% of each run, Pallas kernels for 19% -> 20%
where the time goes in v5:
time: 372 us
  waiting for transfers between devices  175 us (47%)
  Pallas kernels  95.1 us (26%)
  starting transfers between devices  72.3 us (19%)
  between operations  15.4 us (4%)
  local copies, waits for them, and re-layouts  9.83 us (3%)
  other arithmetic  3.79 us (1%)
    ppermute x42, waiting for transfers between devices, send_step(): return lax.ppermute(value, 'fsdp', pairs)  99.1 us
    all_gather x1, waiting for transfers between devices, body(): lax.all_gather(slab, 'fsdp', axis=0, tiled=True, axis_index_groups=by_core)  69.7 us
    ppermute x42, starting transfers between devices, send_step(): return lax.ppermute(value, 'fsdp', pairs)  36.6 us
    ppermute x10, starting transfers between devices, swap(): return lax.ppermute(value, 'fsdp', [(d, d ^ 1) for d in range(count)])  35.6 us
    pallas_call x12, Pallas kernels, weight_gradient(): pl.pallas_call(functools.partial(weight_gradient_kernel, segments, x_coun...  28.9 us
    pallas_call x1, Pallas kernels, attention_backward(): pl.pallas_call(attention_backward_kernel, grid=(steps,), in_specs=[rows,...  18.7 us
    pallas_call x1, Pallas kernels, attention_forward(): pl.pallas_call(attention_forward_kernel, grid_spec=pltpu.PrefetchScalarGr...  16.2 us
    pallas_call x1, Pallas kernels, feedforward(): pl.pallas_call(feedforward_kernel, grid_spec=pltpu.PrefetchScalarGridSpec...  15.5 us
  transfers between devices with their start and end apart: 53, of which 26 were waited for; matrix products, arithmetic and copies ran while one was open for 2% of the time, Pallas kernels for 20%

profile of v5, /device:TPU:1, one launch (start us, length us, event | category | flops | bytes accessed | tf_op | source)
XLA Modules:
  0.0 371.7 jit_solution(243240403077521807)
XLA Ops:
  23.9 2.6 collective-permute-start.6
  29.2 4.2 %collective-permute-done.12 = bf16[4,32,512]{2,1,0:T(8,128)(2,1)S(1)} collective-permute-done((bf16[4,32,512]{2,1,0:T(8,128)(2,1)S(1)}, bf16[4,32,512]{2,1,0:T(8,128)(2,1)S(1)}, u32[]{:S(2)}, u32[]{:S(2)}) %collective-permute-start.12) | collective-permute-done | bytes 131104 | tf_op jit(solution)/shard_map/ppermute | solution.py:983
  36.0 5.0 %collective-permute-done.13 = bf16[8,32,512]{2,1,0:T(8,128)(2,1)S(1)} collective-permute-done((bf16[8,32,512]{2,1,0:T(8,128)(2,1)S(1)}, bf16[8,32,512]{2,1,0:T(8,128)(2,1)S(1)}, u32[]{:S(2)}, u32[]{:S(2)}) %collective-permute-start.13) | collective-permute-done | bytes 262176 | tf_op jit(solution)/shard_map/ppermute | solution.py:983
  44.1 10.3 %collective-permute-done.14 = bf16[16,32,512]{2,1,0:T(8,128)(2,1)S(1)} collective-permute-done((bf16[16,32,512]{2,1,0:T(8,128)(2,1)S(1)}, bf16[16,32,512]{2,1,0:T(8,128)(2,1)S(1)}, u32[]{:S(2)}, u32[]{:S(2)}) %collective-permute-start.14) | collective-permute-done | bytes 524320 | tf_op jit(solution)/shard_map/ppermute | solution.py:983
  58.0 21.6 %collective-permute-start.20 = (bf16[128,1536]{1,0:T(8,128)(2,1)S(1)}, bf16[128,1536]{1,0:T(8,128)(2,1)S(1)}, u32[]{:S(2)}, u32[]{:S(2)}) collective-permute-start(bf16[128,1536]{1,0:T(8,128)(2,1)S(1)} %bitcast_select_fusion.cot_own_ref.cot_ref), channel_id=1, source_target_pairs={{0,1},{1,0},{2,3},{3,2},{4,5},{5,4},{6,7},{7,6},{8,9},{9,8},{10,11... | collective-permute-start | bytes 1179656 | tf_op jit(solution)/shard_map/ppermute | solution.py:71
  82.1 4.7 %collective-permute-done.16.refs_4_ = bf16[32,32,512]{2,1,0:T(8,128)(2,1)} collective-permute-done((bf16[32,32,512]{2,1,0:T(8,128)(2,1)S(1)}, bf16[32,32,512]{2,1,0:T(8,128)(2,1)}, u32[]{:S(2)}, u32[]{:S(2)}) %collective-permute-start.16) | collective-permute-done | bytes 1048608 | tf_op jit(solution)/shard_map/ppermute | solution.py:983
  86.8 8.1 %in_order.1 = bf16[64,32,1536]{2,1,0:T(8,128)(2,1)} custom-call(s32[3,64]{1,0:T(4,128)} %get-tuple-element.111.place_ref, bf16[32,32,512]{2,1,0:T(8,128)(2,1)} %copy-done.29, bf16[32,32,512]{2,1,0:T(8,128)(2,1)} %copy-done.30, bf16[32,32,512]{2,1,0:T(8,128)(2,1)} %constant_dynamic-update-slice_fusion.27.refs_2_, ...), custom_call_target="tpu_custom_call" | custom-call | flops 1 | bytes 1 | tf_op jit(solution)/shard_map/in_order/pallas_call | solution.py:1020
  94.9 69.7 %all-gather.2.cloned.1.call-done.wq_ref.wk_ref.wv_ref.wh_ref.out_lo_ref.out_hi_ref.misc_ref.wg_ref.wu_ref.wo_lo_ref.wo_hi_ref = bf16[3072,8064]{1,0:T(8,128)(2,1)} async-done(((bf16[24,8064]{1,0:T(8,128)(2,1)}), bf16[3072,8064]{1,0:T(8,128)(2,1)}) %all-gather.2.cloned.1.call-update) | async-done | bytes 49545232 | tf_op jit(solution)/shard_map/all_gather | solution.py:1075
  164.6 16.2 %attention_forward.1 = (bf16[1536,128]{1,0:T(8,128)(2,1)}, bf16[128,1536]{1,0:T(8,128)(2,1)}, bf16[128,1536]{1,0:T(8,128)(2,1)}, bf16[128,1536]{1,0:T(8,128)(2,1...) custom-call(s32[1]{0:T(128)} %copy.55.length_ref, ...), custom_call_target="tpu_custom_call" | custom-call | flops 5435817984 | bytes 23592960 | tf_op jit(solution)/shard_map/attention_forward/pallas_call | solution.py:228
  183.9 15.5 %feedforward.1 = (bf16[1536,256]{1,0:T(8,128)(2,1)S(1)}, bf16[2048,256]{1,0:T(8,128)(2,1)S(1)}, bf16[256,2048]{1,0:T(8,128)(2,1)S(1)}, bf16[256,2048]{1,0:T(8,12...) custom-call(s32[1]{0:T(128)} %bitcast.7.core_ref.refs_1_, ...), custom_call_target="tpu_custom_call" | custom-call | flops 9663676416 | bytes 18874368 | tf_op jit(solution)/shard_map/feedforward/pallas_call | solution.py:354
  202.0 2.9 weight_gradient.6
  207.5 2.9 weight_gradient.8
  210.4 2.5 collective-permute-start.30
  212.8 3.0 weight_gradient.7
  216.3 18.7 %attention_backward.1 = (bf16[4,128,1536]{2,1,0:T(8,128)(2,1)}, bf16[128,1536]{1,0:T(8,128)(2,1)}, f32[128,1536]{1,0:T(8,128)}, bf16[1536,128]{1,0:T(8,128)(2,1)}) custom-call(bf16[128,1536]{1,0:T(8,128)(2,1)} %bitcast.91, bf16[1536,128]{1,0:T(8,128)(2,1)} %get-tuple-element.105.normed_t_ref, f32[1,1536]{1,0:T(1,128)} %get-tuple-element.106.gain_ref, ...), custom_call_target="tpu_custom_call" | custom-call | flops 1 | bytes 1 | tf_op jit(solution)/shard_map/attention_backward/pallas_call | solution.py:564
  235.6 3.1 collective-permute-done.26.refs_5_.refs_7_
  243.3 4.7 %collective-permute-done.30.refs_4_.refs_5_ = bf16[32,32,1536]{2,1,0:T(8,128)(2,1)} collective-permute-done((bf16[32,32,1536]{2,1,0:T(8,128)(2,1)}, bf16[32,32,1536]{2,1,0:T(8,128)(2,1)}, u32[]{:S(2)}, u32[]{:S(2)}) %collective-permute-start.30) | collective-permute-done | bytes 3145760 | tf_op jit(solution)/shard_map/ppermute | solution.py:983
  249.7 2.5 collective-permute-start.37
  253.5 2.5 weight_gradient.10
  259.3 4.0 %weight_gradient_add.7 = (bf16[16,24,2048]{2,1,0:T(8,128)(2,1)S(1)}, bf16[16,24,2048]{2,1,0:T(8,128)(2,1)}) custom-call(s32[64]{0:T(128)S(1)} %get-tuple-element.135.refs_0_, s32[1]{0:T(128)} %bitcast.7.core_ref.refs_1_, bf16[64,24,256]{2,1,0:T(8,128)(2,1)S(1)} %bitcast.72, bf16[1,256,2048]{2,1,0:T(8,128)(2,1)S(1)} %bitcast.76, ...), custom_call_target="tpu_custom_call" | custom-call | flops 1 | bytes 1 | tf_op jit(solution)/shard_map/weight_gradient_add/pallas_call | solution.py:713
  263.4 4.1 %weight_gradient_add.8 = (bf16[16,32,1536]{2,1,0:T(8,128)(2,1)S(1)}, bf16[16,32,1536]{2,1,0:T(8,128)(2,1)}) custom-call(s32[64]{0:T(128)S(1)} %get-tuple-element.142.refs_0_, s32[1]{0:T(128)} %bitcast.7.core_ref.refs_1_, bf16[64,32,256]{2,1,0:T(8,128)(2,1)S(1)} %bitcast.74, bf16[1,256,1536]{2,1,0:T(8,128)(2,1)S(1)} %maximum_bitcast_fusion.refs_3_, ...), custom_call_target="tpu_custom_call" | custom-call | flops 1 | bytes 1 | tf_op jit(solution)/shard_map/weight_gradient_add/pallas_call | solution.py:713
  269.3 8.6 %collective-permute-done.37.refs_11_.refs_12_ = bf16[32,24,1408]{2,1,0:T(8,128)(2,1)S(1)} collective-permute-done((bf16[32,24,1408]{2,1,0:T(8,128)(2,1)S(1)}, bf16[32,24,1408]{2,1,0:T(8,128)(2,1)S(1)}, u32[]{:S(2)}, u32[]{:S(2)}) %collective-permute-start.37) | collective-permute-done | bytes 2162720 | tf_op jit(solution)/shard_map/ppermute | solution.py:983
  279.6 8.0 %collective-permute-done.33.refs_6_.refs_7_ = bf16[32,24,1280]{2,1,0:T(8,128)(2,1)S(1)} collective-permute-done((bf16[32,24,1280]{2,1,0:T(8,128)(2,1)}, bf16[32,24,1280]{2,1,0:T(8,128)(2,1)S(1)}, u32[]{:S(2)}, u32[]{:S(2)}) %collective-permute-start.33) | collective-permute-done | bytes 1966112 | tf_op jit(solution)/shard_map/ppermute | solution.py:983
  289.3 6.2 %collective-permute-done.32.refs_10_.refs_11_ = bf16[16,24,2048]{2,1,0:T(8,128)(2,1)S(1)} collective-permute-done((bf16[16,24,2048]{2,1,0:T(8,128)(2,1)}, bf16[16,24,2048]{2,1,0:T(8,128)(2,1)S(1)}, u32[]{:S(2)}, u32[]{:S(2)}) %collective-permute-start.32) | collective-permute-done | bytes 1572896 | tf_op jit(solution)/shard_map/ppermute | solution.py:983
  295.5 3.7 %collective-permute-done.28.refs_2_.refs_3_ = bf16[16,24,2048]{2,1,0:T(8,128)(2,1)S(1)} collective-permute-done((bf16[16,24,2048]{2,1,0:T(8,128)(2,1)S(1)}, bf16[16,24,2048]{2,1,0:T(8,128)(2,1)S(1)}, u32[]{:S(2)}, u32[]{:S(2)}) %collective-permute-start.28) | collective-permute-done | bytes 1572896 | tf_op jit(solution)/shard_map/ppermute | solution.py:983
  299.2 6.8 %collective-permute-done.34.refs_14_.refs_15_ = bf16[16,24,1280]{2,1,0:T(8,128)(2,1)S(1)} collective-permute-done((bf16[16,24,1280]{2,1,0:T(8,128)(2,1)S(1)}, bf16[16,24,1280]{2,1,0:T(8,128)(2,1)S(1)}, u32[]{:S(2)}, u32[]{:S(2)}) %collective-permute-start.34) | collective-permute-done | bytes 983072 | tf_op jit(solution)/shard_map/ppermute | solution.py:983
  312.1 15.0 %collective-permute-done.39.refs_2_.refs_3_ = bf16[8,24,3328]{2,1,0:T(8,128)(2,1)S(1)} collective-permute-done((bf16[8,24,3328]{2,1,0:T(8,128)(2,1)S(1)}, bf16[8,24,3328]{2,1,0:T(8,128)(2,1)S(1)}, u32[]{:S(2)}, u32[]{:S(2)}) %collective-permute-start.39) | collective-permute-done | bytes 1277984 | tf_op jit(solution)/shard_map/ppermute | solution.py:983
  328.9 4.4 %collective-permute-start.21 = (f32[128,1536]{1,0:T(8,128)S(1)}, f32[128,1536]{1,0:T(8,128)S(1)}, u32[]{:S(2)}, u32[]{:S(2)}) collective-permute-start(f32[128,1536]{1,0:T(8,128)S(1)} %copy-done.27), channel_id=1, source_target_pairs={{0,1},{1,0},{2,3},{3,2},{4,5},{5,4},{6,7},{7,6},{8,9},{9,8},{10,11... | collective-permute-start | bytes 2359304 | tf_op jit(solution)/shard_map/ppermute | solution.py:71
  333.2 5.2 %collective-permute-done.42.refs_2_.refs_3_ = bf16[4,24,3328]{2,1,0:T(8,128)(2,1)S(1)} collective-permute-done((bf16[4,24,3328]{2,1,0:T(8,128)(2,1)S(1)}, bf16[4,24,3328]{2,1,0:T(8,128)(2,1)S(1)}, u32[]{:S(2)}, u32[]{:S(2)}) %collective-permute-start.42) | collective-permute-done | bytes 639008 | tf_op jit(solution)/shard_map/ppermute | solution.py:983
  344.1 4.3 %collective-permute-done.45.refs_2_.refs_3_ = bf16[2,24,3328]{2,1,0:T(8,128)(2,1)S(1)} collective-permute-done((bf16[2,24,3328]{2,1,0:T(8,128)(2,1)S(1)}, bf16[2,24,3328]{2,1,0:T(8,128)(2,1)S(1)}, u32[]{:S(2)}, u32[]{:S(2)}) %collective-permute-start.45) | collective-permute-done | bytes 319520 | tf_op jit(solution)/shard_map/ppermute | solution.py:983
  351.2 3.9 %collective-permute-done.48.refs_1_ = bf16[1,24,3328]{2,1,0:T(8,128)(2,1)S(1)} collective-permute-done((bf16[1,24,3328]{2,1,0:T(8,128)(2,1)S(1)}, bf16[1,24,3328]{2,1,0:T(8,128)(2,1)S(1)}, u32[]{:S(2)}, u32[]{:S(2)}) %collective-permute-start.48) | collective-permute-done | bytes 159776 | tf_op jit(solution)/shard_map/ppermute | solution.py:983
  355.8 6.6 %collective-permute-start.51 = (bf16[12,8192]{1,0:T(8,128)(2,1)S(1)}, bf16[12,8192]{1,0:T(8,128)(2,1)S(1)}, u32[]{:S(2)}, u32[]{:S(2)}) collective-permute-start(bf16[12,8192]{1,0:T(8,128)(2,1)S(1)} %get-tuple-element.171), channel_id=1, source_target_pairs={{0,1},{1,0},{2,3},{3,2},{4,5},{5,4},{6,7},{7,6},{8,9},{9,8},{10,11... | collective-permute-start | bytes 589832 | tf_op jit(solution)/shard_map/ppermute | solution.py:71
  (210 shorter events, 74.6 us)
Async XLA Ops:
  7.2 157.4 %all-gather.2.cloned.1.call-start = ((), (), s32[]{:S(2)}) async-start(), calls=%async_computation | async-start | bytes 49932288 | tf_op jit(solution)/shard_map/all_gather | solution.py:1075
  19.3 7.9 %collective-permute-start.11 = (bf16[2,32,512]{2,1,0:T(8,128)(2,1)S(1)}, bf16[2,32,512]{2,1,0:T(8,128)(2,1)S(1)}, u32[]{:S(2)}, u32[]{:S(2)}) collective-permute-start(bf16[2,32,512]{2,1,0:T(8,128)(2,1)S(1)} %pad_maximum_fusion.8), channel_id=1, source_target_pairs={{0,8},{1,25},{2,10},{3,27},{4,12},{5,29},{6,14},{7,31},{8,0},{9,17... | collective-permute-start | bytes 196616 | tf_op jit(solution)/shard_map/ppermute | solution.py:983
  33.6 10.4 %collective-permute-start.3 = (bf16[8,32,512]{2,1,0:T(8,128)(2,1)S(1)}, bf16[8,32,512]{2,1,0:T(8,128)(2,1)S(1)}, u32[]{:S(2)}, u32[]{:S(2)}) collective-permute-start(bf16[8,32,512]{2,1,0:T(8,128)(2,1)S(1)} %pad_maximum_fusion), channel_id=1, source_target_pairs={{0,8},{1,25},{2,10},{3,27},{4,12},{5,29},{6,14},{7,31},{8,0},{9,17... | collective-permute-start | bytes 786440 | tf_op jit(solution)/shard_map/ppermute | solution.py:983
  33.7 10.0 %collective-permute-start.8 = (bf16[8,32,512]{2,1,0:T(8,128)(2,1)S(1)}, bf16[8,32,512]{2,1,0:T(8,128)(2,1)S(1)}, u32[]{:S(2)}, u32[]{:S(2)}) collective-permute-start(bf16[8,32,512]{2,1,0:T(8,128)(2,1)S(1)} %pad_maximum_fusion.1), channel_id=1, source_target_pairs={{0,2},{1,7},{2,0},{3,5},{4,6},{5,3},{6,4},{7,1},{8,10},{9,15},{10,... | collective-permute-start | bytes 786440 | tf_op jit(solution)/shard_map/ppermute | solution.py:983
  41.8 12.7 %collective-permute-start.14 = (bf16[16,32,512]{2,1,0:T(8,128)(2,1)S(1)}, bf16[16,32,512]{2,1,0:T(8,128)(2,1)S(1)}, u32[]{:S(2)}, u32[]{:S(2)}) collective-permute-start(bf16[16,32,512]{2,1,0:T(8,128)(2,1)S(1)} %get-tuple-element.183), channel_id=1, source_target_pairs={{0,6},{1,3},{2,4},{3,1},{4,2},{5,7},{6,0},{7,5},{8,14},{9,11},{10,... | collective-permute-start | bytes 1572872 | tf_op jit(solution)/shard_map/ppermute | solution.py:983
  43.8 11.6 %collective-permute-start.9 = (bf16[16,32,512]{2,1,0:T(8,128)(2,1)S(1)}, bf16[16,32,512]{2,1,0:T(8,128)(2,1)S(1)}, u32[]{:S(2)}, u32[]{:S(2)}) collective-permute-start(bf16[16,32,512]{2,1,0:T(8,128)(2,1)S(1)} %get-tuple-element.185), channel_id=1, source_target_pairs={{0,24},{1,9},{2,26},{3,11},{4,28},{5,13},{6,30},{7,15},{8,16},{9,1... | collective-permute-start | bytes 1572872 | tf_op jit(solution)/shard_map/ppermute | solution.py:983
  44.0 11.4 %collective-permute-start.4 = (bf16[16,32,512]{2,1,0:T(8,128)(2,1)S(1)}, bf16[16,32,512]{2,1,0:T(8,128)(2,1)S(1)}, u32[]{:S(2)}, u32[]{:S(2)}) collective-permute-start(bf16[16,32,512]{2,1,0:T(8,128)(2,1)S(1)} %get-tuple-element.187), channel_id=1, source_target_pairs={{0,96},{1,33},{2,98},{3,35},{4,100},{5,37},{6,102},{7,39},{8,104},... | collective-permute-start | bytes 1572872 | tf_op jit(solution)/shard_map/ppermute | solution.py:983
  55.3 26.8 %collective-permute-start.17 = (bf16[32,32,512]{2,1,0:T(8,128)(2,1)}, bf16[32,32,512]{2,1,0:T(8,128)(2,1)}, u32[]{:S(2)}, u32[]{:S(2)}) collective-permute-start(bf16[32,32,512]{2,1,0:T(8,128)(2,1)} %constant_dynamic-update-slice_fusion.27.refs_2_), channel_id=1, source_target_pairs={{0,2},{1,7},{2,0},{3,5},{4,6},{5,3},{6,4},{7,1},{8,10},{9,15},{10,... | collective-permute-start | bytes 3145736 | tf_op jit(solution)/shard_map/ppermute | solution.py:983
  55.4 31.4 %collective-permute-start.16 = (bf16[32,32,512]{2,1,0:T(8,128)(2,1)S(1)}, bf16[32,32,512]{2,1,0:T(8,128)(2,1)}, u32[]{:S(2)}, u32[]{:S(2)}) collective-permute-start(bf16[32,32,512]{2,1,0:T(8,128)(2,1)S(1)} %constant_dynamic-update-slice_fusion.16.refs_1_), channel_id=1, source_target_pairs={{0,8},{1,25},{2,10},{3,27},{4,12},{5,29},{6,14},{7,31},{8,0},{9,17... | collective-permute-start | bytes 3145736 | tf_op jit(solution)/shard_map/ppermute | solution.py:983
  55.5 31.3 %collective-permute-start.15 = (bf16[32,32,512]{2,1,0:T(8,128)(2,1)S(1)}, bf16[32,32,512]{2,1,0:T(8,128)(2,1)}, u32[]{:S(2)}, u32[]{:S(2)}) collective-permute-start(bf16[32,32,512]{2,1,0:T(8,128)(2,1)S(1)} %constant_dynamic-update-slice_fusion.5.refs_0_), channel_id=1, source_target_pairs={{0,32},{1,97},{2,34},{3,99},{4,36},{5,101},{6,38},{7,103},{8,40},{... | collective-permute-start | bytes 3145736 | tf_op jit(solution)/shard_map/ppermute | solution.py:983
  58.0 123.3 %collective-permute-start.20 = (bf16[128,1536]{1,0:T(8,128)(2,1)S(1)}, bf16[128,1536]{1,0:T(8,128)(2,1)S(1)}, u32[]{:S(2)}, u32[]{:S(2)}) collective-permute-start(bf16[128,1536]{1,0:T(8,128)(2,1)S(1)} %bitcast_select_fusion.cot_own_ref.cot_ref), channel_id=1, source_target_pairs={{0,1},{1,0},{2,3},{3,2},{4,5},{5,4},{6,7},{7,6},{8,9},{9,8},{10,11... | collective-permute-start | bytes 1179656 | tf_op jit(solution)/shard_map/ppermute | solution.py:71
  205.0 38.3 %collective-permute-start.25 = (bf16[32,24,2048]{2,1,0:T(8,128)(2,1)}, bf16[32,24,2048]{2,1,0:T(8,128)(2,1)S(1)}, u32[]{:S(2)}, u32[]{:S(2)}) collective-permute-start(bf16[32,24,2048]{2,1,0:T(8,128)(2,1)} %weight_gradient.6), channel_id=1, source_target_pairs={{0,32},{1,97},{2,34},{3,99},{4,36},{5,101},{6,38},{7,103},{8,40},{... | collective-permute-start | bytes 9437192 | tf_op jit(solution)/shard_map/ppermute | solution.py:983
  210.4 37.6 %collective-permute-start.30 = (bf16[32,32,1536]{2,1,0:T(8,128)(2,1)}, bf16[32,32,1536]{2,1,0:T(8,128)(2,1)}, u32[]{:S(2)}, u32[]{:S(2)}) collective-permute-start(bf16[32,32,1536]{2,1,0:T(8,128)(2,1)} %weight_gradient.8), channel_id=1, source_target_pairs={{0,2},{1,7},{2,0},{3,5},{4,6},{5,3},{6,4},{7,1},{8,10},{9,15},{10,... | collective-permute-start | bytes 9437192 | tf_op jit(solution)/shard_map/ppermute | solution.py:983
  215.8 37.6 %collective-permute-start.29 = (bf16[32,24,2048]{2,1,0:T(8,128)(2,1)}, bf16[32,24,2048]{2,1,0:T(8,128)(2,1)}, u32[]{:S(2)}, u32[]{:S(2)}) collective-permute-start(bf16[32,24,2048]{2,1,0:T(8,128)(2,1)} %weight_gradient.7), channel_id=1, source_target_pairs={{0,8},{1,25},{2,10},{3,27},{4,12},{5,29},{6,14},{7,31},{8,0},{9,17... | collective-permute-start | bytes 9437192 | tf_op jit(solution)/shard_map/ppermute | solution.py:983
  235.1 12.9 %collective-permute-start.36 = (bf16[128,1536]{1,0:T(8,128)(2,1)}, bf16[128,1536]{1,0:T(8,128)(2,1)S(1)}, u32[]{:S(2)}, u32[]{:S(2)}) collective-permute-start(bf16[128,1536]{1,0:T(8,128)(2,1)} %get-tuple-element.140), channel_id=1, source_target_pairs={{0,1},{1,0},{2,3},{3,2},{4,5},{5,4},{6,7},{7,6},{8,9},{9,8},{10,11... | collective-permute-start | bytes 1179656 | tf_op jit(solution)/shard_map/ppermute | solution.py:71
  241.7 25.8 %collective-permute-start.27 = (bf16[32,24,1280]{2,1,0:T(8,128)(2,1)S(1)}, bf16[32,24,1280]{2,1,0:T(8,128)(2,1)S(1)}, u32[]{:S(2)}, u32[]{:S(2)}) collective-permute-start(bf16[32,24,1280]{2,1,0:T(8,128)(2,1)S(1)} %weight_gradient.9), channel_id=1, source_target_pairs={{0,32},{1,97},{2,34},{3,99},{4,36},{5,101},{6,38},{7,103},{8,40},{... | collective-permute-start | bytes 5898248 | tf_op jit(solution)/shard_map/ppermute | solution.py:983
  249.7 28.3 %collective-permute-start.37 = (bf16[32,24,1408]{2,1,0:T(8,128)(2,1)S(1)}, bf16[32,24,1408]{2,1,0:T(8,128)(2,1)S(1)}, u32[]{:S(2)}, u32[]{:S(2)}) collective-permute-start(bf16[32,24,1408]{2,1,0:T(8,128)(2,1)S(1)} %weight_gradient.11), channel_id=1, source_target_pairs={{0,2},{1,7},{2,0},{3,5},{4,6},{5,3},{6,4},{7,1},{8,10},{9,15},{10,... | collective-permute-start | bytes 6488072 | tf_op jit(solution)/shard_map/ppermute | solution.py:983
  255.9 31.7 %collective-permute-start.33 = (bf16[32,24,1280]{2,1,0:T(8,128)(2,1)}, bf16[32,24,1280]{2,1,0:T(8,128)(2,1)S(1)}, u32[]{:S(2)}, u32[]{:S(2)}) collective-permute-start(bf16[32,24,1280]{2,1,0:T(8,128)(2,1)} %weight_gradient.10), channel_id=1, source_target_pairs={{0,8},{1,25},{2,10},{3,27},{4,12},{5,29},{6,14},{7,31},{8,0},{9,17... | collective-permute-start | bytes 5898248 | tf_op jit(solution)/shard_map/ppermute | solution.py:983
  269.1 20.1 %collective-permute-start.31 = (bf16[16,24,1280]{2,1,0:T(8,128)(2,1)S(1)}, bf16[16,24,1280]{2,1,0:T(8,128)(2,1)S(1)}, u32[]{:S(2)}, u32[]{:S(2)}) collective-permute-start(bf16[16,24,1280]{2,1,0:T(8,128)(2,1)S(1)} %get-tuple-element.133), channel_id=1, source_target_pairs={{0,96},{1,33},{2,98},{3,35},{4,100},{5,37},{6,102},{7,39},{8,104},... | collective-permute-start | bytes 2949128 | tf_op jit(solution)/shard_map/ppermute | solution.py:983
  269.2 26.3 %collective-permute-start.32 = (bf16[16,24,2048]{2,1,0:T(8,128)(2,1)}, bf16[16,24,2048]{2,1,0:T(8,128)(2,1)S(1)}, u32[]{:S(2)}, u32[]{:S(2)}) collective-permute-start(bf16[16,24,2048]{2,1,0:T(8,128)(2,1)} %get-tuple-element.134), channel_id=1, source_target_pairs={{0,24},{1,9},{2,26},{3,11},{4,28},{5,13},{6,30},{7,15},{8,16},{9,1... | collective-permute-start | bytes 4718600 | tf_op jit(solution)/shard_map/ppermute | solution.py:983
  269.3 26.2 %collective-permute-start.35 = (bf16[16,32,1536]{2,1,0:T(8,128)(2,1)}, bf16[16,32,1536]{2,1,0:T(8,128)(2,1)S(1)}, u32[]{:S(2)}, u32[]{:S(2)}) collective-permute-start(bf16[16,32,1536]{2,1,0:T(8,128)(2,1)} %get-tuple-element.139), channel_id=1, source_target_pairs={{0,6},{1,3},{2,4},{3,1},{4,2},{5,7},{6,0},{7,5},{8,14},{9,11},{10,... | collective-permute-start | bytes 4718600 | tf_op jit(solution)/shard_map/ppermute | solution.py:983
  278.0 21.2 %collective-permute-start.28 = (bf16[16,24,2048]{2,1,0:T(8,128)(2,1)S(1)}, bf16[16,24,2048]{2,1,0:T(8,128)(2,1)S(1)}, u32[]{:S(2)}, u32[]{:S(2)}) collective-permute-start(bf16[16,24,2048]{2,1,0:T(8,128)(2,1)S(1)} %copy-done.25), channel_id=1, source_target_pairs={{0,96},{1,33},{2,98},{3,35},{4,100},{5,37},{6,102},{7,39},{8,104},... | collective-permute-start | bytes 4718600 | tf_op jit(solution)/shard_map/ppermute | solution.py:983
  287.6 18.4 %collective-permute-start.38 = (bf16[16,24,1408]{2,1,0:T(8,128)(2,1)S(1)}, bf16[16,24,1408]{2,1,0:T(8,128)(2,1)S(1)}, u32[]{:S(2)}, u32[]{:S(2)}) collective-permute-start(bf16[16,24,1408]{2,1,0:T(8,128)(2,1)S(1)} %get-tuple-element.145), channel_id=1, source_target_pairs={{0,6},{1,3},{2,4},{3,1},{4,2},{5,7},{6,0},{7,5},{8,14},{9,11},{10,... | collective-permute-start | bytes 3244040 | tf_op jit(solution)/shard_map/ppermute | solution.py:983
  289.2 16.9 %collective-permute-start.34 = (bf16[16,24,1280]{2,1,0:T(8,128)(2,1)S(1)}, bf16[16,24,1280]{2,1,0:T(8,128)(2,1)S(1)}, u32[]{:S(2)}, u32[]{:S(2)}) collective-permute-start(bf16[16,24,1280]{2,1,0:T(8,128)(2,1)S(1)} %get-tuple-element.138), channel_id=1, source_target_pairs={{0,24},{1,9},{2,26},{3,11},{4,28},{5,13},{6,30},{7,15},{8,16},{9,1... | collective-permute-start | bytes 2949128 | tf_op jit(solution)/shard_map/ppermute | solution.py:983
  307.9 19.7 %collective-permute-start.41 = (bf16[8,32,2688]{2,1,0:T(8,128)(2,1)S(1)}, bf16[8,32,2688]{2,1,0:T(8,128)(2,1)S(1)}, u32[]{:S(2)}, u32[]{:S(2)}) collective-permute-start(bf16[8,32,2688]{2,1,0:T(8,128)(2,1)S(1)} %get-tuple-element.151), channel_id=1, source_target_pairs={{0,32},{1,97},{2,34},{3,99},{4,36},{5,101},{6,38},{7,103},{8,40},{... | collective-permute-start | bytes 4128776 | tf_op jit(solution)/shard_map/ppermute | solution.py:983
  309.8 17.3 %collective-permute-start.39 = (bf16[8,24,3328]{2,1,0:T(8,128)(2,1)S(1)}, bf16[8,24,3328]{2,1,0:T(8,128)(2,1)S(1)}, u32[]{:S(2)}, u32[]{:S(2)}) collective-permute-start(bf16[8,24,3328]{2,1,0:T(8,128)(2,1)S(1)} %get-tuple-element.147), channel_id=1, source_target_pairs={{0,8},{1,25},{2,10},{3,27},{4,12},{5,29},{6,14},{7,31},{8,0},{9,17... | collective-permute-start | bytes 3833864 | tf_op jit(solution)/shard_map/ppermute | solution.py:983
  310.2 17.3 %collective-permute-start.40 = (bf16[8,24,3328]{2,1,0:T(8,128)(2,1)S(1)}, bf16[8,24,3328]{2,1,0:T(8,128)(2,1)S(1)}, u32[]{:S(2)}, u32[]{:S(2)}) collective-permute-start(bf16[8,24,3328]{2,1,0:T(8,128)(2,1)S(1)} %get-tuple-element.149), channel_id=1, source_target_pairs={{0,2},{1,7},{2,0},{3,5},{4,6},{5,3},{6,4},{7,1},{8,10},{9,15},{10,... | collective-permute-start | bytes 3833864 | tf_op jit(solution)/shard_map/ppermute | solution.py:983
  328.5 10.2 %collective-permute-start.44 = (bf16[4,32,2688]{2,1,0:T(8,128)(2,1)S(1)}, bf16[4,32,2688]{2,1,0:T(8,128)(2,1)S(1)}, u32[]{:S(2)}, u32[]{:S(2)}) collective-permute-start(bf16[4,32,2688]{2,1,0:T(8,128)(2,1)S(1)} %get-tuple-element.157), channel_id=1, source_target_pairs={{0,96},{1,33},{2,98},{3,35},{4,100},{5,37},{6,102},{7,39},{8,104},... | collective-permute-start | bytes 2064392 | tf_op jit(solution)/shard_map/ppermute | solution.py:983
  328.9 9.6 %collective-permute-start.42 = (bf16[4,24,3328]{2,1,0:T(8,128)(2,1)S(1)}, bf16[4,24,3328]{2,1,0:T(8,128)(2,1)S(1)}, u32[]{:S(2)}, u32[]{:S(2)}) collective-permute-start(bf16[4,24,3328]{2,1,0:T(8,128)(2,1)S(1)} %get-tuple-element.153), channel_id=1, source_target_pairs={{0,24},{1,9},{2,26},{3,11},{4,28},{5,13},{6,30},{7,15},{8,16},{9,1... | collective-permute-start | bytes 1916936 | tf_op jit(solution)/shard_map/ppermute | solution.py:983
  328.9 9.6 %collective-permute-start.43 = (bf16[4,24,3328]{2,1,0:T(8,128)(2,1)S(1)}, bf16[4,24,3328]{2,1,0:T(8,128)(2,1)S(1)}, u32[]{:S(2)}, u32[]{:S(2)}) collective-permute-start(bf16[4,24,3328]{2,1,0:T(8,128)(2,1)S(1)} %get-tuple-element.155), channel_id=1, source_target_pairs={{0,6},{1,3},{2,4},{3,1},{4,2},{5,7},{6,0},{7,5},{8,14},{9,11},{10,... | collective-permute-start | bytes 1916936 | tf_op jit(solution)/shard_map/ppermute | solution.py:983
  328.9 33.5 %collective-permute-start.21 = (f32[128,1536]{1,0:T(8,128)S(1)}, f32[128,1536]{1,0:T(8,128)S(1)}, u32[]{:S(2)}, u32[]{:S(2)}) collective-permute-start(f32[128,1536]{1,0:T(8,128)S(1)} %copy-done.27), channel_id=1, source_target_pairs={{0,1},{1,0},{2,3},{3,2},{4,5},{5,4},{6,7},{7,6},{8,9},{9,8},{10,11... | collective-permute-start | bytes 2359304 | tf_op jit(solution)/shard_map/ppermute | solution.py:71
  339.1 10.8 %collective-permute-start.47 = (bf16[2,32,2688]{2,1,0:T(8,128)(2,1)S(1)}, bf16[2,32,2688]{2,1,0:T(8,128)(2,1)S(1)}, u32[]{:S(2)}, u32[]{:S(2)}) collective-permute-start(bf16[2,32,2688]{2,1,0:T(8,128)(2,1)S(1)} %get-tuple-element.163), channel_id=1, source_target_pairs={{0,8},{1,25},{2,10},{3,27},{4,12},{5,29},{6,14},{7,31},{8,0},{9,17... | collective-permute-start | bytes 1032200 | tf_op jit(solution)/shard_map/ppermute | solution.py:983
  (60 other events, 637.8 us)
Sparse Core Ops, SparseCore 0:
  14.4 150.1 all-gather.1

commit v6 on v5

--- a/solution.py
+++ b/solution.py
@@ -632,7 +632,7 @@
 
 
 OWNERS = 16
-AHEAD = ((), (1,), (0, 2))
+AHEAD = ((), (1, 2), (0,))
 
 
 def weight_gradient_kernel(segments, x_counts, y_counts, has_misc, second_half, *refs):

time: 372 us -> 373 us (level)
  waiting for transfers between devices: 175 us -> 170 us
  starting transfers between devices: 72.3 us -> 76.2 us
    ppermute x42, waiting for transfers between devices: 99.1 us -> 93.1 us  [send_step(): return lax.ppermute(value, 'fsdp', pairs)]
    unnamed x88 -> x90, local copies, waits for them, and re-layouts: 8.08 us -> 8.15 us
  transfers between devices with their start and end apart: 53 -> 53, of which waited for: 26 -> 30; matrix products, arithmetic and copies ran while one was open for 2% -> 3% of each run, Pallas kernels for 20% -> 20%
where the time goes in v6:
time: 373 us; the launch traced here: 372 us
  waiting for transfers between devices  170 us (46%)
  Pallas kernels  95.1 us (25%)
  starting transfers between devices  76.2 us (20%)
  between operations  15.3 us (4%)
  local copies, waits for them, and re-layouts  11.4 us (3%)
  other arithmetic  3.8 us (1%)
    ppermute x42, waiting for transfers between devices, send_step(): return lax.ppermute(value, 'fsdp', pairs)  93.1 us
    all_gather x1, waiting for transfers between devices, body(): lax.all_gather(slab, 'fsdp', axis=0, tiled=True, axis_index_groups=by_core)  69.2 us
    ppermute x10, starting transfers between devices, swap(): return lax.ppermute(value, 'fsdp', [(d, d ^ 1) for d in range(count)])  39 us
    ppermute x42, starting transfers between devices, send_step(): return lax.ppermute(value, 'fsdp', pairs)  37.1 us
    pallas_call x12, Pallas kernels, weight_gradient(): pl.pallas_call(functools.partial(weight_gradient_kernel, segments, x_coun...  28.9 us
    pallas_call x1, Pallas kernels, attention_backward(): pl.pallas_call(attention_backward_kernel, grid=(steps,), in_specs=[rows,...  18.7 us
    pallas_call x1, Pallas kernels, attention_forward(): pl.pallas_call(attention_forward_kernel, grid_spec=pltpu.PrefetchScalarGr...  16.1 us
    pallas_call x1, Pallas kernels, feedforward(): pl.pallas_call(feedforward_kernel, grid_spec=pltpu.PrefetchScalarGridSpec...  15.7 us
  transfers between devices with their start and end apart: 53, of which 30 were waited for; matrix products, arithmetic and copies ran while one was open for 3% of the time, Pallas kernels for 20%

profile of v6, /device:TPU:1, one launch (start us, length us, event | category | flops | bytes accessed | tf_op | source)
XLA Modules:
  0.0 372.3 jit_solution(16612340019958404296)
XLA Ops:
  23.9 2.6 collective-permute-start.6
  29.8 3.7 %collective-permute-done.12 = bf16[4,32,512]{2,1,0:T(8,128)(2,1)S(1)} collective-permute-done((bf16[4,32,512]{2,1,0:T(8,128)(2,1)S(1)}, bf16[4,32,512]{2,1,0:T(8,128)(2,1)S(1)}, u32[]{:S(2)}, u32[]{:S(2)}) %collective-permute-start.12) | collective-permute-done | bytes 131104 | tf_op jit(solution)/shard_map/ppermute | solution.py:983
  36.7 4.4 %collective-permute-done.13 = bf16[8,32,512]{2,1,0:T(8,128)(2,1)S(1)} collective-permute-done((bf16[8,32,512]{2,1,0:T(8,128)(2,1)S(1)}, bf16[8,32,512]{2,1,0:T(8,128)(2,1)S(1)}, u32[]{:S(2)}, u32[]{:S(2)}) %collective-permute-start.13) | collective-permute-done | bytes 262176 | tf_op jit(solution)/shard_map/ppermute | solution.py:983
  44.9 10.1 %collective-permute-done.14 = bf16[16,32,512]{2,1,0:T(8,128)(2,1)S(1)} collective-permute-done((bf16[16,32,512]{2,1,0:T(8,128)(2,1)S(1)}, bf16[16,32,512]{2,1,0:T(8,128)(2,1)S(1)}, u32[]{:S(2)}, u32[]{:S(2)}) %collective-permute-start.14) | collective-permute-done | bytes 524320 | tf_op jit(solution)/shard_map/ppermute | solution.py:983
  58.6 22.7 %collective-permute-start.20 = (bf16[128,1536]{1,0:T(8,128)(2,1)S(1)}, bf16[128,1536]{1,0:T(8,128)(2,1)S(1)}, u32[]{:S(2)}, u32[]{:S(2)}) collective-permute-start(bf16[128,1536]{1,0:T(8,128)(2,1)S(1)} %bitcast_select_fusion.cot_own_ref.cot_ref), channel_id=1, source_target_pairs={{0,1},{1,0},{2,3},{3,2},{4,5},{5,4},{6,7},{7,6},{8,9},{9,8},{10,11... | collective-permute-start | bytes 1179656 | tf_op jit(solution)/shard_map/ppermute | solution.py:71
  81.9 4.9 %collective-permute-done.16.refs_4_ = bf16[32,32,512]{2,1,0:T(8,128)(2,1)} collective-permute-done((bf16[32,32,512]{2,1,0:T(8,128)(2,1)}, bf16[32,32,512]{2,1,0:T(8,128)(2,1)}, u32[]{:S(2)}, u32[]{:S(2)}) %collective-permute-start.16) | collective-permute-done | bytes 1048608 | tf_op jit(solution)/shard_map/ppermute | solution.py:983
  86.8 8.1 %in_order.1 = bf16[64,32,1536]{2,1,0:T(8,128)(2,1)} custom-call(s32[3,64]{1,0:T(4,128)} %get-tuple-element.111.place_ref, bf16[32,32,512]{2,1,0:T(8,128)(2,1)} %copy-done.31, bf16[32,32,512]{2,1,0:T(8,128)(2,1)} %constant_dynamic-update-slice_fusion.16.refs_1_, bf16[32,32,512]{2,1,0:T(8,128)(2,1)} %constant_dynamic-update-slice_fusion.27.refs_2_, ...), custom_call_target="tpu_custom_call" | custom-call | flops 1 | bytes 1 | tf_op jit(solution)/shard_map/in_order/pallas_call | solution.py:1020
  94.9 69.2 %all-gather.2.cloned.1.call-done.wq_ref.wk_ref.wv_ref.wh_ref.out_lo_ref.out_hi_ref.misc_ref.wg_ref.wu_ref.wo_lo_ref.wo_hi_ref = bf16[3072,8064]{1,0:T(8,128)(2,1)} async-done(((bf16[24,8064]{1,0:T(8,128)(2,1)}), bf16[3072,8064]{1,0:T(8,128)(2,1)}) %all-gather.2.cloned.1.call-update) | async-done | bytes 49545232 | tf_op jit(solution)/shard_map/all_gather | solution.py:1075
  164.1 16.1 %attention_forward.1 = (bf16[1536,128]{1,0:T(8,128)(2,1)}, bf16[128,1536]{1,0:T(8,128)(2,1)}, bf16[128,1536]{1,0:T(8,128)(2,1)}, bf16[128,1536]{1,0:T(8,128)(2,1...) custom-call(s32[1]{0:T(128)} %copy.55.length_ref, ...), custom_call_target="tpu_custom_call" | custom-call | flops 5435817984 | bytes 23592960 | tf_op jit(solution)/shard_map/attention_forward/pallas_call | solution.py:228
  183.2 15.7 %feedforward.1 = (bf16[1536,256]{1,0:T(8,128)(2,1)S(1)}, bf16[2048,256]{1,0:T(8,128)(2,1)S(1)}, bf16[256,2048]{1,0:T(8,128)(2,1)S(1)}, bf16[256,2048]{1,0:T(8,12...) custom-call(s32[1]{0:T(128)} %bitcast.7.core_ref.refs_1_, ...), custom_call_target="tpu_custom_call" | custom-call | flops 9663676416 | bytes 18874368 | tf_op jit(solution)/shard_map/feedforward/pallas_call | solution.py:354
  199.3 2.9 weight_gradient.6
  202.2 2.5 collective-permute-start.25
  207.0 3.0 weight_gradient.7
  211.1 2.9 weight_gradient.8
  215.8 18.7 %attention_backward.1 = (bf16[4,128,1536]{2,1,0:T(8,128)(2,1)}, bf16[128,1536]{1,0:T(8,128)(2,1)}, f32[128,1536]{1,0:T(8,128)}, bf16[1536,128]{1,0:T(8,128)(2,1)}) custom-call(bf16[128,1536]{1,0:T(8,128)(2,1)} %bitcast.91, bf16[1536,128]{1,0:T(8,128)(2,1)} %get-tuple-element.105.normed_t_ref, f32[1,1536]{1,0:T(1,128)} %get-tuple-element.106.gain_ref, ...), custom_call_target="tpu_custom_call" | custom-call | flops 1 | bytes 1 | tf_op jit(solution)/shard_map/attention_backward/pallas_call | solution.py:564
  235.1 3.1 collective-permute-done.26.refs_5_.refs_7_
  244.8 2.9 collective-permute-done.29.refs_4_.refs_5_
  247.6 4.0 %collective-permute-done.30.refs_4_.refs_5_ = bf16[32,32,1536]{2,1,0:T(8,128)(2,1)} collective-permute-done((bf16[32,32,1536]{2,1,0:T(8,128)(2,1)}, bf16[32,32,1536]{2,1,0:T(8,128)(2,1)}, u32[]{:S(2)}, u32[]{:S(2)}) %collective-permute-start.30) | collective-permute-done | bytes 3145760 | tf_op jit(solution)/shard_map/ppermute | solution.py:983
  258.6 4.0 %weight_gradient_add.7 = (bf16[16,24,2048]{2,1,0:T(8,128)(2,1)S(1)}, bf16[16,24,2048]{2,1,0:T(8,128)(2,1)}) custom-call(s32[64]{0:T(128)S(1)} %get-tuple-element.135.refs_0_, s32[1]{0:T(128)} %bitcast.7.core_ref.refs_1_, bf16[64,24,256]{2,1,0:T(8,128)(2,1)S(1)} %bitcast.72, bf16[1,256,2048]{2,1,0:T(8,128)(2,1)S(1)} %bitcast.76, ...), custom_call_target="tpu_custom_call" | custom-call | flops 1 | bytes 1 | tf_op jit(solution)/shard_map/weight_gradient_add/pallas_call | solution.py:713
  262.7 4.1 %weight_gradient_add.8 = (bf16[16,32,1536]{2,1,0:T(8,128)(2,1)S(1)}, bf16[16,32,1536]{2,1,0:T(8,128)(2,1)}) custom-call(s32[64]{0:T(128)S(1)} %get-tuple-element.142.refs_0_, s32[1]{0:T(128)} %bitcast.7.core_ref.refs_1_, bf16[64,32,256]{2,1,0:T(8,128)(2,1)S(1)} %bitcast.74, bf16[1,256,1536]{2,1,0:T(8,128)(2,1)S(1)} %maximum_bitcast_fusion.refs_3_, ...), custom_call_target="tpu_custom_call" | custom-call | flops 1 | bytes 1 | tf_op jit(solution)/shard_map/weight_gradient_add/pallas_call | solution.py:713
  268.8 6.2 %collective-permute-done.37.refs_11_.refs_12_ = bf16[32,24,1408]{2,1,0:T(8,128)(2,1)S(1)} collective-permute-done((bf16[32,24,1408]{2,1,0:T(8,128)(2,1)S(1)}, bf16[32,24,1408]{2,1,0:T(8,128)(2,1)S(1)}, u32[]{:S(2)}, u32[]{:S(2)}) %collective-permute-start.37) | collective-permute-done | bytes 2162720 | tf_op jit(solution)/shard_map/ppermute | solution.py:983
  276.6 7.8 %collective-permute-done.33.refs_6_.refs_7_ = bf16[32,24,1280]{2,1,0:T(8,128)(2,1)S(1)} collective-permute-done((bf16[32,24,1280]{2,1,0:T(8,128)(2,1)}, bf16[32,24,1280]{2,1,0:T(8,128)(2,1)S(1)}, u32[]{:S(2)}, u32[]{:S(2)}) %collective-permute-start.33) | collective-permute-done | bytes 1966112 | tf_op jit(solution)/shard_map/ppermute | solution.py:983
  286.1 9.5 %collective-permute-done.32.refs_10_.refs_11_ = bf16[16,24,2048]{2,1,0:T(8,128)(2,1)S(1)} collective-permute-done((bf16[16,24,2048]{2,1,0:T(8,128)(2,1)}, bf16[16,24,2048]{2,1,0:T(8,128)(2,1)S(1)}, u32[]{:S(2)}, u32[]{:S(2)}) %collective-permute-start.32) | collective-permute-done | bytes 1572896 | tf_op jit(solution)/shard_map/ppermute | solution.py:983
  295.5 3.0 collective-permute-done.28.refs_2_.refs_3_
  298.5 4.4 %collective-permute-done.38.refs_22_.refs_23_ = bf16[16,24,1408]{2,1,0:T(8,128)(2,1)S(1)} collective-permute-done((bf16[16,24,1408]{2,1,0:T(8,128)(2,1)S(1)}, bf16[16,24,1408]{2,1,0:T(8,128)(2,1)S(1)}, u32[]{:S(2)}, u32[]{:S(2)}) %collective-permute-start.38) | collective-permute-done | bytes 1081376 | tf_op jit(solution)/shard_map/ppermute | solution.py:983
  302.9 3.2 collective-permute-done.34.refs_14_.refs_15_
  312.1 13.6 %collective-permute-done.39.refs_2_.refs_3_ = bf16[8,24,3328]{2,1,0:T(8,128)(2,1)S(1)} collective-permute-done((bf16[8,24,3328]{2,1,0:T(8,128)(2,1)S(1)}, bf16[8,24,3328]{2,1,0:T(8,128)(2,1)S(1)}, u32[]{:S(2)}, u32[]{:S(2)}) %collective-permute-start.39) | collective-permute-done | bytes 1277984 | tf_op jit(solution)/shard_map/ppermute | solution.py:983
  329.0 5.2 %collective-permute-start.21 = (f32[128,1536]{1,0:T(8,128)S(1)}, f32[128,1536]{1,0:T(8,128)S(1)}, u32[]{:S(2)}, u32[]{:S(2)}) collective-permute-start(f32[128,1536]{1,0:T(8,128)S(1)} %copy-done.29), channel_id=1, source_target_pairs={{0,1},{1,0},{2,3},{3,2},{4,5},{5,4},{6,7},{7,6},{8,9},{9,8},{10,11... | collective-permute-start | bytes 2359304 | tf_op jit(solution)/shard_map/ppermute | solution.py:71
  334.1 3.8 %collective-permute-done.42.refs_2_.refs_3_ = bf16[4,24,3328]{2,1,0:T(8,128)(2,1)S(1)} collective-permute-done((bf16[4,24,3328]{2,1,0:T(8,128)(2,1)S(1)}, bf16[4,24,3328]{2,1,0:T(8,128)(2,1)S(1)}, u32[]{:S(2)}, u32[]{:S(2)}) %collective-permute-start.42) | collective-permute-done | bytes 639008 | tf_op jit(solution)/shard_map/ppermute | solution.py:983
  344.0 3.4 collective-permute-done.45.refs_2_.refs_3_
  350.4 3.8 %collective-permute-done.48.refs_1_ = bf16[1,24,3328]{2,1,0:T(8,128)(2,1)S(1)} collective-permute-done((bf16[1,24,3328]{2,1,0:T(8,128)(2,1)S(1)}, bf16[1,24,3328]{2,1,0:T(8,128)(2,1)S(1)}, u32[]{:S(2)}, u32[]{:S(2)}) %collective-permute-start.48) | collective-permute-done | bytes 159776 | tf_op jit(solution)/shard_map/ppermute | solution.py:983
  355.0 8.0 %collective-permute-start.51 = (bf16[12,8192]{1,0:T(8,128)(2,1)S(1)}, bf16[12,8192]{1,0:T(8,128)(2,1)S(1)}, u32[]{:S(2)}, u32[]{:S(2)}) collective-permute-start(bf16[12,8192]{1,0:T(8,128)(2,1)S(1)} %get-tuple-element.171), channel_id=1, source_target_pairs={{0,1},{1,0},{2,3},{3,2},{4,5},{5,4},{6,7},{7,6},{8,9},{9,8},{10,11... | collective-permute-start | bytes 589832 | tf_op jit(solution)/shard_map/ppermute | solution.py:71
  (212 shorter events, 79.8 us)
Async XLA Ops:
  7.2 156.9 %all-gather.2.cloned.1.call-start = ((), (), s32[]{:S(2)}) async-start(), calls=%async_computation | async-start | bytes 49932288 | tf_op jit(solution)/shard_map/all_gather | solution.py:1075
  19.3 8.4 %collective-permute-start.11 = (bf16[2,32,512]{2,1,0:T(8,128)(2,1)S(1)}, bf16[2,32,512]{2,1,0:T(8,128)(2,1)S(1)}, u32[]{:S(2)}, u32[]{:S(2)}) collective-permute-start(bf16[2,32,512]{2,1,0:T(8,128)(2,1)S(1)} %pad_maximum_fusion.8), channel_id=1, source_target_pairs={{0,8},{1,25},{2,10},{3,27},{4,12},{5,29},{6,14},{7,31},{8,0},{9,17... | collective-permute-start | bytes 196616 | tf_op jit(solution)/shard_map/ppermute | solution.py:983
  33.7 11.1 %collective-permute-start.3 = (bf16[8,32,512]{2,1,0:T(8,128)(2,1)S(1)}, bf16[8,32,512]{2,1,0:T(8,128)(2,1)S(1)}, u32[]{:S(2)}, u32[]{:S(2)}) collective-permute-start(bf16[8,32,512]{2,1,0:T(8,128)(2,1)S(1)} %pad_maximum_fusion), channel_id=1, source_target_pairs={{0,8},{1,25},{2,10},{3,27},{4,12},{5,29},{6,14},{7,31},{8,0},{9,17... | collective-permute-start | bytes 786440 | tf_op jit(solution)/shard_map/ppermute | solution.py:983
  33.8 10.0 %collective-permute-start.8 = (bf16[8,32,512]{2,1,0:T(8,128)(2,1)S(1)}, bf16[8,32,512]{2,1,0:T(8,128)(2,1)S(1)}, u32[]{:S(2)}, u32[]{:S(2)}) collective-permute-start(bf16[8,32,512]{2,1,0:T(8,128)(2,1)S(1)} %pad_maximum_fusion.1), channel_id=1, source_target_pairs={{0,2},{1,7},{2,0},{3,5},{4,6},{5,3},{6,4},{7,1},{8,10},{9,15},{10,... | collective-permute-start | bytes 786440 | tf_op jit(solution)/shard_map/ppermute | solution.py:983
  41.8 13.2 %collective-permute-start.14 = (bf16[16,32,512]{2,1,0:T(8,128)(2,1)S(1)}, bf16[16,32,512]{2,1,0:T(8,128)(2,1)S(1)}, u32[]{:S(2)}, u32[]{:S(2)}) collective-permute-start(bf16[16,32,512]{2,1,0:T(8,128)(2,1)S(1)} %get-tuple-element.183), channel_id=1, source_target_pairs={{0,6},{1,3},{2,4},{3,1},{4,2},{5,7},{6,0},{7,5},{8,14},{9,11},{10,... | collective-permute-start | bytes 1572872 | tf_op jit(solution)/shard_map/ppermute | solution.py:983
  44.5 11.3 %collective-permute-start.9 = (bf16[16,32,512]{2,1,0:T(8,128)(2,1)S(1)}, bf16[16,32,512]{2,1,0:T(8,128)(2,1)S(1)}, u32[]{:S(2)}, u32[]{:S(2)}) collective-permute-start(bf16[16,32,512]{2,1,0:T(8,128)(2,1)S(1)} %get-tuple-element.185), channel_id=1, source_target_pairs={{0,24},{1,9},{2,26},{3,11},{4,28},{5,13},{6,30},{7,15},{8,16},{9,1... | collective-permute-start | bytes 1572872 | tf_op jit(solution)/shard_map/ppermute | solution.py:983
  44.8 11.8 %collective-permute-start.4 = (bf16[16,32,512]{2,1,0:T(8,128)(2,1)S(1)}, bf16[16,32,512]{2,1,0:T(8,128)(2,1)S(1)}, u32[]{:S(2)}, u32[]{:S(2)}) collective-permute-start(bf16[16,32,512]{2,1,0:T(8,128)(2,1)S(1)} %get-tuple-element.187), channel_id=1, source_target_pairs={{0,96},{1,33},{2,98},{3,35},{4,100},{5,37},{6,102},{7,39},{8,104},... | collective-permute-start | bytes 1572872 | tf_op jit(solution)/shard_map/ppermute | solution.py:983
  55.8 26.1 %collective-permute-start.17 = (bf16[32,32,512]{2,1,0:T(8,128)(2,1)}, bf16[32,32,512]{2,1,0:T(8,128)(2,1)}, u32[]{:S(2)}, u32[]{:S(2)}) collective-permute-start(bf16[32,32,512]{2,1,0:T(8,128)(2,1)} %constant_dynamic-update-slice_fusion.27.refs_2_), channel_id=1, source_target_pairs={{0,2},{1,7},{2,0},{3,5},{4,6},{5,3},{6,4},{7,1},{8,10},{9,15},{10,... | collective-permute-start | bytes 3145736 | tf_op jit(solution)/shard_map/ppermute | solution.py:983
  56.7 30.1 %collective-permute-start.16 = (bf16[32,32,512]{2,1,0:T(8,128)(2,1)}, bf16[32,32,512]{2,1,0:T(8,128)(2,1)}, u32[]{:S(2)}, u32[]{:S(2)}) collective-permute-start(bf16[32,32,512]{2,1,0:T(8,128)(2,1)} %constant_dynamic-update-slice_fusion.16.refs_1_), channel_id=1, source_target_pairs={{0,8},{1,25},{2,10},{3,27},{4,12},{5,29},{6,14},{7,31},{8,0},{9,17... | collective-permute-start | bytes 3145736 | tf_op jit(solution)/shard_map/ppermute | solution.py:983
  56.7 30.1 %collective-permute-start.15 = (bf16[32,32,512]{2,1,0:T(8,128)(2,1)S(1)}, bf16[32,32,512]{2,1,0:T(8,128)(2,1)}, u32[]{:S(2)}, u32[]{:S(2)}) collective-permute-start(bf16[32,32,512]{2,1,0:T(8,128)(2,1)S(1)} %constant_dynamic-update-slice_fusion.5.refs_0_), channel_id=1, source_target_pairs={{0,32},{1,97},{2,34},{3,99},{4,36},{5,101},{6,38},{7,103},{8,40},{... | collective-permute-start | bytes 3145736 | tf_op jit(solution)/shard_map/ppermute | solution.py:983
  58.6 121.9 %collective-permute-start.20 = (bf16[128,1536]{1,0:T(8,128)(2,1)S(1)}, bf16[128,1536]{1,0:T(8,128)(2,1)S(1)}, u32[]{:S(2)}, u32[]{:S(2)}) collective-permute-start(bf16[128,1536]{1,0:T(8,128)(2,1)S(1)} %bitcast_select_fusion.cot_own_ref.cot_ref), channel_id=1, source_target_pairs={{0,1},{1,0},{2,3},{3,2},{4,5},{5,4},{6,7},{7,6},{8,9},{9,8},{10,11... | collective-permute-start | bytes 1179656 | tf_op jit(solution)/shard_map/ppermute | solution.py:71
  202.2 40.6 %collective-permute-start.25 = (bf16[32,24,2048]{2,1,0:T(8,128)(2,1)}, bf16[32,24,2048]{2,1,0:T(8,128)(2,1)S(1)}, u32[]{:S(2)}, u32[]{:S(2)}) collective-permute-start(bf16[32,24,2048]{2,1,0:T(8,128)(2,1)} %weight_gradient.6), channel_id=1, source_target_pairs={{0,32},{1,97},{2,34},{3,99},{4,36},{5,101},{6,38},{7,103},{8,40},{... | collective-permute-start | bytes 9437192 | tf_op jit(solution)/shard_map/ppermute | solution.py:983
  210.0 37.6 %collective-permute-start.29 = (bf16[32,24,2048]{2,1,0:T(8,128)(2,1)}, bf16[32,24,2048]{2,1,0:T(8,128)(2,1)}, u32[]{:S(2)}, u32[]{:S(2)}) collective-permute-start(bf16[32,24,2048]{2,1,0:T(8,128)(2,1)} %weight_gradient.7), channel_id=1, source_target_pairs={{0,8},{1,25},{2,10},{3,27},{4,12},{5,29},{6,14},{7,31},{8,0},{9,17... | collective-permute-start | bytes 9437192 | tf_op jit(solution)/shard_map/ppermute | solution.py:983
  214.0 37.6 %collective-permute-start.30 = (bf16[32,32,1536]{2,1,0:T(8,128)(2,1)}, bf16[32,32,1536]{2,1,0:T(8,128)(2,1)}, u32[]{:S(2)}, u32[]{:S(2)}) collective-permute-start(bf16[32,32,1536]{2,1,0:T(8,128)(2,1)} %weight_gradient.8), channel_id=1, source_target_pairs={{0,2},{1,7},{2,0},{3,5},{4,6},{5,3},{6,4},{7,1},{8,10},{9,15},{10,... | collective-permute-start | bytes 9437192 | tf_op jit(solution)/shard_map/ppermute | solution.py:983
  241.2 25.6 %collective-permute-start.27 = (bf16[32,24,1280]{2,1,0:T(8,128)(2,1)S(1)}, bf16[32,24,1280]{2,1,0:T(8,128)(2,1)S(1)}, u32[]{:S(2)}, u32[]{:S(2)}) collective-permute-start(bf16[32,24,1280]{2,1,0:T(8,128)(2,1)S(1)} %weight_gradient.9), channel_id=1, source_target_pairs={{0,32},{1,97},{2,34},{3,99},{4,36},{5,101},{6,38},{7,103},{8,40},{... | collective-permute-start | bytes 5898248 | tf_op jit(solution)/shard_map/ppermute | solution.py:983
  244.5 30.5 %collective-permute-start.37 = (bf16[32,24,1408]{2,1,0:T(8,128)(2,1)S(1)}, bf16[32,24,1408]{2,1,0:T(8,128)(2,1)S(1)}, u32[]{:S(2)}, u32[]{:S(2)}) collective-permute-start(bf16[32,24,1408]{2,1,0:T(8,128)(2,1)S(1)} %weight_gradient.11), channel_id=1, source_target_pairs={{0,2},{1,7},{2,0},{3,5},{4,6},{5,3},{6,4},{7,1},{8,10},{9,15},{10,... | collective-permute-start | bytes 6488072 | tf_op jit(solution)/shard_map/ppermute | solution.py:983
  254.1 30.3 %collective-permute-start.33 = (bf16[32,24,1280]{2,1,0:T(8,128)(2,1)}, bf16[32,24,1280]{2,1,0:T(8,128)(2,1)S(1)}, u32[]{:S(2)}, u32[]{:S(2)}) collective-permute-start(bf16[32,24,1280]{2,1,0:T(8,128)(2,1)} %weight_gradient.10), channel_id=1, source_target_pairs={{0,8},{1,25},{2,10},{3,27},{4,12},{5,29},{6,14},{7,31},{8,0},{9,17... | collective-permute-start | bytes 5898248 | tf_op jit(solution)/shard_map/ppermute | solution.py:983
  268.3 17.6 %collective-permute-start.31 = (bf16[16,24,1280]{2,1,0:T(8,128)(2,1)S(1)}, bf16[16,24,1280]{2,1,0:T(8,128)(2,1)S(1)}, u32[]{:S(2)}, u32[]{:S(2)}) collective-permute-start(bf16[16,24,1280]{2,1,0:T(8,128)(2,1)S(1)} %get-tuple-element.133), channel_id=1, source_target_pairs={{0,96},{1,33},{2,98},{3,35},{4,100},{5,37},{6,102},{7,39},{8,104},... | collective-permute-start | bytes 2949128 | tf_op jit(solution)/shard_map/ppermute | solution.py:983
  268.4 27.1 %collective-permute-start.32 = (bf16[16,24,2048]{2,1,0:T(8,128)(2,1)}, bf16[16,24,2048]{2,1,0:T(8,128)(2,1)S(1)}, u32[]{:S(2)}, u32[]{:S(2)}) collective-permute-start(bf16[16,24,2048]{2,1,0:T(8,128)(2,1)} %get-tuple-element.134), channel_id=1, source_target_pairs={{0,24},{1,9},{2,26},{3,11},{4,28},{5,13},{6,30},{7,15},{8,16},{9,1... | collective-permute-start | bytes 4718600 | tf_op jit(solution)/shard_map/ppermute | solution.py:983
  268.5 27.0 %collective-permute-start.35 = (bf16[16,32,1536]{2,1,0:T(8,128)(2,1)}, bf16[16,32,1536]{2,1,0:T(8,128)(2,1)S(1)}, u32[]{:S(2)}, u32[]{:S(2)}) collective-permute-start(bf16[16,32,1536]{2,1,0:T(8,128)(2,1)} %get-tuple-element.139), channel_id=1, source_target_pairs={{0,6},{1,3},{2,4},{3,1},{4,2},{5,7},{6,0},{7,5},{8,14},{9,11},{10,... | collective-permute-start | bytes 4718600 | tf_op jit(solution)/shard_map/ppermute | solution.py:983
  275.0 23.5 %collective-permute-start.28 = (bf16[16,24,2048]{2,1,0:T(8,128)(2,1)S(1)}, bf16[16,24,2048]{2,1,0:T(8,128)(2,1)S(1)}, u32[]{:S(2)}, u32[]{:S(2)}) collective-permute-start(bf16[16,24,2048]{2,1,0:T(8,128)(2,1)S(1)} %copy-done.27), channel_id=1, source_target_pairs={{0,96},{1,33},{2,98},{3,35},{4,100},{5,37},{6,102},{7,39},{8,104},... | collective-permute-start | bytes 4718600 | tf_op jit(solution)/shard_map/ppermute | solution.py:983
  284.4 18.4 %collective-permute-start.38 = (bf16[16,24,1408]{2,1,0:T(8,128)(2,1)S(1)}, bf16[16,24,1408]{2,1,0:T(8,128)(2,1)S(1)}, u32[]{:S(2)}, u32[]{:S(2)}) collective-permute-start(bf16[16,24,1408]{2,1,0:T(8,128)(2,1)S(1)} %get-tuple-element.145), channel_id=1, source_target_pairs={{0,6},{1,3},{2,4},{3,1},{4,2},{5,7},{6,0},{7,5},{8,14},{9,11},{10,... | collective-permute-start | bytes 3244040 | tf_op jit(solution)/shard_map/ppermute | solution.py:983
  286.0 20.1 %collective-permute-start.34 = (bf16[16,24,1280]{2,1,0:T(8,128)(2,1)S(1)}, bf16[16,24,1280]{2,1,0:T(8,128)(2,1)S(1)}, u32[]{:S(2)}, u32[]{:S(2)}) collective-permute-start(bf16[16,24,1280]{2,1,0:T(8,128)(2,1)S(1)} %get-tuple-element.138), channel_id=1, source_target_pairs={{0,24},{1,9},{2,26},{3,11},{4,28},{5,13},{6,30},{7,15},{8,16},{9,1... | collective-permute-start | bytes 2949128 | tf_op jit(solution)/shard_map/ppermute | solution.py:983
  307.9 19.1 %collective-permute-start.41 = (bf16[8,32,2688]{2,1,0:T(8,128)(2,1)S(1)}, bf16[8,32,2688]{2,1,0:T(8,128)(2,1)S(1)}, u32[]{:S(2)}, u32[]{:S(2)}) collective-permute-start(bf16[8,32,2688]{2,1,0:T(8,128)(2,1)S(1)} %get-tuple-element.151), channel_id=1, source_target_pairs={{0,32},{1,97},{2,34},{3,99},{4,36},{5,101},{6,38},{7,103},{8,40},{... | collective-permute-start | bytes 4128776 | tf_op jit(solution)/shard_map/ppermute | solution.py:983
  308.3 17.4 %collective-permute-start.39 = (bf16[8,24,3328]{2,1,0:T(8,128)(2,1)S(1)}, bf16[8,24,3328]{2,1,0:T(8,128)(2,1)S(1)}, u32[]{:S(2)}, u32[]{:S(2)}) collective-permute-start(bf16[8,24,3328]{2,1,0:T(8,128)(2,1)S(1)} %get-tuple-element.147), channel_id=1, source_target_pairs={{0,8},{1,25},{2,10},{3,27},{4,12},{5,29},{6,14},{7,31},{8,0},{9,17... | collective-permute-start | bytes 3833864 | tf_op jit(solution)/shard_map/ppermute | solution.py:983
  309.7 17.3 %collective-permute-start.40 = (bf16[8,24,3328]{2,1,0:T(8,128)(2,1)S(1)}, bf16[8,24,3328]{2,1,0:T(8,128)(2,1)S(1)}, u32[]{:S(2)}, u32[]{:S(2)}) collective-permute-start(bf16[8,24,3328]{2,1,0:T(8,128)(2,1)S(1)} %get-tuple-element.149), channel_id=1, source_target_pairs={{0,2},{1,7},{2,0},{3,5},{4,6},{5,3},{6,4},{7,1},{8,10},{9,15},{10,... | collective-permute-start | bytes 3833864 | tf_op jit(solution)/shard_map/ppermute | solution.py:983
  328.0 10.2 %collective-permute-start.44 = (bf16[4,32,2688]{2,1,0:T(8,128)(2,1)S(1)}, bf16[4,32,2688]{2,1,0:T(8,128)(2,1)S(1)}, u32[]{:S(2)}, u32[]{:S(2)}) collective-permute-start(bf16[4,32,2688]{2,1,0:T(8,128)(2,1)S(1)} %get-tuple-element.157), channel_id=1, source_target_pairs={{0,96},{1,33},{2,98},{3,35},{4,100},{5,37},{6,102},{7,39},{8,104},... | collective-permute-start | bytes 2064392 | tf_op jit(solution)/shard_map/ppermute | solution.py:983
  328.3 9.6 %collective-permute-start.42 = (bf16[4,24,3328]{2,1,0:T(8,128)(2,1)S(1)}, bf16[4,24,3328]{2,1,0:T(8,128)(2,1)S(1)}, u32[]{:S(2)}, u32[]{:S(2)}) collective-permute-start(bf16[4,24,3328]{2,1,0:T(8,128)(2,1)S(1)} %get-tuple-element.153), channel_id=1, source_target_pairs={{0,24},{1,9},{2,26},{3,11},{4,28},{5,13},{6,30},{7,15},{8,16},{9,1... | collective-permute-start | bytes 1916936 | tf_op jit(solution)/shard_map/ppermute | solution.py:983
  328.4 9.6 %collective-permute-start.43 = (bf16[4,24,3328]{2,1,0:T(8,128)(2,1)S(1)}, bf16[4,24,3328]{2,1,0:T(8,128)(2,1)S(1)}, u32[]{:S(2)}, u32[]{:S(2)}) collective-permute-start(bf16[4,24,3328]{2,1,0:T(8,128)(2,1)S(1)} %get-tuple-element.155), channel_id=1, source_target_pairs={{0,6},{1,3},{2,4},{3,1},{4,2},{5,7},{6,0},{7,5},{8,14},{9,11},{10,... | collective-permute-start | bytes 1916936 | tf_op jit(solution)/shard_map/ppermute | solution.py:983
  329.0 34.0 %collective-permute-start.21 = (f32[128,1536]{1,0:T(8,128)S(1)}, f32[128,1536]{1,0:T(8,128)S(1)}, u32[]{:S(2)}, u32[]{:S(2)}) collective-permute-start(f32[128,1536]{1,0:T(8,128)S(1)} %copy-done.29), channel_id=1, source_target_pairs={{0,1},{1,0},{2,3},{3,2},{4,5},{5,4},{6,7},{7,6},{8,9},{9,8},{10,11... | collective-permute-start | bytes 2359304 | tf_op jit(solution)/shard_map/ppermute | solution.py:71
  338.6 11.0 %collective-permute-start.47 = (bf16[2,32,2688]{2,1,0:T(8,128)(2,1)S(1)}, bf16[2,32,2688]{2,1,0:T(8,128)(2,1)S(1)}, u32[]{:S(2)}, u32[]{:S(2)}) collective-permute-start(bf16[2,32,2688]{2,1,0:T(8,128)(2,1)S(1)} %get-tuple-element.163), channel_id=1, source_target_pairs={{0,8},{1,25},{2,10},{3,27},{4,12},{5,29},{6,14},{7,31},{8,0},{9,17... | collective-permute-start | bytes 1032200 | tf_op jit(solution)/shard_map/ppermute | solution.py:983
  355.0 9.2 %collective-permute-start.51 = (bf16[12,8192]{1,0:T(8,128)(2,1)S(1)}, bf16[12,8192]{1,0:T(8,128)(2,1)S(1)}, u32[]{:S(2)}, u32[]{:S(2)}) collective-permute-start(bf16[12,8192]{1,0:T(8,128)(2,1)S(1)} %get-tuple-element.171), channel_id=1, source_target_pairs={{0,1},{1,0},{2,3},{3,2},{4,5},{5,4},{6,7},{7,6},{8,9},{9,8},{10,11... | collective-permute-start | bytes 589832 | tf_op jit(solution)/shard_map/ppermute | solution.py:71
  (61 other events, 582.3 us)
Sparse Core Ops, SparseCore 0:
  14.4 149.6 all-gather.1
